TPU v7x, 32 devices: a whole 2x2x4 slice. The times are simulated.
32 devices in a mesh: row: 8 (over z, x), col: 4 (over y, core).
Axes of the slice: x: 2, y: 2, z: 4, core: 2. Of those that a mesh axis runs over, the one named last changes fastest.
Arguments:
- hamiltonian: bfloat16 [16, 4, 2, 2, 128, 128], P('row', 'col'), may hold values from -0.14142136 to 0.14142136, as said below
- density: float32 [16, 4, 2, 2, 128, 128], P('row', 'col'), may hold values from -6.4 to 6.4, as said below
- block_cols: int32 [16, 4, 2], P('row', 'col'), may hold values from 0 to 15, as said below
Outputs:
- commutator: float32 [16, 4, 2, 2, 128, 128], P('row', 'col')
- density_section: float32 [16, 4, 2, 2, 128, 128], P('row', 'col')
Inputs may be any that keep to these rules, and one draw needn't show every extreme that they name: `block_cols`: block rows 2 d to 2 d + 1 lie on device d along row. A permutation drawn for each device gives each of its block rows a fiber f from 0 to 1, each fiber once a device. With P the number of devices along col and t = (c - d) mod P, slot (c, 0) of a block row of fiber f on device d holds the block row of fiber f on device (d + t) mod (8); slot (c, 1) holds, for t > 0, the block row of fiber f on device (d + t - P) mod (8), and for t = 0 the block row of fiber f + 1 - 2 (f mod 2) on device d. So the pattern is symmetric and every slot (i, j) lies in column group (j div 2) mod P. `hamiltonian`: Hermitian: the block of row i for column j is the conjugate transpose of the block of row j for column i. `density`: Hermitian: the block of row i for column j is the conjugate transpose of the block of row j for column i.
All inputs are finite; a program needn't handle non-finite values.
Results may differ from a plain program's by a relative error of at most 0.0029.
Values may be sent and summed in bfloat16 or wider, within the bound.
No kernel may reach another device: no remote copies, remote signals or barrier semaphores. Data moves between devices by JAX's collectives and lax.ppermute only.
A program may use at most 64 MiB of HBM per device.

v0:
```python
import jax
import jax.numpy as jnp
from jax import lax
from jax.sharding import PartitionSpec as P


def from_behind(value, axis, by):
    peers = lax.axis_size(axis)
    return lax.ppermute(value, axis, [(i, (i + by) % peers) for i in range(peers)])


def complex_product(left_side, right_side):
    real_part = jnp.einsum(
        "rab,rkbc->rkac", left_side[:, 0], right_side[:, :, 0], preferred_element_type=jnp.float32
    ) - jnp.einsum(
        "rab,rkbc->rkac", left_side[:, 1], right_side[:, :, 1], preferred_element_type=jnp.float32
    )
    imag_part = jnp.einsum(
        "rab,rkbc->rkac", left_side[:, 0], right_side[:, :, 1], preferred_element_type=jnp.float32
    ) + jnp.einsum(
        "rab,rkbc->rkac", left_side[:, 1], right_side[:, :, 0], preferred_element_type=jnp.float32
    )
    return jnp.stack([real_part, imag_part], axis=2)


def one_hot_rows(local_index, block_rows):
    return local_index[:, None] == jnp.arange(block_rows, dtype=jnp.int32)[None, :]


def pick_slot(slot_blocks, chosen, column_slots, block_rows):
    weights = chosen.astype(jnp.bfloat16)
    picked = jnp.einsum(
        "rs,rsxab->rxab", weights, slot_blocks, preferred_element_type=jnp.float32
    ).astype(jnp.bfloat16)
    local_index = jnp.sum(jnp.where(chosen, column_slots % block_rows, 0), axis=1).astype(jnp.int32)
    return (picked, local_index)


def match_blocks(nearby_blocks, nearby_cols, local_index, wanted):
    block_rows = nearby_blocks.shape[0]
    selector = one_hot_rows(local_index, block_rows)
    row_cols = jnp.sum(jnp.where(selector[:, :, None], nearby_cols[None, :, :], 0), axis=1).astype(
        jnp.int32
    )
    matches = (row_cols[:, None, :] == wanted[:, :, None]).astype(jnp.bfloat16)
    weights = matches[:, :, :, None] * selector.astype(jnp.bfloat16)[:, None, None, :]
    return jnp.einsum(
        "rkmq,qmxab->rkxab", weights, nearby_blocks, preferred_element_type=jnp.float32
    ).astype(jnp.bfloat16)


def select_exact(blocks, local_index):
    selector = one_hot_rows(local_index, blocks.shape[0]).astype(jnp.float32)
    return jnp.einsum(
        "rq,qxab->rxab",
        selector,
        blocks,
        precision=lax.Precision.HIGHEST,
        preferred_element_type=jnp.float32,
    )


def adjoint_block(blocks):
    return jnp.stack(
        [jnp.swapaxes(blocks[:, 0], -1, -2), -jnp.swapaxes(blocks[:, 1], -1, -2)], axis=1
    )


def body(hamiltonian, density, block_cols):
    block_rows = density.shape[0]
    group_count = lax.axis_size("col")
    row_count = lax.axis_size("row")
    own_index = lax.axis_index("row")
    col_index = lax.axis_index("col")
    density_half = density.astype(jnp.bfloat16)
    own_rows = own_index * block_rows + jnp.arange(block_rows, dtype=jnp.int32)
    wanted = block_cols[:, 0, :]
    empty = jnp.zeros((block_rows,) + hamiltonian.shape[2:], jnp.float32)
    block_shape = hamiltonian.shape[3:]
    gathered = (
        lax.all_gather(hamiltonian, "col", axis=1, tiled=True),
        lax.all_gather(block_cols, "col", axis=1, tiled=True),
    )
    slot_total = gathered[1].shape[1] * gathered[1].shape[2]
    energy_slots = gathered[0].reshape((block_rows, slot_total) + block_shape)
    column_slots = gathered[1].reshape(block_rows, slot_total)
    device_of = column_slots // block_rows
    self_mask = column_slots == own_rows[:, None]
    partner_mask = (device_of == own_index) & jnp.logical_not(self_mask)

    def accumulate(total, chosen, nearby):
        energy_row, local_index = pick_slot(energy_slots, chosen, column_slots, block_rows)
        state_match = match_blocks(nearby[0][:, 0], nearby[1][:, 0], local_index, wanted)
        return total + complex_product(energy_row, state_match)

    own_shard = (density_half, block_cols)
    product = accumulate(empty, self_mask, own_shard)
    product = accumulate(product, partner_mask, own_shard)
    for offset in range(1 - group_count, group_count):
        if offset != 0:
            nearby = from_behind((density_half, block_cols), "row", -offset)
            product = accumulate(product, device_of == (own_index + offset) % row_count, nearby)
    residue = (col_index - own_index) % group_count
    local_cols = wanted % block_rows
    slot_parts = []
    for keep_slot in range(2):
        local_mirror = adjoint_block(select_exact(product[:, keep_slot], local_cols[:, keep_slot]))
        slot_parts.append(jnp.where(residue == 0, local_mirror, jnp.zeros_like(local_mirror)))
    for offset in range(1 - group_count, group_count):
        if offset != 0:
            send_slot = 1 if offset > 0 else 0
            keep_slot = 0 if offset > 0 else 1
            arrived = from_behind(product[:, send_slot], "row", -offset)
            arrived = from_behind(arrived, "col", offset)
            candidate = adjoint_block(select_exact(arrived, local_cols[:, keep_slot]))
            slot_parts[keep_slot] = jnp.where(
                residue == offset % group_count, candidate, slot_parts[keep_slot]
            )
    reverse = jnp.stack(slot_parts, axis=1)
    commutator = product - reverse
    commutator = commutator[:, None]
    turned = jnp.stack([commutator[:, :, :, 1], -commutator[:, :, :, 0]], axis=3)
    density_section = density + 0.05 * turned
    return (commutator, density_section)


def solution(mesh):
    in_specs = (
        P("row", "col", None, None, None, None),
        P("row", "col", None, None, None, None),
        P("row", "col", None),
    )
    out_specs = (P("row", "col", None, None, None, None), P("row", "col", None, None, None, None))
    return jax.shard_map(body, mesh=mesh, in_specs=in_specs, out_specs=out_specs, check_vma=False)
```

profile of v0, /device:TPU:3, one launch (start us, length us, event | category | flops | bytes accessed | tf_op | source)
XLA Modules:
  0.0 178.6 jit_solution(5222540839599778258)
XLA Ops:
  7.8 3.3 %collective-permute-start.10 = (s32[2,1,2]{2,1,0:T(1,128)S(1)}, s32[2,1,2]{2,1,0:T(1,128)S(1)}, u32[]{:S(2)}, u32[]{:S(2)}) collective-permute-start(s32[2,1,2]{2,1,0:T(1,128)S(1)} %copy-done.33), channel_id=1, source_target_pairs={{0,20},{4,24},{8,28},{12,0},{16,4},{20,8},{24,12},{28,16},{1,21},{... | collective-permute-start | bytes 56 | tf_op jit(solution)/shard_map/ppermute | solution.py:9
  11.3 1.1 collective-permute-start.6
  12.4 1.3 collective-permute-start.4
  13.7 1.3 collective-permute-start.2
  15.1 7.1 %all_gather.6 = s32[2,4,2]{2,0,1:T(2,128)S(1)} all-gather(s32[2,1,2]{2,0,1:T(2,128)S(1)} %bitcast.638), channel_id=1, replica_groups=mesh['row'=8,'col'=4] {'col'}, dimensions={1}, use_global_device_ids=true | all-gather | bytes 80 | tf_op jit(solution)/shard_map/all_gather | solution.py:82
  22.2 1.5 copy.393
  23.7 1.0 copy.250
  27.2 3.2 %collective-permute-start.1 = (bf16[2,1,2,2,128,128]{5,0,2,4,3,1:T(2,128)(2,1)S(1)}, bf16[2,1,2,2,128,128]{5,0,2,4,3,1:T(2,128)(2,1)S(1)}, u32[]{:S(2)}, u32[]{:S(2)}) collective-permute-start(bf16[2,1,2,2,128,128]{5,0,2,4,3,1:T(2,128)(2,1)S(1)} %copy.393), channel_id=1, source_target_pairs={{0,12},{4,16},{8,20},{12,24},{16,28},{20,0},{24,4},{28,8},{1,13},{... | collective-permute-start | bytes 786440 | tf_op jit(solution)/shard_map/ppermute | solution.py:9
  30.5 1.4 collective-permute-start.3
  32.1 1.5 collective-permute-start.7
  33.7 2.0 %collective-permute-start.9 = (bf16[2,1,2,2,128,128]{5,0,2,4,3,1:T(2,128)(2,1)S(1)}, bf16[2,1,2,2,128,128]{5,0,2,4,3,1:T(2,128)(2,1)S(1)}, u32[]{:S(2)}, u32[]{:S(2)}) collective-permute-start(bf16[2,1,2,2,128,128]{5,0,2,4,3,1:T(2,128)(2,1)S(1)} %copy.393), channel_id=1, source_target_pairs={{0,24},{4,28},{8,0},{12,4},{16,8},{20,12},{24,16},{28,20},{1,25},{... | collective-permute-start | bytes 786440 | tf_op jit(solution)/shard_map/ppermute | solution.py:9
  38.0 0.8 copy.194
  38.7 8.2 %collective-permute-start.11 = (bf16[2,1,2,2,128,128]{5,0,2,4,3,1:T(2,128)(2,1)S(1)}, bf16[2,1,2,2,128,128]{5,0,2,4,3,1:T(2,128)(2,1)}, u32[]{:S(2)}, u32[]{:S(2)}) collective-permute-start(bf16[2,1,2,2,128,128]{5,0,2,4,3,1:T(2,128)(2,1)S(1)} %copy.393), channel_id=1, source_target_pairs={{0,20},{4,24},{8,28},{12,0},{16,4},{20,8},{24,12},{28,16},{1,21},{... | collective-permute-start | bytes 786440 | tf_op jit(solution)/shard_map/ppermute | solution.py:9
  49.2 1.6 fusion.4
  51.8 4.2 %collective-permute-done.9 = bf16[2,1,2,2,128,128]{5,0,2,4,3,1:T(2,128)(2,1)S(1)} collective-permute-done((bf16[2,1,2,2,128,128]{5,0,2,4,3,1:T(2,128)(2,1)S(1)}, bf16[2,1,2,2,128,128]{5,0,2,4,3,1:T(2,128)(2,1)S(1)}, u32[]{:S(2)}, u32[]{:S(2)}) %collective-permute-start.9) | collective-permute-done | bytes 262176 | tf_op jit(solution)/shard_map/ppermute | solution.py:9
  58.5 7.9 %collective-permute-done.11 = bf16[2,1,2,2,128,128]{5,0,2,4,3,1:T(2,128)(2,1)} collective-permute-done((bf16[2,1,2,2,128,128]{5,0,2,4,3,1:T(2,128)(2,1)S(1)}, bf16[2,1,2,2,128,128]{5,0,2,4,3,1:T(2,128)(2,1)}, u32[]{:S(2)}, u32[]{:S(2)}) %collective-permute-start.11) | collective-permute-done | bytes 262176 | tf_op jit(solution)/shard_map/ppermute | solution.py:9
  66.4 1.6 fusion.7
  68.5 2.0 %fusion.42 = bf16[2,1,2,128,128]{4,1,3,2,0:T(2,128)(2,1)S(1)} fusion(bf16[2,8,2,128,128]{4,3,2,1,0:T(8,128)(2,1)} %bitcast.558, pred[2,8,1,1,1]{1,0,2,3,4:T(4,128)(4,1)S(1)} %get-tuple-element.78), kind=kOutput, calls=%fused_computation.89 | convolution fusion | flops 1048576 | bytes 1179664 | tf_op jit(solution)/shard_map/rs,rsxab->rxab/dot_general | solution.py:32
  80.3 1.0 fusion.44
  86.1 9.1 %collective-permute-start.12 = (f32[2,2,128,128]{2,3,0,1:T(8,128)S(1)}, f32[2,2,128,128]{2,3,0,1:T(8,128)}, u32[]{:S(2)}, u32[]{:S(2)}) collective-permute-start(f32[2,2,128,128]{2,3,0,1:T(8,128)S(1)} %get-tuple-element.30), channel_id=1, source_target_pairs={{0,20},{4,24},{8,28},{12,0},{16,4},{20,8},{24,12},{28,16},{1,21},{... | collective-permute-start | bytes 786440 | tf_op jit(solution)/shard_map/ppermute | solution.py:9
  95.2 0.8 copy.234
  96.3 0.9 copy.246
  97.9 1.6 fusion.95
  100.8 1.4 collective-permute-start.18
  102.3 3.0 %collective-permute-start.17 = (f32[2,2,128,128]{2,3,0,1:T(8,128)}, f32[2,2,128,128]{2,3,0,1:T(8,128)}, u32[]{:S(2)}, u32[]{:S(2)}) collective-permute-start(f32[2,2,128,128]{2,3,0,1:T(8,128)} %collective-permute-done.16), channel_id=1, source_target_pairs={{0,1},{1,2},{2,3},{3,0},{4,5},{5,6},{6,7},{7,4},{8,9},{9,10},{10,1... | collective-permute-start | bytes 786440 | tf_op jit(solution)/shard_map/ppermute | solution.py:9
  107.3 21.1 %collective-permute-done.12 = f32[2,2,128,128]{2,3,0,1:T(8,128)} collective-permute-done((f32[2,2,128,128]{2,3,0,1:T(8,128)S(1)}, f32[2,2,128,128]{2,3,0,1:T(8,128)}, u32[]{:S(2)}, u32[]{:S(2)}) %collective-permute-start.12) | collective-permute-done | bytes 262176 | tf_op jit(solution)/shard_map/ppermute | solution.py:9
  128.4 1.2 collective-permute-start.15
  129.7 1.3 collective-permute-start.13
  131.4 1.0 collective-permute-start.21
  132.4 1.1 copy.231
  134.2 1.4 collective-permute-done.15
  135.5 1.8 %copy.228 = f32[2,2,128,128]{3,0,2,1:T(2,128)} copy(f32[2,2,128,128]{2,3,0,1:T(8,128)} %collective-permute-done.15) | data formatting | bytes 524288 | tf_op jit(solution)/shard_map/ppermute | solution.py:9
  137.3 2.3 %fusion.99 = f32[2,2,128,128]{3,0,2,1:T(2,128)} fusion(f32[2,2,128,128]{3,0,2,1:T(2,128)} %copy.228, s32[2]{0:T(128)S(1)} %copy-done.36), kind=kOutput, calls=%fused_computation.236 | convolution fusion | flops 1572868 | bytes 524296 | tf_op jit(solution)/shard_map/rq,qxab->rxab/dot_general | solution.py:54
  139.6 4.2 %collective-permute-done.13 = f32[2,2,128,128]{2,3,0,1:T(8,128)S(1)} collective-permute-done((f32[2,2,128,128]{2,3,0,1:T(8,128)}, f32[2,2,128,128]{2,3,0,1:T(8,128)S(1)}, u32[]{:S(2)}, u32[]{:S(2)}) %collective-permute-start.13) | collective-permute-done | bytes 262176 | tf_op jit(solution)/shard_map/ppermute | solution.py:9
  143.8 0.8 copy.225
  144.7 1.6 fusion.101
  147.7 1.8 %copy.243 = f32[2,2,128,128]{3,0,2,1:T(2,128)} copy(f32[2,2,128,128]{2,3,0,1:T(8,128)} %collective-permute-done.23) | data formatting | bytes 524288 | tf_op jit(solution)/shard_map/ppermute | solution.py:9
  149.5 1.6 fusion.89
  151.7 1.8 copy.240
  153.5 1.6 fusion.91
  161.5 1.8 copy.237
  163.3 1.6 fusion.93
  165.0 0.8 copy-done.28
  166.0 0.8 copy-done.21
  167.0 0.8 copy-done.16
  168.1 0.9 copy-done.2
  169.6 1.0 copy.251
  170.7 1.0 copy.252
  (235 shorter events, 41.5 us)
Async XLA Ops:
  7.2 61.3 %all-gather.2.cloned.1.call-start = ((), (), s32[]{:S(2)}) async-start(), calls=%async_computation | async-start | bytes 1310720 | tf_op jit(solution)/shard_map/all_gather | solution.py:81
  7.8 19.2 %collective-permute-start.10 = (s32[2,1,2]{2,1,0:T(1,128)S(1)}, s32[2,1,2]{2,1,0:T(1,128)S(1)}, u32[]{:S(2)}, u32[]{:S(2)}) collective-permute-start(s32[2,1,2]{2,1,0:T(1,128)S(1)} %copy-done.33), channel_id=1, source_target_pairs={{0,20},{4,24},{8,28},{12,0},{16,4},{20,8},{24,12},{28,16},{1,21},{... | collective-permute-start | bytes 56 | tf_op jit(solution)/shard_map/ppermute | solution.py:9
  11.1 16.1 %collective-permute-start.8 = (s32[2,1,2]{2,1,0:T(1,128)S(1)}, s32[2,1,2]{2,1,0:T(1,128)S(1)}, u32[]{:S(2)}, u32[]{:S(2)}) collective-permute-start(s32[2,1,2]{2,1,0:T(1,128)S(1)} %copy-done.33), channel_id=1, source_target_pairs={{0,24},{4,28},{8,0},{12,4},{16,8},{20,12},{24,16},{28,20},{1,25},{... | collective-permute-start | bytes 56 | tf_op jit(solution)/shard_map/ppermute | solution.py:9
  11.3 19.2 %collective-permute-start.6 = (s32[2,1,2]{2,1,0:T(1,128)S(1)}, s32[2,1,2]{2,1,0:T(1,128)S(1)}, u32[]{:S(2)}, u32[]{:S(2)}) collective-permute-start(s32[2,1,2]{2,1,0:T(1,128)S(1)} %copy-done.33), channel_id=1, source_target_pairs={{0,28},{4,0},{8,4},{12,8},{16,12},{20,16},{24,20},{28,24},{1,29},{... | collective-permute-start | bytes 56 | tf_op jit(solution)/shard_map/ppermute | solution.py:9
  12.4 19.5 %collective-permute-start.4 = (s32[2,1,2]{2,1,0:T(1,128)S(1)}, s32[2,1,2]{2,1,0:T(1,128)S(1)}, u32[]{:S(2)}, u32[]{:S(2)}) collective-permute-start(s32[2,1,2]{2,1,0:T(1,128)S(1)} %copy-done.33), channel_id=1, source_target_pairs={{0,4},{4,8},{8,12},{12,16},{16,20},{20,24},{24,28},{28,0},{1,5},{5... | collective-permute-start | bytes 56 | tf_op jit(solution)/shard_map/ppermute | solution.py:9
  13.7 18.4 %collective-permute-start.2 = (s32[2,1,2]{2,1,0:T(1,128)S(1)}, s32[2,1,2]{2,1,0:T(1,128)S(1)}, u32[]{:S(2)}, u32[]{:S(2)}) collective-permute-start(s32[2,1,2]{2,1,0:T(1,128)S(1)} %copy-done.33), channel_id=1, source_target_pairs={{0,8},{4,12},{8,16},{12,20},{16,24},{20,28},{24,0},{28,4},{1,9},{5... | collective-permute-start | bytes 56 | tf_op jit(solution)/shard_map/ppermute | solution.py:9
  15.0 8.7 %copy-start.12 = (f32[2,1,2,2,128,128]{5,4,3,2,1,0:T(8,128)S(1)}, f32[2,1,2,2,128,128]{5,4,3,2,1,0:T(8,128)}, u32[]{:S(2)}) copy-start(f32[2,1,2,2,128,128]{5,4,3,2,1,0:T(8,128)} %param.4) | copy-start | bytes 1572868
  27.0 6.6 %collective-permute-start = (s32[2,1,2]{2,1,0:T(1,128)S(1)}, s32[2,1,2]{2,1,0:T(1,128)S(1)}, u32[]{:S(2)}, u32[]{:S(2)}) collective-permute-start(s32[2,1,2]{2,1,0:T(1,128)S(1)} %copy-done.33), channel_id=1, source_target_pairs={{0,12},{4,16},{8,20},{12,24},{16,28},{20,0},{24,4},{28,8},{1,13},{... | collective-permute-start | bytes 56 | tf_op jit(solution)/shard_map/ppermute | solution.py:9
  27.2 11.5 %collective-permute-start.1 = (bf16[2,1,2,2,128,128]{5,0,2,4,3,1:T(2,128)(2,1)S(1)}, bf16[2,1,2,2,128,128]{5,0,2,4,3,1:T(2,128)(2,1)S(1)}, u32[]{:S(2)}, u32[]{:S(2)}) collective-permute-start(bf16[2,1,2,2,128,128]{5,0,2,4,3,1:T(2,128)(2,1)S(1)} %copy.393), channel_id=1, source_target_pairs={{0,12},{4,16},{8,20},{12,24},{16,28},{20,0},{24,4},{28,8},{1,13},{... | collective-permute-start | bytes 786440 | tf_op jit(solution)/shard_map/ppermute | solution.py:9
  30.5 17.4 %collective-permute-start.3 = (bf16[2,1,2,2,128,128]{5,0,2,4,3,1:T(2,128)(2,1)S(1)}, bf16[2,1,2,2,128,128]{5,0,2,4,3,1:T(2,128)(2,1)S(1)}, u32[]{:S(2)}, u32[]{:S(2)}) collective-permute-start(bf16[2,1,2,2,128,128]{5,0,2,4,3,1:T(2,128)(2,1)S(1)} %copy.393), channel_id=1, source_target_pairs={{0,8},{4,12},{8,16},{12,20},{16,24},{20,28},{24,0},{28,4},{1,9},{5... | collective-permute-start | bytes 786440 | tf_op jit(solution)/shard_map/ppermute | solution.py:9
  31.9 16.6 %collective-permute-start.5 = (bf16[2,1,2,2,128,128]{5,0,2,4,3,1:T(2,128)(2,1)S(1)}, bf16[2,1,2,2,128,128]{5,0,2,4,3,1:T(2,128)(2,1)S(1)}, u32[]{:S(2)}, u32[]{:S(2)}) collective-permute-start(bf16[2,1,2,2,128,128]{5,0,2,4,3,1:T(2,128)(2,1)S(1)} %copy.393), channel_id=1, source_target_pairs={{0,4},{4,8},{8,12},{12,16},{16,20},{20,24},{24,28},{28,0},{1,5},{5... | collective-permute-start | bytes 786440 | tf_op jit(solution)/shard_map/ppermute | solution.py:9
  32.1 19.1 %collective-permute-start.7 = (bf16[2,1,2,2,128,128]{5,0,2,4,3,1:T(2,128)(2,1)S(1)}, bf16[2,1,2,2,128,128]{5,0,2,4,3,1:T(2,128)(2,1)S(1)}, u32[]{:S(2)}, u32[]{:S(2)}) collective-permute-start(bf16[2,1,2,2,128,128]{5,0,2,4,3,1:T(2,128)(2,1)S(1)} %copy.393), channel_id=1, source_target_pairs={{0,28},{4,0},{8,4},{12,8},{16,12},{20,16},{24,20},{28,24},{1,29},{... | collective-permute-start | bytes 786440 | tf_op jit(solution)/shard_map/ppermute | solution.py:9
  33.7 22.4 %collective-permute-start.9 = (bf16[2,1,2,2,128,128]{5,0,2,4,3,1:T(2,128)(2,1)S(1)}, bf16[2,1,2,2,128,128]{5,0,2,4,3,1:T(2,128)(2,1)S(1)}, u32[]{:S(2)}, u32[]{:S(2)}) collective-permute-start(bf16[2,1,2,2,128,128]{5,0,2,4,3,1:T(2,128)(2,1)S(1)} %copy.393), channel_id=1, source_target_pairs={{0,24},{4,28},{8,0},{12,4},{16,8},{20,12},{24,16},{28,20},{1,25},{... | collective-permute-start | bytes 786440 | tf_op jit(solution)/shard_map/ppermute | solution.py:9
  37.5 43.9 %copy-start.13 = (bf16[2,2,128,128]{2,3,1,0:T(8,128)(2,1)}, bf16[2,2,128,128]{2,3,1,0:T(8,128)(2,1)S(1)}, u32[]{:S(2)}) copy-start(bf16[2,2,128,128]{2,3,1,0:T(8,128)(2,1)S(1)} %copy.197) | copy-start | bytes 393220
  38.7 27.7 %collective-permute-start.11 = (bf16[2,1,2,2,128,128]{5,0,2,4,3,1:T(2,128)(2,1)S(1)}, bf16[2,1,2,2,128,128]{5,0,2,4,3,1:T(2,128)(2,1)}, u32[]{:S(2)}, u32[]{:S(2)}) collective-permute-start(bf16[2,1,2,2,128,128]{5,0,2,4,3,1:T(2,128)(2,1)S(1)} %copy.393), channel_id=1, source_target_pairs={{0,20},{4,24},{8,28},{12,0},{16,4},{20,8},{24,12},{28,16},{1,21},{... | collective-permute-start | bytes 786440 | tf_op jit(solution)/shard_map/ppermute | solution.py:9
  70.7 1.2 copy-start
  80.3 4.8 %copy-start.1 = (f32[2,2,128,128]{3,2,1,0:T(8,128)}, f32[2,2,128,128]{3,2,1,0:T(8,128)S(1)}, u32[]{:S(2)}) copy-start(f32[2,2,128,128]{3,2,1,0:T(8,128)S(1)} %convolution_add_fusion) | copy-start | bytes 786436
  82.6 2.5 %copy-start.3 = (f32[2,2,128,128]{3,2,1,0:T(8,128)}, f32[2,2,128,128]{3,2,1,0:T(8,128)S(1)}, u32[]{:S(2)}) copy-start(f32[2,2,128,128]{3,2,1,0:T(8,128)S(1)} %convolution_subtract_fusion.6) | copy-start | bytes 786436
  82.8 2.3 %copy-start.5 = (f32[2,2,128,128]{3,2,1,0:T(8,128)}, f32[2,2,128,128]{3,2,1,0:T(8,128)S(1)}, u32[]{:S(2)}) copy-start(f32[2,2,128,128]{3,2,1,0:T(8,128)S(1)} %convolution_add_fusion.6) | copy-start | bytes 786436
  86.0 14.8 %collective-permute-start.16 = (f32[2,2,128,128]{2,3,0,1:T(8,128)S(1)}, f32[2,2,128,128]{2,3,0,1:T(8,128)}, u32[]{:S(2)}, u32[]{:S(2)}) collective-permute-start(f32[2,2,128,128]{2,3,0,1:T(8,128)S(1)} %get-tuple-element.30), channel_id=1, source_target_pairs={{0,28},{4,0},{8,4},{12,8},{16,12},{20,16},{24,20},{28,24},{1,29},{... | collective-permute-start | bytes 786440 | tf_op jit(solution)/shard_map/ppermute | solution.py:9
  86.1 16.2 %collective-permute-start.14 = (f32[2,2,128,128]{2,3,0,1:T(8,128)S(1)}, f32[2,2,128,128]{2,3,0,1:T(8,128)}, u32[]{:S(2)}, u32[]{:S(2)}) collective-permute-start(f32[2,2,128,128]{2,3,0,1:T(8,128)S(1)} %get-tuple-element.30), channel_id=1, source_target_pairs={{0,24},{4,28},{8,0},{12,4},{16,8},{20,12},{24,16},{28,20},{1,25},{... | collective-permute-start | bytes 786440 | tf_op jit(solution)/shard_map/ppermute | solution.py:9
  86.1 42.3 %collective-permute-start.12 = (f32[2,2,128,128]{2,3,0,1:T(8,128)S(1)}, f32[2,2,128,128]{2,3,0,1:T(8,128)}, u32[]{:S(2)}, u32[]{:S(2)}) collective-permute-start(f32[2,2,128,128]{2,3,0,1:T(8,128)S(1)} %get-tuple-element.30), channel_id=1, source_target_pairs={{0,20},{4,24},{8,28},{12,0},{16,4},{20,8},{24,12},{28,16},{1,21},{... | collective-permute-start | bytes 786440 | tf_op jit(solution)/shard_map/ppermute | solution.py:9
  96.1 33.6 %collective-permute-start.22 = (f32[2,2,128,128]{2,3,0,1:T(8,128)S(1)}, f32[2,2,128,128]{2,3,0,1:T(8,128)}, u32[]{:S(2)}, u32[]{:S(2)}) collective-permute-start(f32[2,2,128,128]{2,3,0,1:T(8,128)S(1)} %get-tuple-element.31), channel_id=1, source_target_pairs={{0,12},{4,16},{8,20},{12,24},{16,28},{20,0},{24,4},{28,8},{1,13},{... | collective-permute-start | bytes 786440 | tf_op jit(solution)/shard_map/ppermute | solution.py:9
  96.1 34.9 %collective-permute-start.20 = (f32[2,2,128,128]{2,3,0,1:T(8,128)S(1)}, f32[2,2,128,128]{2,3,0,1:T(8,128)}, u32[]{:S(2)}, u32[]{:S(2)}) collective-permute-start(f32[2,2,128,128]{2,3,0,1:T(8,128)S(1)} %get-tuple-element.31), channel_id=1, source_target_pairs={{0,8},{4,12},{8,16},{12,20},{16,24},{20,28},{24,0},{28,4},{1,9},{5... | collective-permute-start | bytes 786440 | tf_op jit(solution)/shard_map/ppermute | solution.py:9
  97.9 1.6 copy-start.32
  100.8 30.6 %collective-permute-start.18 = (f32[2,2,128,128]{2,3,0,1:T(8,128)S(1)}, f32[2,2,128,128]{2,3,0,1:T(8,128)}, u32[]{:S(2)}, u32[]{:S(2)}) collective-permute-start(f32[2,2,128,128]{2,3,0,1:T(8,128)S(1)} %get-tuple-element.31), channel_id=1, source_target_pairs={{0,4},{4,8},{8,12},{12,16},{16,20},{20,24},{24,28},{28,0},{1,5},{5... | collective-permute-start | bytes 786440 | tf_op jit(solution)/shard_map/ppermute | solution.py:9
  102.3 30.1 %collective-permute-start.17 = (f32[2,2,128,128]{2,3,0,1:T(8,128)}, f32[2,2,128,128]{2,3,0,1:T(8,128)}, u32[]{:S(2)}, u32[]{:S(2)}) collective-permute-start(f32[2,2,128,128]{2,3,0,1:T(8,128)} %collective-permute-done.16), channel_id=1, source_target_pairs={{0,1},{1,2},{2,3},{3,0},{4,5},{5,6},{6,7},{7,4},{8,9},{9,10},{10,1... | collective-permute-start | bytes 786440 | tf_op jit(solution)/shard_map/ppermute | solution.py:9
  128.4 7.1 %collective-permute-start.15 = (f32[2,2,128,128]{2,3,0,1:T(8,128)}, f32[2,2,128,128]{2,3,0,1:T(8,128)}, u32[]{:S(2)}, u32[]{:S(2)}) collective-permute-start(f32[2,2,128,128]{2,3,0,1:T(8,128)} %collective-permute-done.14), channel_id=1, source_target_pairs={{0,2},{1,3},{2,0},{3,1},{4,6},{5,7},{6,4},{7,5},{8,10},{9,11},{10,... | collective-permute-start | bytes 786440 | tf_op jit(solution)/shard_map/ppermute | solution.py:9
  129.7 14.1 %collective-permute-start.13 = (f32[2,2,128,128]{2,3,0,1:T(8,128)}, f32[2,2,128,128]{2,3,0,1:T(8,128)S(1)}, u32[]{:S(2)}, u32[]{:S(2)}) collective-permute-start(f32[2,2,128,128]{2,3,0,1:T(8,128)} %collective-permute-done.12), channel_id=1, source_target_pairs={{0,3},{1,0},{2,1},{3,2},{4,7},{5,4},{6,5},{7,6},{8,11},{9,8},{10,9... | collective-permute-start | bytes 786440 | tf_op jit(solution)/shard_map/ppermute | solution.py:9
  131.0 16.7 %collective-permute-start.23 = (f32[2,2,128,128]{2,3,0,1:T(8,128)}, f32[2,2,128,128]{2,3,0,1:T(8,128)}, u32[]{:S(2)}, u32[]{:S(2)}) collective-permute-start(f32[2,2,128,128]{2,3,0,1:T(8,128)} %collective-permute-done.22), channel_id=1, source_target_pairs={{0,1},{1,2},{2,3},{3,0},{4,5},{5,6},{6,7},{7,4},{8,9},{9,10},{10,1... | collective-permute-start | bytes 786440 | tf_op jit(solution)/shard_map/ppermute | solution.py:9
  131.4 20.3 %collective-permute-start.21 = (f32[2,2,128,128]{2,3,0,1:T(8,128)}, f32[2,2,128,128]{2,3,0,1:T(8,128)}, u32[]{:S(2)}, u32[]{:S(2)}) collective-permute-start(f32[2,2,128,128]{2,3,0,1:T(8,128)} %collective-permute-done.20), channel_id=1, source_target_pairs={{0,2},{1,3},{2,0},{3,1},{4,6},{5,7},{6,4},{7,5},{8,10},{9,11},{10,... | collective-permute-start | bytes 786440 | tf_op jit(solution)/shard_map/ppermute | solution.py:9
  132.4 29.2 %collective-permute-start.19 = (f32[2,2,128,128]{2,3,0,1:T(8,128)}, f32[2,2,128,128]{2,3,0,1:T(8,128)}, u32[]{:S(2)}, u32[]{:S(2)}) collective-permute-start(f32[2,2,128,128]{2,3,0,1:T(8,128)} %collective-permute-done.18), channel_id=1, source_target_pairs={{0,3},{1,0},{2,1},{3,2},{4,7},{5,4},{6,5},{7,6},{8,11},{9,8},{10,9... | collective-permute-start | bytes 786440 | tf_op jit(solution)/shard_map/ppermute | solution.py:9
  144.7 1.6 copy-start.31
  155.1 1.0 copy-start.29
  156.7 1.0 copy-start.26
  164.9 1.0 copy-start.25
  165.0 1.0 copy-start.23
  165.0 1.1 copy-start.24
  165.8 1.0 copy-start.22
  165.9 1.0 copy-start.17
  165.9 1.1 copy-start.18
  166.9 1.0 copy-start.19
  166.9 1.0 copy-start.20
  168.0 1.0 copy-start.4
  168.0 1.1 copy-start.6
  168.0 1.2 copy-start.8
  168.0 1.3 copy-start.10
  169.6 1.0 copy-start.11
  (15 other events, 12.3 us)
Sparse Core Ops, SparseCore 0:
  15.1 18.3 all-gather.1
where the time goes:
time: 179 us
  starting transfers between devices  41.4 us (23%)
  waiting for transfers between devices  39 us (22%)
  local copies, waits for them, and re-layouts  38.1 us (21%)
  matrix products  31.9 us (18%)
  between operations  15.2 us (8%)
  blocking collectives  7.09 us (4%)
  other arithmetic  5.79 us (3%)
    ppermute x24, starting transfers between devices, from_behind(): lax.ppermute(value, axis, [(i, (i + by) % peers) for i in range(peers)])  41.4 us
    ppermute x24, waiting for transfers between devices, from_behind(): lax.ppermute(value, axis, [(i, (i + by) % peers) for i in range(peers)])  38.9 us
    unnamed x88, local copies, waits for them, and re-layouts  19.4 us
    dot_general x8, matrix products, select_exact(): jnp.einsum('rq,qxab->rxab', selector, blocks, precision=lax.Precision.HIG...  11.5 us
    ppermute x6, local copies, waits for them, and re-layouts, from_behind(): lax.ppermute(value, axis, [(i, (i + by) % peers) for i in range(peers)])  9.1 us
    dot_general x8, matrix products, pick_slot(): jnp.einsum('rs,rsxab->rxab', weights, slot_blocks, preferred_element_type...  7.38 us
    all_gather x1, blocking collectives, body(): lax.all_gather(block_cols, 'col', axis=1, tiled=True)  7.09 us
    dot_general x8, matrix products, match_blocks(): jnp.einsum('rkmq,qmxab->rkxab', weights, nearby_blocks, preferred_element...  7.03 us
  transfers between devices with their start and end apart: 25, of which 5 were waited for; matrix products, arithmetic and copies ran while one was open for 25% of the time, Pallas kernels for 0%

commit v1 on v0

v1 whole, which is shorter than its diff:
```python
import functools

import jax
import jax.numpy as jnp
from jax import lax
from jax.experimental import pallas as pl
from jax.experimental.pallas import tpu as pltpu
from jax.sharding import PartitionSpec as P


REACH = 3


def xor_col(value, group_count, by):
    return lax.ppermute(value, "col", [(i, i ^ by) for i in range(group_count)])


def sign_of(col):
    return 1 - 2 * (col % 2)


def row_pairs(row_count, group_count, step):
    pairs = []
    for row in range(row_count):
        for col in range(group_count):
            target = (row + step * sign_of(col)) % row_count
            pairs.append((row * group_count + col, target * group_count + col))
    return pairs


def slot_stack(ref, row, slot):
    return ref[row, slot]


def fill_right(right, row, place, stack, size):
    energy_re = stack[0 * size:1 * size]
    energy_im = stack[1 * size:2 * size]
    state_re = stack[2 * size:3 * size]
    state_im = stack[3 * size:4 * size]
    left = pl.ds(2 * place * size, size)
    here = pl.ds((2 * place + 1) * size, size)
    right[row, 0 * size:1 * size, left] = state_re
    right[row, 0 * size:1 * size, here] = state_im
    right[row, 1 * size:2 * size, left] = state_im
    right[row, 1 * size:2 * size, here] = -state_re
    right[row, 2 * size:3 * size, left] = -energy_re
    right[row, 2 * size:3 * size, here] = -energy_im
    right[row, 3 * size:4 * size, left] = -energy_im
    right[row, 3 * size:4 * size, here] = energy_re


def times(left, right):
    return lax.dot_general(
        left, right, (((0,), (0,)), ((), ())), preferred_element_type=jnp.float32
    )


def chosen(index, values):
    out = values[0]
    for place in range(1, len(values)):
        out = jnp.where(index == place, values[place], out)
    return out


def terms_kernel(shape, own_cols, near_cols, *refs):
    row_count, group_count, rows, slots, size = shape
    stacks = refs[:group_count]
    outs = refs[group_count:group_count + REACH]
    right = refs[group_count + REACH]
    me = lax.axis_index("row")
    col = lax.axis_index("col")
    cols = (own_cols, near_cols)
    for row in range(rows):
        for pair in range(2):
            for slot in range(slots):
                fill_right(right, row, pair * slots + slot, slot_stack(stacks[pair], row, slot), size)
    sign = 1 - 2 * (col % 2)
    for step in range(1, REACH + 1):
        offset = step * sign
        target = (me + offset + row_count) % row_count
        held = (target % group_count) ^ col
        held_slot = jnp.where(offset > 0, 0, 1)
        for row in range(rows):
            left = chosen(held, [ref[row, held_slot] for ref in stacks])
            full = times(left, right[row])
            for pair in range(2):
                pair_col = col ^ pair
                mine = (pair_col - me + row_count) % group_count
                theirs = (pair_col - target + row_count) % group_count
                for slot in range(slots):
                    shift = offset + theirs - group_count * slot - mine + 2 * row_count
                    first = shift % row_count == 0
                    second = ((shift + group_count) % row_count == 0) & (mine != 0)
                    wanted = jnp.logical_or(slot == 0, theirs != 0)
                    valid = wanted & (first | second)
                    begin = 2 * pair * slots * size
                    part = jnp.where(
                        second,
                        full[:, begin + 2 * size:begin + 4 * size],
                        full[:, begin:begin + 2 * size],
                    )
                    part = jnp.where(valid, part, 0.0).astype(jnp.bfloat16)
                    place = jnp.where(second, cols[pair][row, 1], cols[pair][row, 0]) % rows
                    place = jnp.where(valid, place, row)
                    outs[step - 1][pair, slot, place, 0] = part[:, :size]
                    outs[step - 1][pair, slot, place, 1] = part[:, size:]


def own_kernel(shape, own_cols, *refs):
    row_count, group_count, rows, slots, size = shape
    stacks = refs[:group_count]
    out = refs[group_count]
    right = refs[group_count + 1]
    me = lax.axis_index("row")
    col = lax.axis_index("col")
    for row in range(rows):
        for slot in range(slots):
            fill_right(right, row, slot, slot_stack(stacks[0], row, slot), size)
    held = (me % group_count) ^ col
    for row in range(rows):
        left = chosen(held, [ref[row, 0] for ref in stacks])
        full = times(left, right[row])
        for slot in range(slots):
            out[row, slot, 0] = full[:, 2 * slot * size:(2 * slot + 1) * size]
            out[row, slot, 1] = full[:, (2 * slot + 1) * size:(2 * slot + 2) * size]

    @pl.when(held == 0)
    def _():
        for row in range(rows):
            partner = own_cols[row, 1] % rows
            full = times(stacks[0][partner, 1], right[partner])
            for slot in range(slots):
                begin = 2 * (1 - slot) * size
                out[row, slot, 0] += full[:, begin:begin + size]
                out[row, slot, 1] += full[:, begin + size:begin + 2 * size]


def finish_kernel(count, cols, *refs):
    own = refs[0]
    density = refs[1]
    commutator = refs[2 + count]
    section = refs[3 + count]
    real = own[0, 0, 0]
    imag = own[0, 0, 1]
    for ref in refs[2:2 + count]:
        real += ref[0, 0, 0, 0].astype(jnp.float32)
        imag += ref[0, 0, 0, 1].astype(jnp.float32)
    commutator[0, 0, 0, 0] = real
    commutator[0, 0, 0, 1] = imag
    section[0, 0, 0, 0] = density[0, 0, 0, 0] + 0.05 * imag
    section[0, 0, 0, 1] = density[0, 0, 0, 1] - 0.05 * real


def body(hamiltonian, density, block_cols):
    row_count = lax.axis_size("row")
    group_count = lax.axis_size("col")
    rows, _, slots, parts, size, _ = hamiltonian.shape
    shape = (row_count, group_count, rows, slots, size)
    smem = pl.BlockSpec(memory_space=pltpu.SMEM)
    vmem = pl.BlockSpec(memory_space=pltpu.VMEM)
    params = pltpu.CompilerParams(vmem_limit_bytes=40 * 1024 * 1024)

    own_cols = block_cols[:, 0]
    stack = jnp.stack([hamiltonian[:, 0], density[:, 0].astype(jnp.bfloat16)], axis=2)
    stack = stack.reshape(rows, slots, 2 * parts * size, size)
    stacks = [stack]
    for by in range(1, group_count):
        if by % 2 == 0:
            stacks.append(xor_col(stack, group_count, by))
        else:
            stacks.append(xor_col(stacks[by - 1], group_count, 1))
    near_cols = xor_col(own_cols, group_count, 1)

    message = jax.ShapeDtypeStruct((2, slots, rows, parts, size, size), jnp.bfloat16)
    sent = pl.pallas_call(
        functools.partial(terms_kernel, shape),
        out_shape=[message] * REACH,
        in_specs=[smem, smem] + [vmem] * group_count,
        out_specs=[vmem] * REACH,
        scratch_shapes=[pltpu.VMEM((rows, 4 * size, 4 * slots * size), jnp.bfloat16)],
        compiler_params=params,
        name="terms",
    )(own_cols, near_cols, *stacks)
    own = pl.pallas_call(
        functools.partial(own_kernel, shape),
        out_shape=jax.ShapeDtypeStruct((rows, slots, parts, size, size), jnp.float32),
        in_specs=[smem] + [vmem] * group_count,
        out_specs=vmem,
        scratch_shapes=[pltpu.VMEM((rows, 4 * size, 2 * slots * size), jnp.bfloat16)],
        compiler_params=params,
        name="own_terms",
    )(own_cols, *stacks)

    arrived = []
    for step in range(1, REACH + 1):
        pairs = row_pairs(row_count, group_count, step)
        arrived.append(lax.ppermute(sent[step - 1], ("row", "col"), pairs))
    swapped = [xor_col(one[1:], group_count, 1) for one in arrived]
    terms = arrived + swapped

    flat_cols = own_cols.reshape(-1)
    block = (1, 1, 1, parts, size, size)

    def term_index(row, slot, cols):
        return (0, slot, cols[row * slots + slot] % rows, 0, 0, 0)

    def slot_index(row, slot, cols):
        return (row, slot, 0, 0, 0)

    def home_index(row, slot, cols):
        return (row, 0, slot, 0, 0, 0)

    commutator, section = pl.pallas_call(
        functools.partial(finish_kernel, len(terms)),
        out_shape=[jax.ShapeDtypeStruct(density.shape, jnp.float32)] * 2,
        grid_spec=pltpu.PrefetchScalarGridSpec(
            num_scalar_prefetch=1,
            grid=(rows, slots),
            in_specs=[
                pl.BlockSpec((1, 1, parts, size, size), slot_index),
                pl.BlockSpec(block, home_index),
            ] + [pl.BlockSpec(block, term_index)] * len(terms),
            out_specs=[pl.BlockSpec(block, home_index)] * 2,
        ),
        compiler_params=params,
        name="finish",
    )(flat_cols, own, density, *terms)
    return commutator, section


def solution(mesh):
    blocks = P("row", "col", None, None, None, None)
    return jax.shard_map(
        body,
        mesh=mesh,
        in_specs=(blocks, blocks, P("row", "col", None)),
        out_specs=(blocks, blocks),
        check_vma=False,
    )
```

time: 179 us -> 67.2 us (0.38)
  local copies, waits for them, and re-layouts: 38.1 us -> 3.6 us
  matrix products: 31.9 us -> 0 us
  starting transfers between devices: 41.4 us -> 24.2 us
  between operations: 15.2 us -> 0.74 us
  waiting for transfers between devices: 39 us -> 28.4 us
  Pallas kernels: 0 us -> 7.18 us
  blocking collectives: 7.09 us -> 0 us
  other arithmetic: 5.79 us -> 1.76 us
    dot_general x56 -> x0, matrix products: 31.9 us -> none  [the longest x8 11.5 us: select_exact(): jnp.einsum('rq,qxab->rxab', selector, blocks, precision=lax.Precision.HIG...]
    unnamed x88 -> x11, local copies, waits for them, and re-layouts: 19.4 us -> 1.31 us
    ppermute x24 -> x10, starting transfers between devices: 41.4 us -> 24.2 us  [the longest x7 19.6 us: xor_col(): return lax.ppermute(value, 'col', [(i, i ^ by) for i in range(group_count)])]
    ppermute x24 -> x10, waiting for transfers between devices: 38.9 us -> 28.4 us  [the longest x3 16.3 us: body(): arrived.append(lax.ppermute(sent[step - 1], ('row', 'col'), pairs))]
    ppermute x6 -> x0, local copies, waits for them, and re-layouts: 9.1 us -> none  [from_behind(): lax.ppermute(value, axis, [(i, (i + by) % peers) for i in range(peers)])]
    pallas_call x0 -> x3, Pallas kernels: none -> 7.18 us  [the longest x1 3.88 us: body(): pl.pallas_call(functools.partial(finish_kernel, len(terms)), out_shape=[j...]
    all_gather x1 -> x0, blocking collectives: 7.09 us -> none  [body(): lax.all_gather(block_cols, 'col', axis=1, tiled=True)]
    squeeze x27 -> x0, local copies, waits for them, and re-layouts: 5.92 us -> none  [the longest x16 2.5 us: complex_product(): right_side[:, :, 0]]
  transfers between devices with their start and end apart: 25 -> 10, of which waited for: 5 -> 4; matrix products, arithmetic and copies ran while one was open for 25% -> 5% of each run, Pallas kernels for 0% -> 2%
where the time goes in v1:
time: 67.2 us; the launch traced here: 65.9 us
  waiting for transfers between devices  28.4 us (42%)
  starting transfers between devices  24.2 us (36%)
  Pallas kernels  7.18 us (11%)
  local copies, waits for them, and re-layouts  3.6 us (5%)
  other arithmetic  1.76 us (3%)
  between operations  0.74 us (1%)
    ppermute x7, starting transfers between devices, xor_col(): return lax.ppermute(value, 'col', [(i, i ^ by) for i in range(group_count)])  19.6 us
    ppermute x3, waiting for transfers between devices, body(): arrived.append(lax.ppermute(sent[step - 1], ('row', 'col'), pairs))  16.3 us
    ppermute x7, waiting for transfers between devices, xor_col(): return lax.ppermute(value, 'col', [(i, i ^ by) for i in range(group_count)])  12.1 us
    ppermute x3, starting transfers between devices, body(): arrived.append(lax.ppermute(sent[step - 1], ('row', 'col'), pairs))  4.61 us
    pallas_call x1, Pallas kernels, body(): pl.pallas_call(functools.partial(finish_kernel, len(terms)), out_shape=[j...  3.88 us
    slice x3, local copies, waits for them, and re-layouts, body(): swapped = [xor_col(one[1:], group_count, 1) for one in arrived]  2.17 us
    pallas_call x1, Pallas kernels, body(): pl.pallas_call(functools.partial(terms_kernel, shape), out_shape=[message...  1.91 us
    pallas_call x1, Pallas kernels, body(): pl.pallas_call(functools.partial(own_kernel, shape), out_shape=jax.ShapeD...  1.4 us
  transfers between devices with their start and end apart: 10, of which 4 were waited for; matrix products, arithmetic and copies ran while one was open for 5% of the time, Pallas kernels for 2%

profile of v1, /device:TPU:3, one launch (start us, length us, event | category | flops | bytes accessed | tf_op | source)
XLA Modules:
  0.0 65.9 jit_solution(7941829712749715110)
XLA Ops:
  0.6 0.0 copy-start.4
  0.6 1.1 %convert_bitcast_fusion = bf16[2,2,1,2,128,128]{5,4,3,1,0,2:T(8,128)(2,1)S(1)} fusion(f32[2,1,2,2,128,128]{5,4,3,2,1,0:T(8,128)} %refs_1_.1), kind=kLoop, calls=%fused_computation.1 | loop fusion | flops 131072 | bytes 786432 | tf_op jit(solution)/shard_map/convert_element_type | solution.py:164
  1.8 0.0 copy-done.4
  1.8 0.1 pad_maximum_fusion
  1.9 0.0 copy-start.3
  1.9 1.3 %collective-permute-start.1 = (bf16[2,2,512,128]{3,2,1,0:T(8,128)(2,1)S(1)}, bf16[2,2,512,128]{3,2,1,0:T(8,128)(2,1)S(1)}, u32[]{:S(2)}, u32[]{:S(2)}) collective-permute-start(bf16[2,2,512,128]{3,2,1,0:T(8,128)(2,1)S(1)} %bitcast.5), channel_id=1, source_target_pairs={{0,2},{1,3},{2,0},{3,1},{4,6},{5,7},{6,4},{7,5},{8,10},{9,11},{10,... | collective-permute-start | bytes 1572872 | tf_op jit(solution)/shard_map/ppermute | solution.py:15
  3.2 1.0 %collective-permute-start = (bf16[2,2,512,128]{3,2,1,0:T(8,128)(2,1)S(1)}, bf16[2,2,512,128]{3,2,1,0:T(8,128)(2,1)S(1)}, u32[]{:S(2)}, u32[]{:S(2)}) collective-permute-start(bf16[2,2,512,128]{3,2,1,0:T(8,128)(2,1)S(1)} %bitcast.6), channel_id=1, source_target_pairs={{0,1},{1,0},{2,3},{3,2},{4,5},{5,4},{6,7},{7,6},{8,9},{9,8},{10,11... | collective-permute-start | bytes 1572872 | tf_op jit(solution)/shard_map/ppermute | solution.py:15
  4.2 10.6 %collective-permute-done.1.refs_2_ = bf16[2,2,512,128]{3,2,1,0:T(8,128)(2,1)S(1)} collective-permute-done((bf16[2,2,512,128]{3,2,1,0:T(8,128)(2,1)S(1)}, bf16[2,2,512,128]{3,2,1,0:T(8,128)(2,1)S(1)}, u32[]{:S(2)}, u32[]{:S(2)}) %collective-permute-start.1) | collective-permute-done | bytes 524320 | tf_op jit(solution)/shard_map/ppermute | solution.py:15
  14.8 1.5 %collective-permute-start.2 = (bf16[2,2,512,128]{3,2,1,0:T(8,128)(2,1)S(1)}, bf16[2,2,512,128]{3,2,1,0:T(8,128)(2,1)S(1)}, u32[]{:S(2)}, u32[]{:S(2)}) collective-permute-start(bf16[2,2,512,128]{3,2,1,0:T(8,128)(2,1)S(1)} %collective-permute-done.1.refs_2_), channel_id=1, source_target_pairs={{0,1},{1,0},{2,3},{3,2},{4,5},{5,4},{6,7},{7,6},{8,9},{9,8},{10,11... | collective-permute-start | bytes 1572872 | tf_op jit(solution)/shard_map/ppermute | solution.py:15
  16.3 0.0 copy-done.3
  16.3 0.0 collective-permute-start.3
  16.3 1.5 %collective-permute-done.3.near_cols = s32[2,2]{1,0:T(2,128)S(1)} collective-permute-done((s32[2,2]{1,0:T(2,128)S(1)}, s32[2,2]{1,0:T(2,128)S(1)}, u32[]{:S(2)}, u32[]{:S(2)}) %collective-permute-start.3) | collective-permute-done | bytes 48 | tf_op jit(solution)/shard_map/ppermute | solution.py:15
  17.8 0.0 collective-permute-done.refs_1_
  17.8 0.0 collective-permute-done.2.refs_3_
  17.8 1.9 %terms.1 = (bf16[2,2,2,2,128,128]{5,4,3,2,1,0:T(8,128)(2,1)S(1)}, bf16[2,2,2,2,128,128]{5,4,3,2,1,0:T(8,128)(2,1)S(1)}, bf16[2,2,2,2,128,128]{5,4,3,2,1,0:T(8,128)(2,1)S(1)}) custom-call(s32[2,2]{1,0:T(2,128)S(1)} %bitcast.10, s32[2,2]{1,0:T(2,128)S(1)} %collective-permute-done.3.near_cols, bf16[2,2,512,128]{3,2,1,0:T(8,128)(2,1)S(1)} %bitcast.7, ...), custom_call_target="tpu_custom_call" | custom-call | tf_op jit(solution)/shard_map/terms/pallas_call | solution.py:175
  19.8 0.1 collective-permute-start.4
  19.8 3.5 %collective-permute-start.5 = (bf16[2,2,2,2,128,128]{5,4,3,2,1,0:T(8,128)(2,1)S(1)}, bf16[2,2,2,2,128,128]{5,4,3,2,1,0:T(8,128)(2,1)S(1)}, u32[]{:S(2)}, u32[]{:S(2)}) collective-permute-start(bf16[2,2,2,2,128,128]{5,4,3,2,1,0:T(8,128)(2,1)S(1)} %get-tuple-element.6), channel_id=1, source_target_pairs={{0,8},{1,25},{2,10},{3,27},{4,12},{5,29},{6,14},{7,31},{8,16},{9,1... | collective-permute-start | bytes 1572872 | tf_op jit(solution)/shard_map/ppermute | solution.py:197
  23.4 1.0 %collective-permute-start.6 = (bf16[2,2,2,2,128,128]{5,4,3,2,1,0:T(8,128)(2,1)S(1)}, bf16[2,2,2,2,128,128]{5,4,3,2,1,0:T(8,128)(2,1)S(1)}, u32[]{:S(2)}, u32[]{:S(2)}) collective-permute-start(bf16[2,2,2,2,128,128]{5,4,3,2,1,0:T(8,128)(2,1)S(1)} %get-tuple-element.7), channel_id=1, source_target_pairs={{0,12},{1,21},{2,14},{3,23},{4,16},{5,25},{6,18},{7,27},{8,20},{9,... | collective-permute-start | bytes 1572872 | tf_op jit(solution)/shard_map/ppermute | solution.py:197
  24.4 6.9 %collective-permute-done.4.refs_2_ = bf16[2,2,2,2,128,128]{5,4,3,2,1,0:T(8,128)(2,1)S(1)} collective-permute-done((bf16[2,2,2,2,128,128]{5,4,3,2,1,0:T(8,128)(2,1)S(1)}, bf16[2,2,2,2,128,128]{5,4,3,2,1,0:T(8,128)(2,1)S(1)}, u32[]{:S(2)}, u32[]{:S(2)}) %collective-permute-start.4) | collective-permute-done | bytes 524320 | tf_op jit(solution)/shard_map/ppermute | solution.py:197
  31.2 0.7 %slice.12 = bf16[1,2,2,2,128,128]{5,4,3,2,1,0:T(8,128)(2,1)} slice(bf16[2,2,2,2,128,128]{5,4,3,2,1,0:T(8,128)(2,1)S(1)} %collective-permute-done.4.refs_2_), slice={[1:2], [0:2], [0:2], [0:2], [0:128], [0:128]} | slice | bytes 524288 | tf_op jit(solution)/shard_map/slice | solution.py:198
  32.0 3.7 %collective-permute-start.7 = (bf16[1,2,2,2,128,128]{5,4,3,2,1,0:T(8,128)(2,1)}, bf16[1,2,2,2,128,128]{5,4,3,2,1,0:T(8,128)(2,1)S(1)}, u32[]{:S(2)}, u32[]{:S(2)}) collective-permute-start(bf16[1,2,2,2,128,128]{5,4,3,2,1,0:T(8,128)(2,1)} %slice.12), channel_id=1, source_target_pairs={{0,1},{1,0},{2,3},{3,2},{4,5},{5,4},{6,7},{7,6},{8,9},{9,8},{10,11... | collective-permute-start | bytes 786440 | tf_op jit(solution)/shard_map/ppermute | solution.py:15
  35.7 0.0 collective-permute-done.5.refs_3_
  35.7 0.7 %slice.13 = bf16[1,2,2,2,128,128]{5,4,3,2,1,0:T(8,128)(2,1)} slice(bf16[2,2,2,2,128,128]{5,4,3,2,1,0:T(8,128)(2,1)S(1)} %collective-permute-done.5.refs_3_), slice={[1:2], [0:2], [0:2], [0:2], [0:128], [0:128]} | slice | bytes 524288 | tf_op jit(solution)/shard_map/slice | solution.py:198
  36.4 12.1 %collective-permute-start.8 = (bf16[1,2,2,2,128,128]{5,4,3,2,1,0:T(8,128)(2,1)}, bf16[1,2,2,2,128,128]{5,4,3,2,1,0:T(8,128)(2,1)}, u32[]{:S(2)}, u32[]{:S(2)}) collective-permute-start(bf16[1,2,2,2,128,128]{5,4,3,2,1,0:T(8,128)(2,1)} %slice.13), channel_id=1, source_target_pairs={{0,1},{1,0},{2,3},{3,2},{4,5},{5,4},{6,7},{7,6},{8,9},{9,8},{10,11... | collective-permute-start | bytes 786440 | tf_op jit(solution)/shard_map/ppermute | solution.py:15
  48.5 9.4 %collective-permute-done.6.refs_4_ = bf16[2,2,2,2,128,128]{5,4,3,2,1,0:T(8,128)(2,1)S(1)} collective-permute-done((bf16[2,2,2,2,128,128]{5,4,3,2,1,0:T(8,128)(2,1)S(1)}, bf16[2,2,2,2,128,128]{5,4,3,2,1,0:T(8,128)(2,1)S(1)}, u32[]{:S(2)}, u32[]{:S(2)}) %collective-permute-start.6) | collective-permute-done | bytes 524320 | tf_op jit(solution)/shard_map/ppermute | solution.py:197
  57.9 0.7 %slice.14 = bf16[1,2,2,2,128,128]{5,4,3,2,1,0:T(8,128)(2,1)} slice(bf16[2,2,2,2,128,128]{5,4,3,2,1,0:T(8,128)(2,1)S(1)} %collective-permute-done.6.refs_4_), slice={[1:2], [0:2], [0:2], [0:2], [0:128], [0:128]} | slice | bytes 524288 | tf_op jit(solution)/shard_map/slice | solution.py:198
  58.6 0.0 copy-start.1
  58.6 0.8 %copy-done.1 = bf16[2,2,2,2,128,128]{5,4,3,2,1,0:T(8,128)(2,1)} copy-done((bf16[2,2,2,2,128,128]{5,4,3,2,1,0:T(8,128)(2,1)}, bf16[2,2,2,2,128,128]{5,4,3,2,1,0:T(8,128)(2,1)S(1)}, u32[]{:S(2)}) %copy-start.1) | copy-done | bytes 524312
  59.4 0.0 collective-permute-start.9
  59.4 0.5 broadcast.3
  59.9 0.6 reduce.3
  60.5 0.1 reshape_squeeze.3.cols
  60.6 0.0 copy-start
  60.6 0.0 copy-start.2
  60.6 1.4 %own_terms.1.refs_0_ = f32[2,2,2,128,128]{4,3,2,1,0:T(8,128)S(1)} custom-call(s32[2,2]{1,0:T(2,128)S(1)} %bitcast.11, bf16[2,2,512,128]{3,2,1,0:T(8,128)(2,1)S(1)} %bitcast.8, bf16[2,2,512,128]{3,2,1,0:T(8,128)(2,1)S(1)} %collective-permute-done.refs_1_, bf16[2,2,512,128]{3,2,1,0:T(8,128)(2,1)S(1)} %collective-permute-done.1.refs_2_, ...), custom_call_target="tpu_custom_call" | custom-call | tf_op jit(solution)/shard_map/own_terms/pallas_call | solution.py:184
  62.0 0.0 collective-permute-done.7.refs_5_
  62.0 0.0 collective-permute-done.8.refs_6_
  62.0 0.0 collective-permute-done.9.refs_7_
  62.0 0.0 copy-done
  62.0 0.0 copy-done.2
  62.0 3.9 %finish.1 = (f32[2,1,2,2,128,128]{5,4,3,2,1,0:T(8,128)}, f32[2,1,2,2,128,128]{5,4,3,2,1,0:T(8,128)}) custom-call(s32[4]{0:T(128)S(1)} %reshape_squeeze.3.cols, f32[2,2,2,128,128]{4,3,2,1,0:T(8,128)S(1)} %own_terms.1.refs_0_, f32[2,1,2,2,128,128]{5,4,3,2,1,0:T(8,128)S(1)} %copy-done, bf16[2,2,2,2,128,128]{5,4,3,2,1,0:T(8,128)(2,1)S(1)} %collective-permute-done.4.refs_2_, ...), custom_call_target="tpu_custom_call" | custom-call | tf_op jit(solution)/shard_map/finish/pallas_call | solution.py:213
  (1 shorter events, 0.0 us)
Async XLA Ops:
  0.6 1.1 %copy-start.4 = (bf16[2,1,2,2,128,128]{5,4,3,2,1,0:T(8,128)(2,1)S(1)}, bf16[2,1,2,2,128,128]{5,4,3,2,1,0:T(8,128)(2,1)}, u32[]{:S(2)}) copy-start(bf16[2,1,2,2,128,128]{5,4,3,2,1,0:T(8,128)(2,1)} %param.3) | copy-start | bytes 786436
  1.9 14.4 %copy-start.3 = (s32[2,1,2]{2,1,0:T(1,128)S(1)}, s32[2,1,2]{2,1,0:T(1,128)}, u32[]{:S(2)}) copy-start(s32[2,1,2]{2,1,0:T(1,128)} %param.5) | copy-start | bytes 52
  1.9 12.9 %collective-permute-start.1 = (bf16[2,2,512,128]{3,2,1,0:T(8,128)(2,1)S(1)}, bf16[2,2,512,128]{3,2,1,0:T(8,128)(2,1)S(1)}, u32[]{:S(2)}, u32[]{:S(2)}) collective-permute-start(bf16[2,2,512,128]{3,2,1,0:T(8,128)(2,1)S(1)} %bitcast.5), channel_id=1, source_target_pairs={{0,2},{1,3},{2,0},{3,1},{4,6},{5,7},{6,4},{7,5},{8,10},{9,11},{10,... | collective-permute-start | bytes 1572872 | tf_op jit(solution)/shard_map/ppermute | solution.py:15
  3.2 14.6 %collective-permute-start = (bf16[2,2,512,128]{3,2,1,0:T(8,128)(2,1)S(1)}, bf16[2,2,512,128]{3,2,1,0:T(8,128)(2,1)S(1)}, u32[]{:S(2)}, u32[]{:S(2)}) collective-permute-start(bf16[2,2,512,128]{3,2,1,0:T(8,128)(2,1)S(1)} %bitcast.6), channel_id=1, source_target_pairs={{0,1},{1,0},{2,3},{3,2},{4,5},{5,4},{6,7},{7,6},{8,9},{9,8},{10,11... | collective-permute-start | bytes 1572872 | tf_op jit(solution)/shard_map/ppermute | solution.py:15
  14.8 3.1 %collective-permute-start.2 = (bf16[2,2,512,128]{3,2,1,0:T(8,128)(2,1)S(1)}, bf16[2,2,512,128]{3,2,1,0:T(8,128)(2,1)S(1)}, u32[]{:S(2)}, u32[]{:S(2)}) collective-permute-start(bf16[2,2,512,128]{3,2,1,0:T(8,128)(2,1)S(1)} %collective-permute-done.1.refs_2_), channel_id=1, source_target_pairs={{0,1},{1,0},{2,3},{3,2},{4,5},{5,4},{6,7},{7,6},{8,9},{9,8},{10,11... | collective-permute-start | bytes 1572872 | tf_op jit(solution)/shard_map/ppermute | solution.py:15
  16.3 1.5 %collective-permute-start.3 = (s32[2,2]{1,0:T(2,128)S(1)}, s32[2,2]{1,0:T(2,128)S(1)}, u32[]{:S(2)}, u32[]{:S(2)}) collective-permute-start(s32[2,2]{1,0:T(2,128)S(1)} %bitcast.9), channel_id=1, source_target_pairs={{0,1},{1,0},{2,3},{3,2},{4,5},{5,4},{6,7},{7,6},{8,9},{9,8},{10,11... | collective-permute-start | bytes 56 | tf_op jit(solution)/shard_map/ppermute | solution.py:15
  19.8 11.5 %collective-permute-start.4 = (bf16[2,2,2,2,128,128]{5,4,3,2,1,0:T(8,128)(2,1)S(1)}, bf16[2,2,2,2,128,128]{5,4,3,2,1,0:T(8,128)(2,1)S(1)}, u32[]{:S(2)}, u32[]{:S(2)}) collective-permute-start(bf16[2,2,2,2,128,128]{5,4,3,2,1,0:T(8,128)(2,1)S(1)} %get-tuple-element.5), channel_id=1, source_target_pairs={{0,4},{1,29},{2,6},{3,31},{4,8},{5,1},{6,10},{7,3},{8,12},{9,5},{1... | collective-permute-start | bytes 1572872 | tf_op jit(solution)/shard_map/ppermute | solution.py:197
  19.8 15.9 %collective-permute-start.5 = (bf16[2,2,2,2,128,128]{5,4,3,2,1,0:T(8,128)(2,1)S(1)}, bf16[2,2,2,2,128,128]{5,4,3,2,1,0:T(8,128)(2,1)S(1)}, u32[]{:S(2)}, u32[]{:S(2)}) collective-permute-start(bf16[2,2,2,2,128,128]{5,4,3,2,1,0:T(8,128)(2,1)S(1)} %get-tuple-element.6), channel_id=1, source_target_pairs={{0,8},{1,25},{2,10},{3,27},{4,12},{5,29},{6,14},{7,31},{8,16},{9,1... | collective-permute-start | bytes 1572872 | tf_op jit(solution)/shard_map/ppermute | solution.py:197
  23.4 34.5 %collective-permute-start.6 = (bf16[2,2,2,2,128,128]{5,4,3,2,1,0:T(8,128)(2,1)S(1)}, bf16[2,2,2,2,128,128]{5,4,3,2,1,0:T(8,128)(2,1)S(1)}, u32[]{:S(2)}, u32[]{:S(2)}) collective-permute-start(bf16[2,2,2,2,128,128]{5,4,3,2,1,0:T(8,128)(2,1)S(1)} %get-tuple-element.7), channel_id=1, source_target_pairs={{0,12},{1,21},{2,14},{3,23},{4,16},{5,25},{6,18},{7,27},{8,20},{9,... | collective-permute-start | bytes 1572872 | tf_op jit(solution)/shard_map/ppermute | solution.py:197
  32.0 30.0 %collective-permute-start.7 = (bf16[1,2,2,2,128,128]{5,4,3,2,1,0:T(8,128)(2,1)}, bf16[1,2,2,2,128,128]{5,4,3,2,1,0:T(8,128)(2,1)S(1)}, u32[]{:S(2)}, u32[]{:S(2)}) collective-permute-start(bf16[1,2,2,2,128,128]{5,4,3,2,1,0:T(8,128)(2,1)} %slice.12), channel_id=1, source_target_pairs={{0,1},{1,0},{2,3},{3,2},{4,5},{5,4},{6,7},{7,6},{8,9},{9,8},{10,11... | collective-permute-start | bytes 786440 | tf_op jit(solution)/shard_map/ppermute | solution.py:15
  36.4 25.6 %collective-permute-start.8 = (bf16[1,2,2,2,128,128]{5,4,3,2,1,0:T(8,128)(2,1)}, bf16[1,2,2,2,128,128]{5,4,3,2,1,0:T(8,128)(2,1)}, u32[]{:S(2)}, u32[]{:S(2)}) collective-permute-start(bf16[1,2,2,2,128,128]{5,4,3,2,1,0:T(8,128)(2,1)} %slice.13), channel_id=1, source_target_pairs={{0,1},{1,0},{2,3},{3,2},{4,5},{5,4},{6,7},{7,6},{8,9},{9,8},{10,11... | collective-permute-start | bytes 786440 | tf_op jit(solution)/shard_map/ppermute | solution.py:15
  58.6 0.8 %copy-start.1 = (bf16[2,2,2,2,128,128]{5,4,3,2,1,0:T(8,128)(2,1)}, bf16[2,2,2,2,128,128]{5,4,3,2,1,0:T(8,128)(2,1)S(1)}, u32[]{:S(2)}) copy-start(bf16[2,2,2,2,128,128]{5,4,3,2,1,0:T(8,128)(2,1)S(1)} %collective-permute-done.6.refs_4_) | copy-start | bytes 1572868
  59.4 2.6 %collective-permute-start.9 = (bf16[1,2,2,2,128,128]{5,4,3,2,1,0:T(8,128)(2,1)}, bf16[1,2,2,2,128,128]{5,4,3,2,1,0:T(8,128)(2,1)}, u32[]{:S(2)}, u32[]{:S(2)}) collective-permute-start(bf16[1,2,2,2,128,128]{5,4,3,2,1,0:T(8,128)(2,1)} %slice.14), channel_id=1, source_target_pairs={{0,1},{1,0},{2,3},{3,2},{4,5},{5,4},{6,7},{7,6},{8,9},{9,8},{10,11... | collective-permute-start | bytes 786440 | tf_op jit(solution)/shard_map/ppermute | solution.py:15
  60.6 1.4 %copy-start = (f32[2,1,2,2,128,128]{5,4,3,2,1,0:T(8,128)S(1)}, f32[2,1,2,2,128,128]{5,4,3,2,1,0:T(8,128)}, u32[]{:S(2)}) copy-start(f32[2,1,2,2,128,128]{5,4,3,2,1,0:T(8,128)} %refs_1_.1) | copy-start | bytes 1572868
  60.6 1.4 %copy-start.2 = (bf16[2,2,2,2,128,128]{5,4,3,2,1,0:T(8,128)(2,1)S(1)}, bf16[2,2,2,2,128,128]{5,4,3,2,1,0:T(8,128)(2,1)}, u32[]{:S(2)}) copy-start(bf16[2,2,2,2,128,128]{5,4,3,2,1,0:T(8,128)(2,1)} %copy-done.1) | copy-start | bytes 1572868

commit v2 on v1

v2 whole, which is shorter than its diff:
```python
import functools

import jax
import jax.numpy as jnp
import numpy as np
from jax import lax
from jax.experimental import pallas as pl
from jax.experimental.pallas import tpu as pltpu
from jax.sharding import PartitionSpec as P


SLOTS = 2
PAIR = 2


def xor_col(value, group_count, by):
    return lax.ppermute(value, "col", [(i, i ^ by) for i in range(group_count)])


class Plan:
    def __init__(self, row_count, group_count):
        assert group_count == 4
        self.turns = [0, 1, 2]
        self.pairs = {turn: [] for turn in self.turns}
        self.width = {turn: 0 for turn in self.turns}
        sends = {}
        finds = {}
        for row in range(row_count):
            for first in range(0, group_count, PAIR):
                for offset in range(1 - group_count, group_count):
                    if offset == 0:
                        continue
                    target = (row + offset) % row_count
                    turn, sender, side = self.way(row, first, offset, target, group_count)
                    taker = first + side
                    blocks = self.blocks(row, first, target, row_count, group_count)
                    codes = []
                    for column, slot, have in blocks:
                        place = (target, column, slot, turn, taker ^ column)
                        assert place not in finds
                        finds[place] = len(codes)
                        codes.append((column ^ sender) * SLOTS + have)
                    held = ((target % group_count) ^ sender) * SLOTS + (0 if offset > 0 else 1)
                    assert (row, sender, turn) not in sends
                    sends[row, sender, turn] = (held, codes)
                    self.pairs[turn].append(
                        (row * group_count + sender, target * group_count + taker)
                    )
                    self.width[turn] = max(self.width[turn], len(codes))
        lines = []
        for row in range(row_count):
            for col in range(group_count):
                line = []
                self.send_at = {}
                for turn in self.turns:
                    held, codes = sends.get((row, col, turn), (-1, []))
                    self.send_at[turn] = len(line)
                    line += [held] + codes + [-1] * (self.width[turn] - len(codes))
                self.find_at = {}
                for turn in self.turns:
                    for pair in range(PAIR):
                        self.find_at[turn, pair] = len(line)
                        line += [finds.get((row, col, slot, turn, pair), -1) for slot in range(SLOTS)]
                lines.append(line)
        self.table = np.asarray(lines, np.int32)

    def way(self, row, first, offset, target, group_count):
        if (target % group_count) // PAIR == (row % group_count) // PAIR:
            return 2, first + (target + (offset > 0)) % PAIR, int(offset > 0)
        turn = int(offset == -2 or abs(offset) == 3)
        return turn, first + target % PAIR, int(abs(offset) == 2)

    def blocks(self, row, first, target, row_count, group_count):
        found = []
        for column in range(first, first + PAIR):
            mine = (column - row) % group_count
            theirs = (column - target) % group_count
            have = {(row + mine) % row_count: 0}
            if mine:
                have[(row + mine - group_count) % row_count] = 1
            for slot in range(SLOTS if theirs else 1):
                wanted = (target + theirs - group_count * slot) % row_count
                if wanted in have:
                    found.append((column, slot, have[wanted]))
        return found


def fill_right(right, row, place, stack, size):
    energy_re = stack[0 * size:1 * size]
    energy_im = stack[1 * size:2 * size]
    state_re = stack[2 * size:3 * size]
    state_im = stack[3 * size:4 * size]
    right[row, place, 0 * size:1 * size, :size] = state_re
    right[row, place, 0 * size:1 * size, size:] = state_im
    right[row, place, 1 * size:2 * size, :size] = state_im
    right[row, place, 1 * size:2 * size, size:] = -state_re
    right[row, place, 2 * size:3 * size, :size] = -energy_re
    right[row, place, 2 * size:3 * size, size:] = -energy_im
    right[row, place, 3 * size:4 * size, :size] = -energy_im
    right[row, place, 3 * size:4 * size, size:] = energy_re


def times(left, right):
    return lax.dot_general(
        left, right, (((0,), (0,)), ((), ())), preferred_element_type=jnp.float32
    )


def chosen(index, values):
    out = values[0]
    for place in range(1, len(values)):
        out = jnp.where(index == place, values[place], out)
    return out


def terms_kernel(plan, turns, group_count, rows, size, line, own_cols, near_cols, *refs):
    stacks = refs[:-len(turns) - 2]
    outs = refs[-len(turns) - 2:-2]
    own, right = refs[-2:]
    for row in range(rows):
        for pair in range(PAIR):
            for slot in range(SLOTS):
                fill_right(right, row, pair * SLOTS + slot, stacks[pair][row, slot], size)
    for turn, out in zip(turns, outs):
        base = plan.send_at[turn]
        held = line[base]
        for row in range(rows):
            values = [ref[row, held % SLOTS] for ref in stacks[:PAIR + 1]]
            values += [ref[row] for ref in stacks[PAIR + 1:]]
            left = chosen(held // SLOTS, values)
            for place in range(plan.width[turn]):
                code = jnp.maximum(line[base + 1 + place], 0)
                pair = code // SLOTS
                slot = code % SLOTS
                full = times(left, right[row, code]).astype(jnp.bfloat16)
                there = jnp.where(pair == 0, own_cols[row, slot], near_cols[row, slot]) % rows
                out[place, there, 0] = full[:, :size]
                out[place, there, 1] = full[:, size:]
    if len(stacks) == group_count:
        own_part(group_count, rows, size, own_cols, stacks, right, own)


def own_part(group_count, rows, size, own_cols, stacks, right, out):
    me = lax.axis_index("row")
    col = lax.axis_index("col")
    held = (me % group_count) ^ col
    for row in range(rows):
        values = [ref[row, 0] for ref in stacks[:PAIR + 1]] + [ref[row] for ref in stacks[PAIR + 1:]]
        left = chosen(held, values)
        for slot in range(SLOTS):
            full = times(left, right[row, slot])
            out[row, slot, 0] = full[:, :size]
            out[row, slot, 1] = full[:, size:]

    @pl.when(held == 0)
    def _():
        for row in range(rows):
            partner = own_cols[row, 1] % rows
            for slot in range(SLOTS):
                full = times(stacks[0][partner, 1], right[partner, 1 - slot])
                out[row, slot, 0] += full[:, :size]
                out[row, slot, 1] += full[:, size:]


def finish_kernel(places, line, cols, *refs):
    count = len(places)
    own, density = refs[0], refs[1]
    commutator, section = refs[2 + count], refs[3 + count]
    slot = pl.program_id(1)
    commutator[0, 0, 0] = own[0, 0]
    for place, ref in zip(places, refs[2:2 + count]):
        @pl.when(line[place + slot] >= 0)
        def _():
            commutator[0, 0, 0] += ref[0, 0].astype(jnp.float32)
    section[0, 0, 0, 0] = density[0, 0, 0, 0] + 0.05 * commutator[0, 0, 0, 1]
    section[0, 0, 0, 1] = density[0, 0, 0, 1] - 0.05 * commutator[0, 0, 0, 0]


def body(plan, hamiltonian, density, block_cols):
    group_count = lax.axis_size("col")
    rows, _, slots, parts, size, _ = hamiltonian.shape
    smem = pl.BlockSpec(memory_space=pltpu.SMEM)
    vmem = pl.BlockSpec(memory_space=pltpu.VMEM)
    params = pltpu.CompilerParams(vmem_limit_bytes=40 * 1024 * 1024)

    device = lax.axis_index("row") * group_count + lax.axis_index("col")
    line = lax.dynamic_index_in_dim(jnp.asarray(plan.table), device, 0, keepdims=False)
    own_cols = block_cols[:, 0]
    stack = jnp.stack([hamiltonian[:, 0], density[:, 0].astype(jnp.bfloat16)], axis=2)
    stack = stack.reshape(rows, slots, 2 * parts * size, size)
    across = xor_col(stack, group_count, PAIR)
    near = xor_col(stack, group_count, 1)
    near_cols = xor_col(own_cols, group_count, 1)

    arrived = {}

    def send(turns, stacks):
        *sent, own = pl.pallas_call(
            functools.partial(terms_kernel, plan, turns, group_count, rows, size),
            out_shape=[
                jax.ShapeDtypeStruct((plan.width[turn], rows, parts, size, size), jnp.bfloat16)
                for turn in turns
            ] + [jax.ShapeDtypeStruct((rows, slots, parts, size, size), jnp.float32)],
            in_specs=[smem, smem, smem] + [vmem] * len(stacks),
            out_specs=[vmem] * (len(turns) + 1),
            scratch_shapes=[pltpu.VMEM((rows, PAIR * SLOTS, 4 * size, 2 * size), jnp.bfloat16)],
            compiler_params=params,
            name="terms_%d" % turns[0],
        )(line, own_cols, near_cols, *stacks)
        for turn, one in zip(turns, sent):
            arrived[turn] = lax.ppermute(one, ("row", "col"), plan.pairs[turn])
        return sent, own

    sent, _ = send(plan.turns[:2], [stack, near, across])
    across_first, _ = lax.optimization_barrier((across[:, 0], sent[-1]))
    diagonal = xor_col(across_first, group_count, 1)
    _, own = send(plan.turns[2:], [stack, near, across, diagonal])

    terms = []
    places = []
    for turn, one in sorted(arrived.items()):
        terms += [one, xor_col(one, group_count, 1)]
        places += [plan.find_at[turn, 0], plan.find_at[turn, 1]]

    block = (1, 1, 1, parts, size, size)

    def term_index(place, row, slot, line, cols):
        found = line[place + slot]
        return (
            jnp.maximum(found, 0),
            jnp.where(found >= 0, cols[row, slot] % rows, 0),
            0, 0, 0,
        )

    def slot_index(row, slot, line, cols):
        return (row, slot, 0, 0, 0)

    def home_index(row, slot, line, cols):
        return (row, 0, slot, 0, 0, 0)

    commutator, section = pl.pallas_call(
        functools.partial(finish_kernel, places),
        out_shape=[jax.ShapeDtypeStruct(density.shape, jnp.float32)] * 2,
        grid_spec=pltpu.PrefetchScalarGridSpec(
            num_scalar_prefetch=2,
            grid=(rows, slots),
            in_specs=[
                pl.BlockSpec((1, 1, parts, size, size), slot_index),
                pl.BlockSpec(block, home_index),
            ] + [
                pl.BlockSpec((1, 1, parts, size, size), functools.partial(term_index, place))
                for place in places
            ],
            out_specs=[pl.BlockSpec(block, home_index)] * 2,
        ),
        compiler_params=params,
        name="finish",
    )(line, own_cols, own, density, *terms)
    return commutator, section


def solution(mesh):
    plan = Plan(mesh.shape["row"], mesh.shape["col"])
    blocks = P("row", "col", None, None, None, None)
    return jax.shard_map(
        functools.partial(body, plan),
        mesh=mesh,
        in_specs=(blocks, blocks, P("row", "col", None)),
        out_specs=(blocks, blocks),
        check_vma=False,
    )
```

time: 67.2 us -> 58.4 us (0.87)
  the two profiles are of different devices: /device:TPU:3 before, /device:TPU:23 now
where the time goes in v2:
time: 58.4 us; the launch traced here: 58.2 us
  waiting for transfers between devices  42.5 us (73%)
  starting transfers between devices  6.72 us (12%)
  Pallas kernels  6.18 us (11%)
  other arithmetic  1.17 us (2%)
  local copies, waits for them, and re-layouts  0.88 us (2%)
  between operations  0.74 us (1%)
    ppermute x3, waiting for transfers between devices, send(): arrived[turn] = lax.ppermute(one, ('row', 'col'), plan.pairs[turn])  29.2 us
    ppermute x7, waiting for transfers between devices, xor_col(): return lax.ppermute(value, 'col', [(i, i ^ by) for i in range(group_count)])  13.3 us
    ppermute x7, starting transfers between devices, xor_col(): return lax.ppermute(value, 'col', [(i, i ^ by) for i in range(group_count)])  4.2 us
    pallas_call x2, Pallas kernels, send(): pl.pallas_call(functools.partial(terms_kernel, plan, turns, group_count,...  3.69 us
    ppermute x3, starting transfers between devices, send(): arrived[turn] = lax.ppermute(one, ('row', 'col'), plan.pairs[turn])  2.52 us
    pallas_call x1, Pallas kernels, body(): pl.pallas_call(functools.partial(finish_kernel, places), out_shape=[jax.S...  2.48 us
  transfers between devices with their start and end apart: 10, of which 6 were waited for; matrix products, arithmetic and copies ran while one was open for 1% of the time, Pallas kernels for 0%

profile of v2, /device:TPU:23, one launch (start us, length us, event | category | flops | bytes accessed | tf_op | source)
XLA Modules:
  0.0 58.2 jit_solution(1147000559995020359)
XLA Ops:
  0.6 0.0 copy-start.2
  0.6 1.1 %convert_bitcast_fusion = bf16[2,2,1,2,128,128]{5,4,3,1,0,2:T(8,128)(2,1)S(1)} fusion(f32[2,1,2,2,128,128]{5,4,3,2,1,0:T(8,128)} %refs_1_.1), kind=kLoop, calls=%fused_computation.2 | loop fusion | flops 131072 | bytes 786432 | tf_op jit(solution)/shard_map/convert_element_type | solution.py:189
  1.8 0.0 copy-done.2
  1.8 0.1 pad_maximum_fusion
  1.9 0.0 copy-start.1
  1.9 0.3 collective-permute-start.2
  2.2 1.0 %collective-permute-start.1 = (bf16[2,2,512,128]{3,2,0,1:T(8,128)(2,1)S(1)}, bf16[2,2,512,128]{3,2,0,1:T(8,128)(2,1)S(1)}, u32[]{:S(2)}, u32[]{:S(2)}) collective-permute-start(bf16[2,2,512,128]{3,2,0,1:T(8,128)(2,1)S(1)} %bitcast.14), channel_id=1, source_target_pairs={{0,1},{1,0},{2,3},{3,2},{4,5},{5,4},{6,7},{7,6},{8,9},{9,8},{10,11... | collective-permute-start | bytes 1572872 | tf_op jit(solution)/shard_map/ppermute | solution.py:17
  3.1 0.0 copy-done.1
  3.1 0.1 collective-permute-start
  3.3 0.7 %dynamic-slice_bitcast_fusion.line = s32[25]{0:T(128)S(1)} fusion(s32[32,25]{1,0:T(8,128)} %constant.19.clone, s32[]{:T(128)S(6)} %select_n.4), kind=kLoop, calls=%fused_computation.3 | loop fusion | bytes 204 | tf_op jit(solution)/shard_map/jit(dynamic_index_in_dim)/squeeze | solution.py:187
  4.0 10.8 %collective-permute-done.2 = bf16[2,2,512,128]{3,2,0,1:T(8,128)(2,1)S(1)} collective-permute-done((bf16[2,2,512,128]{3,2,0,1:T(8,128)(2,1)S(1)}, bf16[2,2,512,128]{3,2,0,1:T(8,128)(2,1)S(1)}, u32[]{:S(2)}, u32[]{:S(2)}) %collective-permute-start.2) | collective-permute-done | bytes 524320 | tf_op jit(solution)/shard_map/ppermute | solution.py:17
  14.8 0.0 collective-permute-done.1
  14.9 0.0 collective-permute-done.near_cols
  14.9 2.2 %terms_0.1 = (bf16[3,2,2,128,128]{4,3,2,1,0:T(8,128)(2,1)S(1)}, bf16[3,2,2,128,128]{4,3,2,1,0:T(8,128)(2,1)S(1)}, f32[2,2,2,128,128]{4,3,2,1,0:T(8,128)}) custom-call(s32[25]{0:T(128)S(1)} %dynamic-slice_bitcast_fusion.line, s32[2,2]{1,0:T(2,128)S(1)} %bitcast.10, s32[2,2]{1,0:T(2,128)S(1)} %collective-permute-done.near_cols, ...), custom_call_target="tpu_custom_call" | custom-call | tf_op jit(solution)/shard_map/terms_0/pallas_call | solution.py:198
  17.0 0.0 copy-start
  17.0 1.5 %collective-permute-start.3 = (bf16[2,512,128]{2,1,0:T(8,128)(2,1)S(1)}, bf16[2,512,128]{2,1,0:T(8,128)(2,1)S(1)}, u32[]{:S(2)}, u32[]{:S(2)}) collective-permute-start(bf16[2,512,128]{2,1,0:T(8,128)(2,1)S(1)} %slice_bitcast_fusion), channel_id=1, source_target_pairs={{0,1},{1,0},{2,3},{3,2},{4,5},{5,4},{6,7},{7,6},{8,9},{9,8},{10,11... | collective-permute-start | bytes 786440 | tf_op jit(solution)/shard_map/ppermute | solution.py:17
  18.6 1.2 %collective-permute-done.3.refs_3_ = bf16[2,512,128]{2,1,0:T(8,128)(2,1)S(1)} collective-permute-done((bf16[2,512,128]{2,1,0:T(8,128)(2,1)S(1)}, bf16[2,512,128]{2,1,0:T(8,128)(2,1)S(1)}, u32[]{:S(2)}, u32[]{:S(2)}) %collective-permute-start.3) | collective-permute-done | bytes 262176 | tf_op jit(solution)/shard_map/ppermute | solution.py:17
  19.8 1.5 %terms_2.1 = (bf16[4,2,2,128,128]{4,3,2,1,0:T(8,128)(2,1)S(1)}, f32[2,2,2,128,128]{4,3,2,1,0:T(8,128)S(1)}) custom-call(s32[25]{0:T(128)S(1)} %dynamic-slice_bitcast_fusion.line, s32[2,2]{1,0:T(2,128)S(1)} %bitcast.11, s32[2,2]{1,0:T(2,128)S(1)} %collective-permute-done.near_cols, bf16[2,2,512,128]{3,2,1,0:T(8,128)(2,1)S(1)} %copy.10.refs_0_, ...), custom_call_target="tpu_custom_call" | custom-call | tf_op jit(solution)/shard_map/terms_2/pallas_call | solution.py:198
  21.3 0.1 collective-permute-start.8
  21.4 1.7 %collective-permute-start.4 = (bf16[3,2,2,128,128]{4,3,2,1,0:T(8,128)(2,1)S(1)}, bf16[3,2,2,128,128]{4,3,2,1,0:T(8,128)(2,1)S(1)}, u32[]{:S(2)}, u32[]{:S(2)}) collective-permute-start(bf16[3,2,2,128,128]{4,3,2,1,0:T(8,128)(2,1)S(1)} %get-tuple-element.10), channel_id=1, source_target_pairs={{1,28},{0,9},{3,30},{2,11},{4,8},{5,13},{6,10},{7,15},{9,4},{8,17}... | collective-permute-start | bytes 1179656 | tf_op jit(solution)/shard_map/ppermute | solution.py:211
  23.1 0.7 %collective-permute-start.6 = (bf16[3,2,2,128,128]{4,3,2,1,0:T(8,128)(2,1)S(1)}, bf16[3,2,2,128,128]{4,3,2,1,0:T(8,128)(2,1)S(1)}, u32[]{:S(2)}, u32[]{:S(2)}) collective-permute-start(bf16[3,2,2,128,128]{4,3,2,1,0:T(8,128)(2,1)S(1)} %get-tuple-element.7), channel_id=1, source_target_pairs={{0,25},{1,12},{2,27},{3,14},{4,24},{5,29},{6,26},{7,31},{8,1},{9,2... | collective-permute-start | bytes 1179656 | tf_op jit(solution)/shard_map/ppermute | solution.py:211
  23.8 21.8 %collective-permute-done.8.refs_6_ = bf16[4,2,2,128,128]{4,3,2,1,0:T(8,128)(2,1)S(1)} collective-permute-done((bf16[4,2,2,128,128]{4,3,2,1,0:T(8,128)(2,1)S(1)}, bf16[4,2,2,128,128]{4,3,2,1,0:T(8,128)(2,1)S(1)}, u32[]{:S(2)}, u32[]{:S(2)}) %collective-permute-start.8) | collective-permute-done | bytes 524320 | tf_op jit(solution)/shard_map/ppermute | solution.py:211
  45.6 0.0 collective-permute-start.9
  45.6 7.4 %collective-permute-done.4.refs_2_ = bf16[3,2,2,128,128]{4,3,2,1,0:T(8,128)(2,1)S(1)} collective-permute-done((bf16[3,2,2,128,128]{4,3,2,1,0:T(8,128)(2,1)S(1)}, bf16[3,2,2,128,128]{4,3,2,1,0:T(8,128)(2,1)S(1)}, u32[]{:S(2)}, u32[]{:S(2)}) %collective-permute-start.4) | collective-permute-done | bytes 393248 | tf_op jit(solution)/shard_map/ppermute | solution.py:211
  53.0 0.0 collective-permute-start.5
  53.0 0.0 collective-permute-done.6.refs_4_
  53.0 1.3 %collective-permute-start.7 = (bf16[3,2,2,128,128]{4,3,2,1,0:T(8,128)(2,1)S(1)}, bf16[3,2,2,128,128]{4,3,2,1,0:T(8,128)(2,1)S(1)}, u32[]{:S(2)}, u32[]{:S(2)}) collective-permute-start(bf16[3,2,2,128,128]{4,3,2,1,0:T(8,128)(2,1)S(1)} %collective-permute-done.6.refs_4_), channel_id=1, source_target_pairs={{0,1},{1,0},{2,3},{3,2},{4,5},{5,4},{6,7},{7,6},{8,9},{9,8},{10,11... | collective-permute-start | bytes 1179656 | tf_op jit(solution)/shard_map/ppermute | solution.py:17
  54.3 0.4 collective-permute-done.5.refs_3_
  54.8 0.9 %collective-permute-done.7.refs_5_ = bf16[3,2,2,128,128]{4,3,2,1,0:T(8,128)(2,1)S(1)} collective-permute-done((bf16[3,2,2,128,128]{4,3,2,1,0:T(8,128)(2,1)S(1)}, bf16[3,2,2,128,128]{4,3,2,1,0:T(8,128)(2,1)S(1)}, u32[]{:S(2)}, u32[]{:S(2)}) %collective-permute-start.7) | collective-permute-done | bytes 393248 | tf_op jit(solution)/shard_map/ppermute | solution.py:17
  55.7 0.0 collective-permute-done.9.refs_7_
  55.7 0.0 copy-done
  55.7 2.5 %finish.1 = (f32[2,1,2,2,128,128]{5,4,3,2,1,0:T(8,128)}, f32[2,1,2,2,128,128]{5,4,3,2,1,0:T(8,128)}) custom-call(s32[25]{0:T(128)S(1)} %dynamic-slice_bitcast_fusion.line, s32[2,2]{1,0:T(2,128)S(1)} %bitcast.12, f32[2,2,2,128,128]{4,3,2,1,0:T(8,128)S(1)} %get-tuple-element.9.refs_0_, f32[2,1,2,2,128,128]{5,4,3,2,1,0:T(8,128)S(1)} %copy-done, ...), custom_call_target="tpu_custom_call" | custom-call | tf_op jit(solution)/shard_map/finish/pallas_call | solution.py:241
  (5 shorter events, 0.2 us)
Async XLA Ops:
  0.6 1.1 %copy-start.2 = (bf16[2,1,2,2,128,128]{5,4,3,2,1,0:T(8,128)(2,1)S(1)}, bf16[2,1,2,2,128,128]{5,4,3,2,1,0:T(8,128)(2,1)}, u32[]{:S(2)}) copy-start(bf16[2,1,2,2,128,128]{5,4,3,2,1,0:T(8,128)(2,1)} %param.4) | copy-start | bytes 786436
  1.9 1.3 %copy-start.1 = (s32[2,1,2]{2,1,0:T(1,128)S(1)}, s32[2,1,2]{2,1,0:T(1,128)}, u32[]{:S(2)}) copy-start(s32[2,1,2]{2,1,0:T(1,128)} %param.6) | copy-start | bytes 52
  1.9 12.9 %collective-permute-start.2 = (bf16[2,2,512,128]{3,2,0,1:T(8,128)(2,1)S(1)}, bf16[2,2,512,128]{3,2,0,1:T(8,128)(2,1)S(1)}, u32[]{:S(2)}, u32[]{:S(2)}) collective-permute-start(bf16[2,2,512,128]{3,2,0,1:T(8,128)(2,1)S(1)} %bitcast.13), channel_id=1, source_target_pairs={{0,2},{1,3},{2,0},{3,1},{4,6},{5,7},{6,4},{7,5},{8,10},{9,11},{10,... | collective-permute-start | bytes 1572872 | tf_op jit(solution)/shard_map/ppermute | solution.py:17
  2.2 12.6 %collective-permute-start.1 = (bf16[2,2,512,128]{3,2,0,1:T(8,128)(2,1)S(1)}, bf16[2,2,512,128]{3,2,0,1:T(8,128)(2,1)S(1)}, u32[]{:S(2)}, u32[]{:S(2)}) collective-permute-start(bf16[2,2,512,128]{3,2,0,1:T(8,128)(2,1)S(1)} %bitcast.14), channel_id=1, source_target_pairs={{0,1},{1,0},{2,3},{3,2},{4,5},{5,4},{6,7},{7,6},{8,9},{9,8},{10,11... | collective-permute-start | bytes 1572872 | tf_op jit(solution)/shard_map/ppermute | solution.py:17
  3.1 11.7 %collective-permute-start = (s32[2,2]{1,0:T(2,128)S(1)}, s32[2,2]{1,0:T(2,128)S(1)}, u32[]{:S(2)}, u32[]{:S(2)}) collective-permute-start(s32[2,2]{1,0:T(2,128)S(1)} %bitcast.9), channel_id=1, source_target_pairs={{0,1},{1,0},{2,3},{3,2},{4,5},{5,4},{6,7},{7,6},{8,9},{9,8},{10,11... | collective-permute-start | bytes 56 | tf_op jit(solution)/shard_map/ppermute | solution.py:17
  17.0 38.7 %copy-start = (f32[2,1,2,2,128,128]{5,4,3,2,1,0:T(8,128)S(1)}, f32[2,1,2,2,128,128]{5,4,3,2,1,0:T(8,128)}, u32[]{:S(2)}) copy-start(f32[2,1,2,2,128,128]{5,4,3,2,1,0:T(8,128)} %refs_1_.1) | copy-start | bytes 1572868
  17.0 2.7 %collective-permute-start.3 = (bf16[2,512,128]{2,1,0:T(8,128)(2,1)S(1)}, bf16[2,512,128]{2,1,0:T(8,128)(2,1)S(1)}, u32[]{:S(2)}, u32[]{:S(2)}) collective-permute-start(bf16[2,512,128]{2,1,0:T(8,128)(2,1)S(1)} %slice_bitcast_fusion), channel_id=1, source_target_pairs={{0,1},{1,0},{2,3},{3,2},{4,5},{5,4},{6,7},{7,6},{8,9},{9,8},{10,11... | collective-permute-start | bytes 786440 | tf_op jit(solution)/shard_map/ppermute | solution.py:17
  21.3 24.3 %collective-permute-start.8 = (bf16[4,2,2,128,128]{4,3,2,1,0:T(8,128)(2,1)S(1)}, bf16[4,2,2,128,128]{4,3,2,1,0:T(8,128)(2,1)S(1)}, u32[]{:S(2)}, u32[]{:S(2)}) collective-permute-start(bf16[4,2,2,128,128]{4,3,2,1,0:T(8,128)(2,1)S(1)} %get-tuple-element.11), channel_id=1, source_target_pairs={{1,20},{0,5},{3,22},{2,7},{4,0},{5,17},{6,2},{7,19},{9,28},{8,13},... | collective-permute-start | bytes 1572872 | tf_op jit(solution)/shard_map/ppermute | solution.py:211
  21.4 31.6 %collective-permute-start.4 = (bf16[3,2,2,128,128]{4,3,2,1,0:T(8,128)(2,1)S(1)}, bf16[3,2,2,128,128]{4,3,2,1,0:T(8,128)(2,1)S(1)}, u32[]{:S(2)}, u32[]{:S(2)}) collective-permute-start(bf16[3,2,2,128,128]{4,3,2,1,0:T(8,128)(2,1)S(1)} %get-tuple-element.10), channel_id=1, source_target_pairs={{1,28},{0,9},{3,30},{2,11},{4,8},{5,13},{6,10},{7,15},{9,4},{8,17}... | collective-permute-start | bytes 1179656 | tf_op jit(solution)/shard_map/ppermute | solution.py:211
  23.1 29.9 %collective-permute-start.6 = (bf16[3,2,2,128,128]{4,3,2,1,0:T(8,128)(2,1)S(1)}, bf16[3,2,2,128,128]{4,3,2,1,0:T(8,128)(2,1)S(1)}, u32[]{:S(2)}, u32[]{:S(2)}) collective-permute-start(bf16[3,2,2,128,128]{4,3,2,1,0:T(8,128)(2,1)S(1)} %get-tuple-element.7), channel_id=1, source_target_pairs={{0,25},{1,12},{2,27},{3,14},{4,24},{5,29},{6,26},{7,31},{8,1},{9,2... | collective-permute-start | bytes 1179656 | tf_op jit(solution)/shard_map/ppermute | solution.py:211
  45.6 10.1 %collective-permute-start.9 = (bf16[4,2,2,128,128]{4,3,2,1,0:T(8,128)(2,1)S(1)}, bf16[4,2,2,128,128]{4,3,2,1,0:T(8,128)(2,1)S(1)}, u32[]{:S(2)}, u32[]{:S(2)}) collective-permute-start(bf16[4,2,2,128,128]{4,3,2,1,0:T(8,128)(2,1)S(1)} %collective-permute-done.8.refs_6_), channel_id=1, source_target_pairs={{0,1},{1,0},{2,3},{3,2},{4,5},{5,4},{6,7},{7,6},{8,9},{9,8},{10,11... | collective-permute-start | bytes 1572872 | tf_op jit(solution)/shard_map/ppermute | solution.py:17
  53.0 1.7 %collective-permute-start.5 = (bf16[3,2,2,128,128]{4,3,2,1,0:T(8,128)(2,1)S(1)}, bf16[3,2,2,128,128]{4,3,2,1,0:T(8,128)(2,1)S(1)}, u32[]{:S(2)}, u32[]{:S(2)}) collective-permute-start(bf16[3,2,2,128,128]{4,3,2,1,0:T(8,128)(2,1)S(1)} %collective-permute-done.4.refs_2_), channel_id=1, source_target_pairs={{0,1},{1,0},{2,3},{3,2},{4,5},{5,4},{6,7},{7,6},{8,9},{9,8},{10,11... | collective-permute-start | bytes 1179656 | tf_op jit(solution)/shard_map/ppermute | solution.py:17
  53.0 2.7 %collective-permute-start.7 = (bf16[3,2,2,128,128]{4,3,2,1,0:T(8,128)(2,1)S(1)}, bf16[3,2,2,128,128]{4,3,2,1,0:T(8,128)(2,1)S(1)}, u32[]{:S(2)}, u32[]{:S(2)}) collective-permute-start(bf16[3,2,2,128,128]{4,3,2,1,0:T(8,128)(2,1)S(1)} %collective-permute-done.6.refs_4_), channel_id=1, source_target_pairs={{0,1},{1,0},{2,3},{3,2},{4,5},{5,4},{6,7},{7,6},{8,9},{9,8},{10,11... | collective-permute-start | bytes 1179656 | tf_op jit(solution)/shard_map/ppermute | solution.py:17

commit v3 on v2

--- a/solution.py
+++ b/solution.py
@@ -10,6 +10,8 @@
 
 
 SLOTS = 2
+B1 = ()
+B2 = (0,)
 PAIR = 2
 
 
@@ -67,8 +69,7 @@
     def way(self, row, first, offset, target, group_count):
         if (target % group_count) // PAIR == (row % group_count) // PAIR:
             return 2, first + (target + (offset > 0)) % PAIR, int(offset > 0)
-        turn = int(offset == -2 or abs(offset) == 3)
-        return turn, first + target % PAIR, int(abs(offset) == 2)
+        return int(offset < 0), first + target % PAIR, int(abs(offset) == 2)
 
     def blocks(self, row, first, target, row_count, group_count):
         found = []
@@ -85,6 +86,17 @@
         return found
 
 
+def pack_kernel(energy, state, *outs):
+    rows, _, slots, parts, size, _ = energy.shape
+    for slot in range(slots):
+        for row in range(rows):
+            for part in range(parts):
+                outs[slot][row, part * size:(part + 1) * size] = energy[row, 0, slot, part]
+                outs[slot][row, (parts + part) * size:(parts + part + 1) * size] = state[
+                    row, 0, slot, part
+                ].astype(jnp.bfloat16)
+
+
 def fill_right(right, row, place, stack, size):
     energy_re = stack[0 * size:1 * size]
     energy_im = stack[1 * size:2 * size]
@@ -106,47 +118,42 @@
     )
 
 
-def chosen(index, values):
-    out = values[0]
-    for place in range(1, len(values)):
-        out = jnp.where(index == place, values[place], out)
-    return out
-
-
-def terms_kernel(plan, turns, group_count, rows, size, line, own_cols, near_cols, *refs):
-    stacks = refs[:-len(turns) - 2]
-    outs = refs[-len(turns) - 2:-2]
-    own, right = refs[-2:]
+def terms_kernel(plan, turn, held_codes, rows, size, line, own_cols, near_cols, *refs):
+    columns = refs[:PAIR * SLOTS]
+    targets = refs[PAIR * SLOTS:PAIR * SLOTS + len(held_codes)]
+    out, right = refs[PAIR * SLOTS + len(held_codes)], refs[-1]
     for row in range(rows):
-        for pair in range(PAIR):
-            for slot in range(SLOTS):
-                fill_right(right, row, pair * SLOTS + slot, stacks[pair][row, slot], size)
-    for turn, out in zip(turns, outs):
-        base = plan.send_at[turn]
-        held = line[base]
-        for row in range(rows):
-            values = [ref[row, held % SLOTS] for ref in stacks[:PAIR + 1]]
-            values += [ref[row] for ref in stacks[PAIR + 1:]]
-            left = chosen(held // SLOTS, values)
-            for place in range(plan.width[turn]):
-                code = jnp.maximum(line[base + 1 + place], 0)
-                pair = code // SLOTS
-                slot = code % SLOTS
-                full = times(left, right[row, code]).astype(jnp.bfloat16)
-                there = jnp.where(pair == 0, own_cols[row, slot], near_cols[row, slot]) % rows
-                out[place, there, 0] = full[:, :size]
-                out[place, there, 1] = full[:, size:]
-    if len(stacks) == group_count:
-        own_part(group_count, rows, size, own_cols, stacks, right, own)
-
-
-def own_part(group_count, rows, size, own_cols, stacks, right, out):
+        for code in range(PAIR * SLOTS):
+            fill_right(right, row, code, columns[code][row], size)
+    base = plan.send_at[turn]
+    held = line[base]
+    for row in range(rows):
+        left = targets[0][row]
+        for code, ref in zip(held_codes[1:], targets[1:]):
+            left = jnp.where(held == code, ref[row], left)
+        for place in range(plan.width[turn]):
+            code = jnp.maximum(line[base + 1 + place], 0)
+            pair = code // SLOTS
+            slot = code % SLOTS
+            full = times(left, right[row, code]).astype(jnp.bfloat16)
+            there = jnp.where(pair == 0, own_cols[row, slot], near_cols[row, slot]) % rows
+            out[place, there, 0] = full[:, :size]
+            out[place, there, 1] = full[:, size:]
+
+
+def own_kernel(group_count, rows, size, own_cols, *refs):
+    firsts = refs[SLOTS:SLOTS + group_count]
+    out, right = refs[-2:]
     me = lax.axis_index("row")
     col = lax.axis_index("col")
+    for row in range(rows):
+        for slot in range(SLOTS):
+            fill_right(right, row, slot, refs[slot][row], size)
     held = (me % group_count) ^ col
     for row in range(rows):
-        values = [ref[row, 0] for ref in stacks[:PAIR + 1]] + [ref[row] for ref in stacks[PAIR + 1:]]
-        left = chosen(held, values)
+        left = firsts[0][row]
+        for place in range(1, group_count):
+            left = jnp.where(held == place, firsts[place][row], left)
         for slot in range(SLOTS):
             full = times(left, right[row, slot])
             out[row, slot, 0] = full[:, :size]
@@ -157,7 +164,7 @@
         for row in range(rows):
             partner = own_cols[row, 1] % rows
             for slot in range(SLOTS):
-                full = times(stacks[0][partner, 1], right[partner, 1 - slot])
+                full = times(refs[1][partner], right[partner, 1 - slot])
                 out[row, slot, 0] += full[:, :size]
                 out[row, slot, 1] += full[:, size:]
 
@@ -186,41 +193,68 @@
     device = lax.axis_index("row") * group_count + lax.axis_index("col")
     line = lax.dynamic_index_in_dim(jnp.asarray(plan.table), device, 0, keepdims=False)
     own_cols = block_cols[:, 0]
-    stack = jnp.stack([hamiltonian[:, 0], density[:, 0].astype(jnp.bfloat16)], axis=2)
-    stack = stack.reshape(rows, slots, 2 * parts * size, size)
-    across = xor_col(stack, group_count, PAIR)
-    near = xor_col(stack, group_count, 1)
+    stacks = dict(enumerate(pl.pallas_call(
+        pack_kernel,
+        out_shape=[jax.ShapeDtypeStruct((rows, 2 * parts * size, size), jnp.bfloat16)] * slots,
+        in_specs=[vmem] * 2,
+        out_specs=[vmem] * slots,
+        compiler_params=params,
+        name="pack",
+    )(hamiltonian, density)))
+    for slot in range(SLOTS):
+        stacks[PAIR * SLOTS + slot] = xor_col(stacks[slot], group_count, PAIR)
+        stacks[SLOTS + slot] = xor_col(stacks[slot], group_count, 1)
     near_cols = xor_col(own_cols, group_count, 1)
+    columns = [stacks[code] for code in range(PAIR * SLOTS)]
 
     arrived = {}
 
-    def send(turns, stacks):
-        *sent, own = pl.pallas_call(
-            functools.partial(terms_kernel, plan, turns, group_count, rows, size),
-            out_shape=[
-                jax.ShapeDtypeStruct((plan.width[turn], rows, parts, size, size), jnp.bfloat16)
-                for turn in turns
-            ] + [jax.ShapeDtypeStruct((rows, slots, parts, size, size), jnp.float32)],
-            in_specs=[smem, smem, smem] + [vmem] * len(stacks),
-            out_specs=[vmem] * (len(turns) + 1),
+    def send(turn, held_codes, after=()):
+        sent = pl.pallas_call(
+            functools.partial(terms_kernel, plan, turn, held_codes, rows, size),
+            out_shape=jax.ShapeDtypeStruct(
+                (plan.width[turn], rows, parts, size, size), jnp.bfloat16
+            ),
+            in_specs=[smem, smem, smem] + [vmem] * (len(columns) + len(held_codes)),
+            out_specs=vmem,
             scratch_shapes=[pltpu.VMEM((rows, PAIR * SLOTS, 4 * size, 2 * size), jnp.bfloat16)],
             compiler_params=params,
-            name="terms_%d" % turns[0],
-        )(line, own_cols, near_cols, *stacks)
-        for turn, one in zip(turns, sent):
-            arrived[turn] = lax.ppermute(one, ("row", "col"), plan.pairs[turn])
-        return sent, own
-
-    sent, _ = send(plan.turns[:2], [stack, near, across])
-    across_first, _ = lax.optimization_barrier((across[:, 0], sent[-1]))
-    diagonal = xor_col(across_first, group_count, 1)
-    _, own = send(plan.turns[2:], [stack, near, across, diagonal])
+            name="terms_%d" % turn,
+        )(line, own_cols, near_cols, *columns, *[stacks[code] for code in held_codes])
+        for other in after:
+            sent, arrived[other] = lax.optimization_barrier((sent, arrived[other]))
+        return sent, lax.ppermute(sent, ("row", "col"), plan.pairs[turn])
+
+    ahead, behind = PAIR * SLOTS, PAIR * SLOTS + 1
+    corner = ahead + SLOTS
+    sent, arrived[0] = send(0, [0, ahead])
+    first, _ = lax.optimization_barrier((stacks[ahead], sent))
+    stacks[corner] = xor_col(first, group_count, 1)
+    sent, arrived[1] = send(1, [1, behind], B1)
+    _, arrived[2] = send(2, [1, SLOTS, behind, corner], B2)
+
+    own = pl.pallas_call(
+        functools.partial(own_kernel, group_count, rows, size),
+        out_shape=jax.ShapeDtypeStruct((rows, slots, parts, size, size), jnp.float32),
+        in_specs=[smem] + [vmem] * (SLOTS + group_count),
+        out_specs=vmem,
+        scratch_shapes=[pltpu.VMEM((rows, SLOTS, 4 * size, 2 * size), jnp.bfloat16)],
+        compiler_params=params,
+        name="own_terms",
+    )(own_cols, stacks[0], stacks[1], stacks[0], stacks[SLOTS], stacks[ahead], stacks[corner])
 
     terms = []
     places = []
+    swapped = None
     for turn, one in sorted(arrived.items()):
-        terms += [one, xor_col(one, group_count, 1)]
+        if swapped is not None:
+            one, swapped = lax.optimization_barrier((one, swapped))
+            terms.append(swapped)
+        swapped = xor_col(one, group_count, 1)
+        terms.append(one)
         places += [plan.find_at[turn, 0], plan.find_at[turn, 1]]
+
+    terms.append(swapped)
 
     block = (1, 1, 1, parts, size, size)
 

time: 58.4 us -> 51.4 us (0.88)
  the two profiles are of different devices: /device:TPU:23 before, /device:TPU:3 now
where the time goes in v3:
time: 51.4 us; the launch traced here: 51.1 us
  starting transfers between devices  24.9 us (48%)
  waiting for transfers between devices  14.4 us (28%)
  Pallas kernels  7.81 us (15%)
  local copies, waits for them, and re-layouts  3.36 us (7%)
  between operations  0.7 us (1%)
    ppermute x9, starting transfers between devices, xor_col(): return lax.ppermute(value, 'col', [(i, i ^ by) for i in range(group_count)])  21.1 us
    ppermute x3, waiting for transfers between devices, send(): return (sent, lax.ppermute(sent, ('row', 'col'), plan.pairs[turn]))  7.98 us
    ppermute x9, waiting for transfers between devices, xor_col(): return lax.ppermute(value, 'col', [(i, i ^ by) for i in range(group_count)])  6.4 us
    pallas_call x3, Pallas kernels, send(): pl.pallas_call(functools.partial(terms_kernel, plan, turn, held_codes, ro...  3.9 us
    ppermute x3, starting transfers between devices, send(): return (sent, lax.ppermute(sent, ('row', 'col'), plan.pairs[turn]))  3.78 us
    unnamed x8, local copies, waits for them, and re-layouts  2.67 us
    pallas_call x1, Pallas kernels, body(): pl.pallas_call(functools.partial(finish_kernel, places), out_shape=[jax.S...  2.42 us
    pallas_call x1, Pallas kernels, body(): pl.pallas_call(functools.partial(own_kernel, group_count, rows, size), ou...  1.44 us
  transfers between devices with their start and end apart: 12, of which 6 were waited for; matrix products, arithmetic and copies ran while one was open for 1% of the time, Pallas kernels for 8%

profile of v3, /device:TPU:3, one launch (start us, length us, event | category | flops | bytes accessed | tf_op | source)
XLA Modules:
  0.0 51.1 jit_solution(8559262421066565279)
XLA Ops:
  0.6 0.0 copy-start
  0.6 1.0 %copy-done = f32[2,1,2,2,128,128]{5,4,3,2,1,0:T(8,128)S(1)} copy-done((f32[2,1,2,2,128,128]{5,4,3,2,1,0:T(8,128)S(1)}, f32[2,1,2,2,128,128]{5,4,3,2,1,0:T(8,128)}, u32[]{:S(2)}) %copy-start) | copy-done | bytes 524312
  1.7 0.0 copy-start.2
  1.7 0.9 %copy-done.2 = bf16[2,1,2,2,128,128]{5,4,3,2,1,0:T(8,128)(2,1)S(1)} copy-done((bf16[2,1,2,2,128,128]{5,4,3,2,1,0:T(8,128)(2,1)S(1)}, bf16[2,1,2,2,128,128]{5,4,3,2,1,0:T(8,128)(2,1)}, u32[]{:S(2)}) %copy-start.2) | copy-done | bytes 262168
  2.7 1.3 %collective-permute-start.1 = (bf16[2,512,128]{2,1,0:T(8,128)(2,1)S(1)}, bf16[2,512,128]{2,1,0:T(8,128)(2,1)S(1)}, u32[]{:S(2)}, u32[]{:S(2)}) collective-permute-start(bf16[2,512,128]{2,1,0:T(8,128)(2,1)S(1)} %get-tuple-element.11.refs_0_.refs_4_.refs_2_), channel_id=1, source_target_pairs={{0,2},{1,3},{2,0},{3,1},{4,6},{5,7},{6,4},{7,5},{8,10},{9,11},{10,... | collective-permute-start | bytes 786440 | tf_op jit(solution)/shard_map/ppermute | solution.py:19
  4.0 1.0 %collective-permute-start = (bf16[2,512,128]{2,1,0:T(8,128)(2,1)S(1)}, bf16[2,512,128]{2,1,0:T(8,128)(2,1)S(1)}, u32[]{:S(2)}, u32[]{:S(2)}) collective-permute-start(bf16[2,512,128]{2,1,0:T(8,128)(2,1)S(1)} %get-tuple-element.11.refs_0_.refs_4_.refs_2_), channel_id=1, source_target_pairs={{0,1},{1,0},{2,3},{3,2},{4,5},{5,4},{6,7},{7,6},{8,9},{9,8},{10,11... | collective-permute-start | bytes 786440 | tf_op jit(solution)/shard_map/ppermute | solution.py:19
  4.9 0.0 copy-start.3
  4.9 0.0 collective-permute-start.3
  4.9 0.7 %copy-done.3 = s32[2,1,2]{2,1,0:T(1,128)S(1)} copy-done((s32[2,1,2]{2,1,0:T(1,128)S(1)}, s32[2,1,2]{2,1,0:T(1,128)}, u32[]{:S(2)}) %copy-start.3) | copy-done | bytes 40
  5.6 0.0 collective-permute-start.2
  5.6 0.7 %dynamic-slice_bitcast_fusion.line = s32[25]{0:T(128)S(1)} fusion(s32[32,25]{1,0:T(8,128)} %constant.19.clone, s32[]{:T(128)S(6)} %select_n.4), kind=kLoop, calls=%fused_computation | loop fusion | bytes 204 | tf_op jit(solution)/shard_map/jit(dynamic_index_in_dim)/squeeze | solution.py:194
  6.3 0.4 collective-permute-done.2.near_cols
  6.8 3.2 %collective-permute-done.1.refs_5_.refs_4_ = bf16[2,512,128]{2,1,0:T(8,128)(2,1)S(1)} collective-permute-done((bf16[2,512,128]{2,1,0:T(8,128)(2,1)S(1)}, bf16[2,512,128]{2,1,0:T(8,128)(2,1)S(1)}, u32[]{:S(2)}, u32[]{:S(2)}) %collective-permute-start.1) | collective-permute-done | bytes 262176 | tf_op jit(solution)/shard_map/ppermute | solution.py:19
  9.9 0.0 collective-permute-done.refs_2_.refs_3_.refs_5_
  9.9 0.0 collective-permute-done.3.refs_3_
  9.9 1.3 %terms_0.1 = bf16[3,2,2,128,128]{4,3,2,1,0:T(8,128)(2,1)S(1)} custom-call(s32[25]{0:T(128)S(1)} %dynamic-slice_bitcast_fusion.line, s32[2,2]{1,0:T(2,128)S(1)} %bitcast.4, s32[2,2]{1,0:T(2,128)S(1)} %collective-permute-done.2.near_cols, bf16[2,512,128]{2,1,0:T(8,128)(2,1)S(1)} %get-tuple-element.11.refs_0_.refs_4_.refs_2_, ...), custom_call_target="tpu_custom_call" | custom-call | tf_op jit(solution)/shard_map/terms_0/pallas_call | solution.py:213
  11.2 1.4 %collective-permute-start.6 = (bf16[3,2,2,128,128]{4,3,2,1,0:T(8,128)(2,1)S(1)}, bf16[3,2,2,128,128]{4,3,2,1,0:T(8,128)(2,1)S(1)}, u32[]{:S(2)}, u32[]{:S(2)}) collective-permute-start(bf16[3,2,2,128,128]{4,3,2,1,0:T(8,128)(2,1)S(1)} %terms_0.1), channel_id=1, source_target_pairs={{0,9},{1,12},{2,11},{3,14},{4,8},{5,13},{6,10},{7,15},{8,17},{9,20... | collective-permute-start | bytes 1179656 | tf_op jit(solution)/shard_map/ppermute | solution.py:226
  12.6 1.2 %collective-permute-start.5 = (bf16[2,512,128]{2,1,0:T(8,128)(2,1)S(1)}, bf16[2,512,128]{2,1,0:T(8,128)(2,1)S(1)}, u32[]{:S(2)}, u32[]{:S(2)}) collective-permute-start(bf16[2,512,128]{2,1,0:T(8,128)(2,1)S(1)} %get-tuple-element.12.refs_1_.refs_4_), channel_id=1, source_target_pairs={{0,2},{1,3},{2,0},{3,1},{4,6},{5,7},{6,4},{7,5},{8,10},{9,11},{10,... | collective-permute-start | bytes 786440 | tf_op jit(solution)/shard_map/ppermute | solution.py:19
  13.8 2.1 %collective-permute-start.4 = (bf16[2,512,128]{2,1,0:T(8,128)(2,1)S(1)}, bf16[2,512,128]{2,1,0:T(8,128)(2,1)S(1)}, u32[]{:S(2)}, u32[]{:S(2)}) collective-permute-start(bf16[2,512,128]{2,1,0:T(8,128)(2,1)S(1)} %collective-permute-done.1.refs_5_.refs_4_), channel_id=1, source_target_pairs={{0,1},{1,0},{2,3},{3,2},{4,5},{5,4},{6,7},{7,6},{8,9},{9,8},{10,11... | collective-permute-start | bytes 786440 | tf_op jit(solution)/shard_map/ppermute | solution.py:19
  15.9 2.7 %collective-permute-done.5.refs_6_.refs_5_ = bf16[2,512,128]{2,1,0:T(8,128)(2,1)S(1)} collective-permute-done((bf16[2,512,128]{2,1,0:T(8,128)(2,1)S(1)}, bf16[2,512,128]{2,1,0:T(8,128)(2,1)S(1)}, u32[]{:S(2)}, u32[]{:S(2)}) %collective-permute-start.5) | collective-permute-done | bytes 262176 | tf_op jit(solution)/shard_map/ppermute | solution.py:19
  18.6 1.3 %terms_1.1 = bf16[3,2,2,128,128]{4,3,2,1,0:T(8,128)(2,1)S(1)} custom-call(s32[25]{0:T(128)S(1)} %dynamic-slice_bitcast_fusion.line, s32[2,2]{1,0:T(2,128)S(1)} %bitcast.5, s32[2,2]{1,0:T(2,128)S(1)} %collective-permute-done.2.near_cols, bf16[2,512,128]{2,1,0:T(8,128)(2,1)S(1)} %get-tuple-element.11.refs_0_.refs_4_.refs_2_, ...), custom_call_target="tpu_custom_call" | custom-call | tf_op jit(solution)/shard_map/terms_1/pallas_call | solution.py:213
  19.8 2.4 %collective-permute-start.7 = (bf16[3,2,2,128,128]{4,3,2,1,0:T(8,128)(2,1)S(1)}, bf16[3,2,2,128,128]{4,3,2,1,0:T(8,128)(2,1)S(1)}, u32[]{:S(2)}, u32[]{:S(2)}) collective-permute-start(bf16[3,2,2,128,128]{4,3,2,1,0:T(8,128)(2,1)S(1)} %terms_1.1), channel_id=1, source_target_pairs={{0,25},{1,28},{2,27},{3,30},{4,24},{5,29},{6,26},{7,31},{8,1},{9,4... | collective-permute-start | bytes 1179656 | tf_op jit(solution)/shard_map/ppermute | solution.py:226
  22.3 0.0 collective-permute-done.4.refs_5_.refs_7_
  22.3 1.4 %terms_2.1 = bf16[4,2,2,128,128]{4,3,2,1,0:T(8,128)(2,1)S(1)} custom-call(s32[25]{0:T(128)S(1)} %dynamic-slice_bitcast_fusion.line, s32[2,2]{1,0:T(2,128)S(1)} %bitcast.6, s32[2,2]{1,0:T(2,128)S(1)} %collective-permute-done.2.near_cols, bf16[2,512,128]{2,1,0:T(8,128)(2,1)S(1)} %get-tuple-element.11.refs_0_.refs_4_.refs_2_, ...), custom_call_target="tpu_custom_call" | custom-call | tf_op jit(solution)/shard_map/terms_2/pallas_call | solution.py:213
  23.6 0.0 copy-start.1
  23.6 0.0 collective-permute-done.6.refs_2_
  23.7 4.6 %collective-permute-start.8 = (bf16[3,2,2,128,128]{4,3,2,1,0:T(8,128)(2,1)S(1)}, bf16[3,2,2,128,128]{4,3,2,1,0:T(8,128)(2,1)S(1)}, u32[]{:S(2)}, u32[]{:S(2)}) collective-permute-start(bf16[3,2,2,128,128]{4,3,2,1,0:T(8,128)(2,1)S(1)} %collective-permute-done.6.refs_2_), channel_id=1, source_target_pairs={{0,1},{1,0},{2,3},{3,2},{4,5},{5,4},{6,7},{7,6},{8,9},{9,8},{10,11... | collective-permute-start | bytes 1179656 | tf_op jit(solution)/shard_map/ppermute | solution.py:19
  28.2 0.0 collective-permute-start.9
  28.2 3.3 %collective-permute-done.7.refs_4_ = bf16[3,2,2,128,128]{4,3,2,1,0:T(8,128)(2,1)S(1)} collective-permute-done((bf16[3,2,2,128,128]{4,3,2,1,0:T(8,128)(2,1)S(1)}, bf16[3,2,2,128,128]{4,3,2,1,0:T(8,128)(2,1)S(1)}, u32[]{:S(2)}, u32[]{:S(2)}) %collective-permute-start.7) | collective-permute-done | bytes 393248 | tf_op jit(solution)/shard_map/ppermute | solution.py:226
  31.5 0.0 collective-permute-done.8.refs_3_
  31.5 3.4 %collective-permute-start.10 = (bf16[3,2,2,128,128]{4,3,2,1,0:T(8,128)(2,1)S(1)}, bf16[3,2,2,128,128]{4,3,2,1,0:T(8,128)(2,1)S(1)}, u32[]{:S(2)}, u32[]{:S(2)}) collective-permute-start(bf16[3,2,2,128,128]{4,3,2,1,0:T(8,128)(2,1)S(1)} %collective-permute-done.7.refs_4_), channel_id=1, source_target_pairs={{0,1},{1,0},{2,3},{3,2},{4,5},{5,4},{6,7},{7,6},{8,9},{9,8},{10,11... | collective-permute-start | bytes 1179656 | tf_op jit(solution)/shard_map/ppermute | solution.py:19
  35.0 4.7 %collective-permute-done.9.refs_6_ = bf16[4,2,2,128,128]{4,3,2,1,0:T(8,128)(2,1)S(1)} collective-permute-done((bf16[4,2,2,128,128]{4,3,2,1,0:T(8,128)(2,1)S(1)}, bf16[4,2,2,128,128]{4,3,2,1,0:T(8,128)(2,1)S(1)}, u32[]{:S(2)}, u32[]{:S(2)}) %collective-permute-start.9) | collective-permute-done | bytes 524320 | tf_op jit(solution)/shard_map/ppermute | solution.py:226
  39.6 0.0 collective-permute-done.10.refs_5_
  39.6 7.5 %collective-permute-start.11 = (bf16[4,2,2,128,128]{4,3,2,1,0:T(8,128)(2,1)S(1)}, bf16[4,2,2,128,128]{4,3,2,1,0:T(8,128)(2,1)S(1)}, u32[]{:S(2)}, u32[]{:S(2)}) collective-permute-start(bf16[4,2,2,128,128]{4,3,2,1,0:T(8,128)(2,1)S(1)} %collective-permute-done.9.refs_6_), channel_id=1, source_target_pairs={{0,1},{1,0},{2,3},{3,2},{4,5},{5,4},{6,7},{7,6},{8,9},{9,8},{10,11... | collective-permute-start | bytes 1572872 | tf_op jit(solution)/shard_map/ppermute | solution.py:19
  47.2 1.4 %own_terms.1.refs_0_ = f32[2,2,2,128,128]{4,3,2,1,0:T(8,128)S(1)} custom-call(s32[2,2]{1,0:T(2,128)S(1)} %bitcast.7, bf16[2,512,128]{2,1,0:T(8,128)(2,1)S(1)} %get-tuple-element.11.refs_0_.refs_4_.refs_2_, bf16[2,512,128]{2,1,0:T(8,128)(2,1)S(1)} %get-tuple-element.12.refs_1_.refs_4_, bf16[2,512,128]{2,1,0:T(8,128)(2,1)S(1)} %get-tuple-element.11.refs_0_.refs_4_.refs_2_, ...), custom_call_target="tpu_custom_call" | custom-call | tf_op jit(solution)/shard_map/own_terms/pallas_call | solution.py:236
  48.6 0.1 collective-permute-done.11.refs_7_
  48.7 0.0 copy-done.1
  48.7 2.4 %finish.1 = (f32[2,1,2,2,128,128]{5,4,3,2,1,0:T(8,128)}, f32[2,1,2,2,128,128]{5,4,3,2,1,0:T(8,128)}) custom-call(s32[25]{0:T(128)S(1)} %dynamic-slice_bitcast_fusion.line, s32[2,2]{1,0:T(2,128)S(1)} %bitcast.8, f32[2,2,2,128,128]{4,3,2,1,0:T(8,128)S(1)} %own_terms.1.refs_0_, f32[2,1,2,2,128,128]{5,4,3,2,1,0:T(8,128)S(1)} %copy-done.1, ...), custom_call_target="tpu_custom_call" | custom-call | tf_op jit(solution)/shard_map/finish/pallas_call | solution.py:275
  (1 shorter events, 0.0 us)
Async XLA Ops:
  0.6 1.0 %copy-start = (f32[2,1,2,2,128,128]{5,4,3,2,1,0:T(8,128)S(1)}, f32[2,1,2,2,128,128]{5,4,3,2,1,0:T(8,128)}, u32[]{:S(2)}) copy-start(f32[2,1,2,2,128,128]{5,4,3,2,1,0:T(8,128)} %refs_1_.1) | copy-start | bytes 1572868
  1.7 0.9 %copy-start.2 = (bf16[2,1,2,2,128,128]{5,4,3,2,1,0:T(8,128)(2,1)S(1)}, bf16[2,1,2,2,128,128]{5,4,3,2,1,0:T(8,128)(2,1)}, u32[]{:S(2)}) copy-start(bf16[2,1,2,2,128,128]{5,4,3,2,1,0:T(8,128)(2,1)} %energy.1) | copy-start | bytes 786436
  2.7 7.2 %collective-permute-start.1 = (bf16[2,512,128]{2,1,0:T(8,128)(2,1)S(1)}, bf16[2,512,128]{2,1,0:T(8,128)(2,1)S(1)}, u32[]{:S(2)}, u32[]{:S(2)}) collective-permute-start(bf16[2,512,128]{2,1,0:T(8,128)(2,1)S(1)} %get-tuple-element.11.refs_0_.refs_4_.refs_2_), channel_id=1, source_target_pairs={{0,2},{1,3},{2,0},{3,1},{4,6},{5,7},{6,4},{7,5},{8,10},{9,11},{10,... | collective-permute-start | bytes 786440 | tf_op jit(solution)/shard_map/ppermute | solution.py:19
  4.0 5.9 %collective-permute-start = (bf16[2,512,128]{2,1,0:T(8,128)(2,1)S(1)}, bf16[2,512,128]{2,1,0:T(8,128)(2,1)S(1)}, u32[]{:S(2)}, u32[]{:S(2)}) collective-permute-start(bf16[2,512,128]{2,1,0:T(8,128)(2,1)S(1)} %get-tuple-element.11.refs_0_.refs_4_.refs_2_), channel_id=1, source_target_pairs={{0,1},{1,0},{2,3},{3,2},{4,5},{5,4},{6,7},{7,6},{8,9},{9,8},{10,11... | collective-permute-start | bytes 786440 | tf_op jit(solution)/shard_map/ppermute | solution.py:19
  4.9 0.7 %copy-start.3 = (s32[2,1,2]{2,1,0:T(1,128)S(1)}, s32[2,1,2]{2,1,0:T(1,128)}, u32[]{:S(2)}) copy-start(s32[2,1,2]{2,1,0:T(1,128)} %param.6) | copy-start | bytes 52
  4.9 5.0 %collective-permute-start.3 = (bf16[2,512,128]{2,1,0:T(8,128)(2,1)S(1)}, bf16[2,512,128]{2,1,0:T(8,128)(2,1)S(1)}, u32[]{:S(2)}, u32[]{:S(2)}) collective-permute-start(bf16[2,512,128]{2,1,0:T(8,128)(2,1)S(1)} %get-tuple-element.12.refs_1_.refs_4_), channel_id=1, source_target_pairs={{0,1},{1,0},{2,3},{3,2},{4,5},{5,4},{6,7},{7,6},{8,9},{9,8},{10,11... | collective-permute-start | bytes 786440 | tf_op jit(solution)/shard_map/ppermute | solution.py:19
  5.6 1.1 %collective-permute-start.2 = (s32[2,2]{1,0:T(2,128)S(1)}, s32[2,2]{1,0:T(2,128)S(1)}, u32[]{:S(2)}, u32[]{:S(2)}) collective-permute-start(s32[2,2]{1,0:T(2,128)S(1)} %bitcast.3), channel_id=1, source_target_pairs={{0,1},{1,0},{2,3},{3,2},{4,5},{5,4},{6,7},{7,6},{8,9},{9,8},{10,11... | collective-permute-start | bytes 56 | tf_op jit(solution)/shard_map/ppermute | solution.py:19
  11.2 12.5 %collective-permute-start.6 = (bf16[3,2,2,128,128]{4,3,2,1,0:T(8,128)(2,1)S(1)}, bf16[3,2,2,128,128]{4,3,2,1,0:T(8,128)(2,1)S(1)}, u32[]{:S(2)}, u32[]{:S(2)}) collective-permute-start(bf16[3,2,2,128,128]{4,3,2,1,0:T(8,128)(2,1)S(1)} %terms_0.1), channel_id=1, source_target_pairs={{0,9},{1,12},{2,11},{3,14},{4,8},{5,13},{6,10},{7,15},{8,17},{9,20... | collective-permute-start | bytes 1179656 | tf_op jit(solution)/shard_map/ppermute | solution.py:226
  12.6 6.0 %collective-permute-start.5 = (bf16[2,512,128]{2,1,0:T(8,128)(2,1)S(1)}, bf16[2,512,128]{2,1,0:T(8,128)(2,1)S(1)}, u32[]{:S(2)}, u32[]{:S(2)}) collective-permute-start(bf16[2,512,128]{2,1,0:T(8,128)(2,1)S(1)} %get-tuple-element.12.refs_1_.refs_4_), channel_id=1, source_target_pairs={{0,2},{1,3},{2,0},{3,1},{4,6},{5,7},{6,4},{7,5},{8,10},{9,11},{10,... | collective-permute-start | bytes 786440 | tf_op jit(solution)/shard_map/ppermute | solution.py:19
  13.8 8.5 %collective-permute-start.4 = (bf16[2,512,128]{2,1,0:T(8,128)(2,1)S(1)}, bf16[2,512,128]{2,1,0:T(8,128)(2,1)S(1)}, u32[]{:S(2)}, u32[]{:S(2)}) collective-permute-start(bf16[2,512,128]{2,1,0:T(8,128)(2,1)S(1)} %collective-permute-done.1.refs_5_.refs_4_), channel_id=1, source_target_pairs={{0,1},{1,0},{2,3},{3,2},{4,5},{5,4},{6,7},{7,6},{8,9},{9,8},{10,11... | collective-permute-start | bytes 786440 | tf_op jit(solution)/shard_map/ppermute | solution.py:19
  19.8 11.7 %collective-permute-start.7 = (bf16[3,2,2,128,128]{4,3,2,1,0:T(8,128)(2,1)S(1)}, bf16[3,2,2,128,128]{4,3,2,1,0:T(8,128)(2,1)S(1)}, u32[]{:S(2)}, u32[]{:S(2)}) collective-permute-start(bf16[3,2,2,128,128]{4,3,2,1,0:T(8,128)(2,1)S(1)} %terms_1.1), channel_id=1, source_target_pairs={{0,25},{1,28},{2,27},{3,30},{4,24},{5,29},{6,26},{7,31},{8,1},{9,4... | collective-permute-start | bytes 1179656 | tf_op jit(solution)/shard_map/ppermute | solution.py:226
  23.6 25.1 %copy-start.1 = (f32[2,1,2,2,128,128]{5,4,3,2,1,0:T(8,128)S(1)}, f32[2,1,2,2,128,128]{5,4,3,2,1,0:T(8,128)}, u32[]{:S(2)}) copy-start(f32[2,1,2,2,128,128]{5,4,3,2,1,0:T(8,128)} %refs_1_.1) | copy-start | bytes 1572868
  23.7 7.9 %collective-permute-start.8 = (bf16[3,2,2,128,128]{4,3,2,1,0:T(8,128)(2,1)S(1)}, bf16[3,2,2,128,128]{4,3,2,1,0:T(8,128)(2,1)S(1)}, u32[]{:S(2)}, u32[]{:S(2)}) collective-permute-start(bf16[3,2,2,128,128]{4,3,2,1,0:T(8,128)(2,1)S(1)} %collective-permute-done.6.refs_2_), channel_id=1, source_target_pairs={{0,1},{1,0},{2,3},{3,2},{4,5},{5,4},{6,7},{7,6},{8,9},{9,8},{10,11... | collective-permute-start | bytes 1179656 | tf_op jit(solution)/shard_map/ppermute | solution.py:19
  28.2 11.4 %collective-permute-start.9 = (bf16[4,2,2,128,128]{4,3,2,1,0:T(8,128)(2,1)S(1)}, bf16[4,2,2,128,128]{4,3,2,1,0:T(8,128)(2,1)S(1)}, u32[]{:S(2)}, u32[]{:S(2)}) collective-permute-start(bf16[4,2,2,128,128]{4,3,2,1,0:T(8,128)(2,1)S(1)} %terms_2.1), channel_id=1, source_target_pairs={{1,20},{0,5},{3,22},{2,7},{4,0},{5,17},{6,2},{7,19},{9,28},{8,13},... | collective-permute-start | bytes 1572872 | tf_op jit(solution)/shard_map/ppermute | solution.py:226
  31.5 8.1 %collective-permute-start.10 = (bf16[3,2,2,128,128]{4,3,2,1,0:T(8,128)(2,1)S(1)}, bf16[3,2,2,128,128]{4,3,2,1,0:T(8,128)(2,1)S(1)}, u32[]{:S(2)}, u32[]{:S(2)}) collective-permute-start(bf16[3,2,2,128,128]{4,3,2,1,0:T(8,128)(2,1)S(1)} %collective-permute-done.7.refs_4_), channel_id=1, source_target_pairs={{0,1},{1,0},{2,3},{3,2},{4,5},{5,4},{6,7},{7,6},{8,9},{9,8},{10,11... | collective-permute-start | bytes 1179656 | tf_op jit(solution)/shard_map/ppermute | solution.py:19
  39.6 9.1 %collective-permute-start.11 = (bf16[4,2,2,128,128]{4,3,2,1,0:T(8,128)(2,1)S(1)}, bf16[4,2,2,128,128]{4,3,2,1,0:T(8,128)(2,1)S(1)}, u32[]{:S(2)}, u32[]{:S(2)}) collective-permute-start(bf16[4,2,2,128,128]{4,3,2,1,0:T(8,128)(2,1)S(1)} %collective-permute-done.9.refs_6_), channel_id=1, source_target_pairs={{0,1},{1,0},{2,3},{3,2},{4,5},{5,4},{6,7},{7,6},{8,9},{9,8},{10,11... | collective-permute-start | bytes 1572872 | tf_op jit(solution)/shard_map/ppermute | solution.py:19

commit v4 on v3

--- a/solution.py
+++ b/solution.py
@@ -10,8 +10,11 @@
 
 
 SLOTS = 2
+OWN = 0
+CHAIN = [(0, 1)]
+ORDER = (0, 1, 2)
 B1 = ()
-B2 = (0,)
+B2 = ()
 PAIR = 2
 
 
@@ -86,8 +89,20 @@
         return found
 
 
-def pack_kernel(energy, state, *outs):
+def same_pair(group_count):
+    pair = (lax.axis_index("row") % group_count) // PAIR
+    return (pair == lax.axis_index("col") // PAIR).astype(jnp.int32)
+
+
+def pack_kernel(group_count, energy, state, *outs):
     rows, _, slots, parts, size, _ = energy.shape
+    crossing = same_pair(group_count)
+    for row in range(rows):
+        for part in range(parts):
+            here = pl.ds(part * size, size)
+            there = pl.ds((parts + part) * size, size)
+            outs[slots][row, here] = energy[row, 0, crossing, part]
+            outs[slots][row, there] = state[row, 0, crossing, part].astype(jnp.bfloat16)
     for slot in range(slots):
         for row in range(rows):
             for part in range(parts):
@@ -169,18 +184,20 @@
                 out[row, slot, 1] += full[:, size:]
 
 
-def finish_kernel(places, line, cols, *refs):
-    count = len(places)
-    own, density = refs[0], refs[1]
-    commutator, section = refs[2 + count], refs[3 + count]
-    slot = pl.program_id(1)
-    commutator[0, 0, 0] = own[0, 0]
-    for place, ref in zip(places, refs[2:2 + count]):
-        @pl.when(line[place + slot] >= 0)
-        def _():
-            commutator[0, 0, 0] += ref[0, 0].astype(jnp.float32)
-    section[0, 0, 0, 0] = density[0, 0, 0, 0] + 0.05 * commutator[0, 0, 0, 1]
-    section[0, 0, 0, 1] = density[0, 0, 0, 1] - 0.05 * commutator[0, 0, 0, 0]
+def finish_kernel(places, line, cols, own, density, *refs):
+    terms = refs[:len(places)]
+    commutator, section = refs[len(places):]
+    rows, slots = own.shape[:2]
+    for row in range(rows):
+        for slot in range(slots):
+            total = own[row, slot]
+            for place, ref in zip(places, terms):
+                found = line[place + slot]
+                block = ref[jnp.maximum(found, 0), cols[row, slot] % rows]
+                total += jnp.where(found >= 0, block, 0.0).astype(jnp.float32)
+            commutator[row, 0, slot] = total
+            section[row, 0, slot, 0] = density[row, 0, slot, 0] + 0.05 * total[1]
+            section[row, 0, slot, 1] = density[row, 0, slot, 1] - 0.05 * total[0]
 
 
 def body(plan, hamiltonian, density, block_cols):
@@ -193,45 +210,45 @@
     device = lax.axis_index("row") * group_count + lax.axis_index("col")
     line = lax.dynamic_index_in_dim(jnp.asarray(plan.table), device, 0, keepdims=False)
     own_cols = block_cols[:, 0]
-    stacks = dict(enumerate(pl.pallas_call(
-        pack_kernel,
-        out_shape=[jax.ShapeDtypeStruct((rows, 2 * parts * size, size), jnp.bfloat16)] * slots,
+    own_0, own_1, first_out = pl.pallas_call(
+        functools.partial(pack_kernel, group_count),
+        out_shape=[jax.ShapeDtypeStruct((rows, 2 * parts * size, size), jnp.bfloat16)] * 3,
         in_specs=[vmem] * 2,
-        out_specs=[vmem] * slots,
+        out_specs=[vmem] * 3,
         compiler_params=params,
         name="pack",
-    )(hamiltonian, density)))
-    for slot in range(SLOTS):
-        stacks[PAIR * SLOTS + slot] = xor_col(stacks[slot], group_count, PAIR)
-        stacks[SLOTS + slot] = xor_col(stacks[slot], group_count, 1)
+    )(hamiltonian, density)
+    first_in = xor_col(first_out, group_count, PAIR)
+    near_0 = xor_col(own_0, group_count, 1)
+    near_1 = xor_col(own_1, group_count, 1)
+    second_out = jnp.where(same_pair(group_count) == 1, near_0, own_1)
+    second_in = xor_col(second_out, group_count, PAIR)
+    columns = [own_0, own_1, near_0, near_1]
     near_cols = xor_col(own_cols, group_count, 1)
-    columns = [stacks[code] for code in range(PAIR * SLOTS)]
 
     arrived = {}
 
-    def send(turn, held_codes, after=()):
+    def send(turn, held, after=()):
         sent = pl.pallas_call(
-            functools.partial(terms_kernel, plan, turn, held_codes, rows, size),
+            functools.partial(terms_kernel, plan, turn, list(held), rows, size),
             out_shape=jax.ShapeDtypeStruct(
                 (plan.width[turn], rows, parts, size, size), jnp.bfloat16
             ),
-            in_specs=[smem, smem, smem] + [vmem] * (len(columns) + len(held_codes)),
+            in_specs=[smem, smem, smem] + [vmem] * (len(columns) + len(held)),
             out_specs=vmem,
             scratch_shapes=[pltpu.VMEM((rows, PAIR * SLOTS, 4 * size, 2 * size), jnp.bfloat16)],
             compiler_params=params,
             name="terms_%d" % turn,
-        )(line, own_cols, near_cols, *columns, *[stacks[code] for code in held_codes])
+        )(line, own_cols, near_cols, *columns, *held.values())
         for other in after:
             sent, arrived[other] = lax.optimization_barrier((sent, arrived[other]))
         return sent, lax.ppermute(sent, ("row", "col"), plan.pairs[turn])
 
-    ahead, behind = PAIR * SLOTS, PAIR * SLOTS + 1
-    corner = ahead + SLOTS
-    sent, arrived[0] = send(0, [0, ahead])
-    first, _ = lax.optimization_barrier((stacks[ahead], sent))
-    stacks[corner] = xor_col(first, group_count, 1)
-    sent, arrived[1] = send(1, [1, behind], B1)
-    _, arrived[2] = send(2, [1, SLOTS, behind, corner], B2)
+    _, arrived[0] = send(0, {0: own_0, 4: first_in})
+    _, arrived[1] = send(1, {1: own_1, 5: second_in}, B1)
+    sent, arrived[2] = send(2, {1: own_1, 2: near_0, 5: first_in, 6: second_in}, B2)
+    late, _ = lax.optimization_barrier((second_in, sent))
+    late = xor_col(late, group_count, 1)
 
     own = pl.pallas_call(
         functools.partial(own_kernel, group_count, rows, size),
@@ -241,52 +258,29 @@
         scratch_shapes=[pltpu.VMEM((rows, SLOTS, 4 * size, 2 * size), jnp.bfloat16)],
         compiler_params=params,
         name="own_terms",
-    )(own_cols, stacks[0], stacks[1], stacks[0], stacks[SLOTS], stacks[ahead], stacks[corner])
+    )(own_cols, own_0, own_1, own_0, near_0, late, second_in)
 
     terms = []
     places = []
-    swapped = None
-    for turn, one in sorted(arrived.items()):
-        if swapped is not None:
-            one, swapped = lax.optimization_barrier((one, swapped))
-            terms.append(swapped)
-        swapped = xor_col(one, group_count, 1)
-        terms.append(one)
+    swapped = {}
+    for turn in ORDER:
+        one = arrived[turn]
+        for before, after in CHAIN:
+            if after == turn:
+                one, swapped[before] = lax.optimization_barrier((one, swapped[before]))
+        if turn == OWN:
+            one, own = lax.optimization_barrier((one, own))
+        arrived[turn] = one
+        swapped[turn] = xor_col(one, group_count, 1)
+    for turn in plan.turns:
+        terms += [arrived[turn], swapped[turn]]
         places += [plan.find_at[turn, 0], plan.find_at[turn, 1]]
-
-    terms.append(swapped)
-
-    block = (1, 1, 1, parts, size, size)
-
-    def term_index(place, row, slot, line, cols):
-        found = line[place + slot]
-        return (
-            jnp.maximum(found, 0),
-            jnp.where(found >= 0, cols[row, slot] % rows, 0),
-            0, 0, 0,
-        )
-
-    def slot_index(row, slot, line, cols):
-        return (row, slot, 0, 0, 0)
-
-    def home_index(row, slot, line, cols):
-        return (row, 0, slot, 0, 0, 0)
 
     commutator, section = pl.pallas_call(
         functools.partial(finish_kernel, places),
         out_shape=[jax.ShapeDtypeStruct(density.shape, jnp.float32)] * 2,
-        grid_spec=pltpu.PrefetchScalarGridSpec(
-            num_scalar_prefetch=2,
-            grid=(rows, slots),
-            in_specs=[
-                pl.BlockSpec((1, 1, parts, size, size), slot_index),
-                pl.BlockSpec(block, home_index),
-            ] + [
-                pl.BlockSpec((1, 1, parts, size, size), functools.partial(term_index, place))
-                for place in places
-            ],
-            out_specs=[pl.BlockSpec(block, home_index)] * 2,
-        ),
+        in_specs=[smem] * 2 + [vmem] * (2 + len(terms)),
+        out_specs=[vmem] * 2,
         compiler_params=params,
         name="finish",
     )(line, own_cols, own, density, *terms)

time: 51.4 us -> 49.6 us (0.965)
  the two profiles are of different devices: /device:TPU:3 before, /device:TPU:15 now
where the time goes in v4:
time: 49.6 us; the launch traced here: 49.4 us
  starting transfers between devices  23.3 us (47%)
  waiting for transfers between devices  15.4 us (31%)
  Pallas kernels  7.29 us (15%)
  local copies, waits for them, and re-layouts  2.69 us (5%)
  between operations  0.71 us (1%)
    ppermute x9, starting transfers between devices, xor_col(): return lax.ppermute(value, 'col', [(i, i ^ by) for i in range(group_count)])  19.5 us
    ppermute x9, waiting for transfers between devices, xor_col(): return lax.ppermute(value, 'col', [(i, i ^ by) for i in range(group_count)])  9.72 us
    ppermute x3, waiting for transfers between devices, send(): return (sent, lax.ppermute(sent, ('row', 'col'), plan.pairs[turn]))  5.65 us
    pallas_call x3, Pallas kernels, send(): pl.pallas_call(functools.partial(terms_kernel, plan, turn, list(held), ro...  3.89 us
    ppermute x3, starting transfers between devices, send(): return (sent, lax.ppermute(sent, ('row', 'col'), plan.pairs[turn]))  3.86 us
    unnamed x8, local copies, waits for them, and re-layouts  2 us
    pallas_call x1, Pallas kernels, body(): pl.pallas_call(functools.partial(finish_kernel, places), out_shape=[jax.S...  1.89 us
    pallas_call x1, Pallas kernels, body(): pl.pallas_call(functools.partial(own_kernel, group_count, rows, size), ou...  1.45 us
  transfers between devices with their start and end apart: 12, of which 7 were waited for; matrix products, arithmetic and copies ran while one was open for 1% of the time, Pallas kernels for 11%

profile of v4, /device:TPU:15, one launch (start us, length us, event | category | flops | bytes accessed | tf_op | source)
XLA Modules:
  0.0 49.4 jit_solution(7547252666862923715)
XLA Ops:
  0.6 0.0 copy-start
  0.6 1.0 %copy-done = f32[2,1,2,2,128,128]{5,4,3,2,1,0:T(8,128)S(1)} copy-done((f32[2,1,2,2,128,128]{5,4,3,2,1,0:T(8,128)S(1)}, f32[2,1,2,2,128,128]{5,4,3,2,1,0:T(8,128)}, u32[]{:S(2)}) %copy-start) | copy-done | bytes 524312
  1.7 0.0 copy-start.2
  1.7 0.9 %copy-done.2 = bf16[2,1,2,2,128,128]{5,4,3,2,1,0:T(8,128)(2,1)S(1)} copy-done((bf16[2,1,2,2,128,128]{5,4,3,2,1,0:T(8,128)(2,1)S(1)}, bf16[2,1,2,2,128,128]{5,4,3,2,1,0:T(8,128)(2,1)}, u32[]{:S(2)}) %copy-start.2) | copy-done | bytes 262168
  2.6 0.1 pack.1
  2.7 0.7 %collective-permute-start.1 = (bf16[2,512,128]{2,1,0:T(8,128)(2,1)S(1)}, bf16[2,512,128]{2,1,0:T(8,128)(2,1)S(1)}, u32[]{:S(2)}, u32[]{:S(2)}) collective-permute-start(bf16[2,512,128]{2,1,0:T(8,128)(2,1)S(1)} %get-tuple-element.10.refs_0_.refs_4_.refs_2_), channel_id=1, source_target_pairs={{0,1},{1,0},{2,3},{3,2},{4,5},{5,4},{6,7},{7,6},{8,9},{9,8},{10,11... | collective-permute-start | bytes 786440 | tf_op jit(solution)/shard_map/ppermute | solution.py:22
  3.4 0.2 collective-permute-start.3
  3.7 0.3 collective-permute-start.2
  4.0 0.6 %collective-permute-done.1.refs_2_.refs_5_.refs_3_ = bf16[2,512,128]{2,1,0:T(8,128)(2,1)S(1)} collective-permute-done((bf16[2,512,128]{2,1,0:T(8,128)(2,1)S(1)}, bf16[2,512,128]{2,1,0:T(8,128)(2,1)S(1)}, u32[]{:S(2)}, u32[]{:S(2)}) %collective-permute-start.1) | collective-permute-done | bytes 262176 | tf_op jit(solution)/shard_map/ppermute | solution.py:22
  4.6 0.0 copy-start.3
  4.6 0.7 %collective-permute-start.5 = (bf16[2,512,128]{2,1,0:T(8,128)(2,1)S(1)}, bf16[2,512,128]{2,1,0:T(8,128)(2,1)S(1)}, u32[]{:S(2)}, u32[]{:S(2)}) collective-permute-start(bf16[2,512,128]{2,1,0:T(8,128)(2,1)S(1)} %broadcast_select_fusion), channel_id=1, source_target_pairs={{0,2},{1,3},{2,0},{3,1},{4,6},{5,7},{6,4},{7,5},{8,10},{9,11},{10,... | collective-permute-start | bytes 786440 | tf_op jit(solution)/shard_map/ppermute | solution.py:22
  5.4 0.0 copy-done.3
  5.4 0.4 collective-permute-start
  5.8 0.7 %dynamic-slice_bitcast_fusion.line = s32[25]{0:T(128)S(1)} fusion(s32[32,25]{1,0:T(8,128)} %constant.50.clone, s32[]{:T(128)S(6)} %select_n.26), kind=kLoop, calls=%fused_computation.1 | loop fusion | bytes 204 | tf_op jit(solution)/shard_map/jit(dynamic_index_in_dim)/squeeze | solution.py:211
  6.5 0.1 collective-permute-done.near_cols
  6.6 4.7 %collective-permute-done.3.refs_5_.refs_6_ = bf16[2,512,128]{2,1,0:T(8,128)(2,1)S(1)} collective-permute-done((bf16[2,512,128]{2,1,0:T(8,128)(2,1)S(1)}, bf16[2,512,128]{2,1,0:T(8,128)(2,1)S(1)}, u32[]{:S(2)}, u32[]{:S(2)}) %collective-permute-start.3) | collective-permute-done | bytes 262176 | tf_op jit(solution)/shard_map/ppermute | solution.py:22
  11.3 0.0 collective-permute-done.2.refs_3_
  11.3 1.3 %terms_0.1 = bf16[3,2,2,128,128]{4,3,2,1,0:T(8,128)(2,1)S(1)} custom-call(s32[25]{0:T(128)S(1)} %dynamic-slice_bitcast_fusion.line, s32[2,2]{1,0:T(2,128)S(1)} %bitcast.4, s32[2,2]{1,0:T(2,128)S(1)} %collective-permute-done.near_cols, bf16[2,512,128]{2,1,0:T(8,128)(2,1)S(1)} %get-tuple-element.10.refs_0_.refs_4_.refs_2_, ...), custom_call_target="tpu_custom_call" | custom-call | tf_op jit(solution)/shard_map/terms_0/pallas_call | solution.py:232
  12.6 1.4 %collective-permute-start.4 = (bf16[3,2,2,128,128]{4,3,2,1,0:T(8,128)(2,1)S(1)}, bf16[3,2,2,128,128]{4,3,2,1,0:T(8,128)(2,1)S(1)}, u32[]{:S(2)}, u32[]{:S(2)}) collective-permute-start(bf16[3,2,2,128,128]{4,3,2,1,0:T(8,128)(2,1)S(1)} %terms_0.1), channel_id=1, source_target_pairs={{0,9},{1,12},{2,11},{3,14},{4,8},{5,13},{6,10},{7,15},{8,17},{9,20... | collective-permute-start | bytes 1179656 | tf_op jit(solution)/shard_map/ppermute | solution.py:245
  14.0 3.0 %collective-permute-done.5.refs_7_.refs_5_ = bf16[2,512,128]{2,1,0:T(8,128)(2,1)S(1)} collective-permute-done((bf16[2,512,128]{2,1,0:T(8,128)(2,1)S(1)}, bf16[2,512,128]{2,1,0:T(8,128)(2,1)S(1)}, u32[]{:S(2)}, u32[]{:S(2)}) %collective-permute-start.5) | collective-permute-done | bytes 262176 | tf_op jit(solution)/shard_map/ppermute | solution.py:22
  16.9 1.4 %terms_2.1 = bf16[4,2,2,128,128]{4,3,2,1,0:T(8,128)(2,1)S(1)} custom-call(s32[25]{0:T(128)S(1)} %dynamic-slice_bitcast_fusion.line, s32[2,2]{1,0:T(2,128)S(1)} %bitcast.5, s32[2,2]{1,0:T(2,128)S(1)} %collective-permute-done.near_cols, bf16[2,512,128]{2,1,0:T(8,128)(2,1)S(1)} %get-tuple-element.10.refs_0_.refs_4_.refs_2_, ...), custom_call_target="tpu_custom_call" | custom-call | tf_op jit(solution)/shard_map/terms_2/pallas_call | solution.py:232
  18.3 0.9 %collective-permute-start.6 = (bf16[2,512,128]{2,1,0:T(8,128)(2,1)S(1)}, bf16[2,512,128]{2,1,0:T(8,128)(2,1)S(1)}, u32[]{:S(2)}, u32[]{:S(2)}) collective-permute-start(bf16[2,512,128]{2,1,0:T(8,128)(2,1)S(1)} %collective-permute-done.5.refs_7_.refs_5_), channel_id=1, source_target_pairs={{0,1},{1,0},{2,3},{3,2},{4,5},{5,4},{6,7},{7,6},{8,9},{9,8},{10,11... | collective-permute-start | bytes 786440 | tf_op jit(solution)/shard_map/ppermute | solution.py:22
  19.2 2.3 %collective-permute-start.10 = (bf16[4,2,2,128,128]{4,3,2,1,0:T(8,128)(2,1)S(1)}, bf16[4,2,2,128,128]{4,3,2,1,0:T(8,128)(2,1)S(1)}, u32[]{:S(2)}, u32[]{:S(2)}) collective-permute-start(bf16[4,2,2,128,128]{4,3,2,1,0:T(8,128)(2,1)S(1)} %terms_2.1), channel_id=1, source_target_pairs={{1,20},{0,5},{3,22},{2,7},{4,0},{5,17},{6,2},{7,19},{9,28},{8,13},... | collective-permute-start | bytes 1572872 | tf_op jit(solution)/shard_map/ppermute | solution.py:245
  21.5 1.3 %terms_1.1 = bf16[3,2,2,128,128]{4,3,2,1,0:T(8,128)(2,1)S(1)} custom-call(s32[25]{0:T(128)S(1)} %dynamic-slice_bitcast_fusion.line, s32[2,2]{1,0:T(2,128)S(1)} %bitcast.6, s32[2,2]{1,0:T(2,128)S(1)} %collective-permute-done.near_cols, bf16[2,512,128]{2,1,0:T(8,128)(2,1)S(1)} %get-tuple-element.10.refs_0_.refs_4_.refs_2_, ...), custom_call_target="tpu_custom_call" | custom-call | tf_op jit(solution)/shard_map/terms_1/pallas_call | solution.py:232
  22.8 0.0 copy-start.1
  22.8 0.2 collective-permute-start.7
  23.0 0.0 collective-permute-done.6.refs_4_
  23.0 1.4 %own_terms.1.own = f32[2,2,2,128,128]{4,3,2,1,0:T(8,128)S(1)} custom-call(s32[2,2]{1,0:T(2,128)S(1)} %bitcast.7, bf16[2,512,128]{2,1,0:T(8,128)(2,1)S(1)} %get-tuple-element.10.refs_0_.refs_4_.refs_2_, bf16[2,512,128]{2,1,0:T(8,128)(2,1)S(1)} %get-tuple-element.11.refs_1_.refs_4_, bf16[2,512,128]{2,1,0:T(8,128)(2,1)S(1)} %get-tuple-element.10.refs_0_.refs_4_.refs_2_, ...), custom_call_target="tpu_custom_call" | custom-call | tf_op jit(solution)/shard_map/own_terms/pallas_call | solution.py:253
  24.5 0.0 collective-permute-done.4.refs_0_
  24.5 14.2 %collective-permute-start.8 = (bf16[3,2,2,128,128]{4,3,2,1,0:T(8,128)(2,1)S(1)}, bf16[3,2,2,128,128]{4,3,2,1,0:T(8,128)(2,1)S(1)}, u32[]{:S(2)}, u32[]{:S(2)}) collective-permute-start(bf16[3,2,2,128,128]{4,3,2,1,0:T(8,128)(2,1)S(1)} %collective-permute-done.4.refs_0_), channel_id=1, source_target_pairs={{0,1},{1,0},{2,3},{3,2},{4,5},{5,4},{6,7},{7,6},{8,9},{9,8},{10,11... | collective-permute-start | bytes 1179656 | tf_op jit(solution)/shard_map/ppermute | solution.py:22
  38.7 4.4 %collective-permute-done.10.refs_4_ = bf16[4,2,2,128,128]{4,3,2,1,0:T(8,128)(2,1)S(1)} collective-permute-done((bf16[4,2,2,128,128]{4,3,2,1,0:T(8,128)(2,1)S(1)}, bf16[4,2,2,128,128]{4,3,2,1,0:T(8,128)(2,1)S(1)}, u32[]{:S(2)}, u32[]{:S(2)}) %collective-permute-start.10) | collective-permute-done | bytes 524320 | tf_op jit(solution)/shard_map/ppermute | solution.py:245
  43.0 0.0 collective-permute-start.11
  43.1 1.3 %collective-permute-done.7.refs_2_ = bf16[3,2,2,128,128]{4,3,2,1,0:T(8,128)(2,1)S(1)} collective-permute-done((bf16[3,2,2,128,128]{4,3,2,1,0:T(8,128)(2,1)S(1)}, bf16[3,2,2,128,128]{4,3,2,1,0:T(8,128)(2,1)S(1)}, u32[]{:S(2)}, u32[]{:S(2)}) %collective-permute-start.7) | collective-permute-done | bytes 393248 | tf_op jit(solution)/shard_map/ppermute | solution.py:245
  44.3 0.0 collective-permute-done.8.refs_1_
  44.3 1.9 %collective-permute-start.9 = (bf16[3,2,2,128,128]{4,3,2,1,0:T(8,128)(2,1)S(1)}, bf16[3,2,2,128,128]{4,3,2,1,0:T(8,128)(2,1)S(1)}, u32[]{:S(2)}, u32[]{:S(2)}) collective-permute-start(bf16[3,2,2,128,128]{4,3,2,1,0:T(8,128)(2,1)S(1)} %collective-permute-done.7.refs_2_), channel_id=1, source_target_pairs={{0,1},{1,0},{2,3},{3,2},{4,5},{5,4},{6,7},{7,6},{8,9},{9,8},{10,11... | collective-permute-start | bytes 1179656 | tf_op jit(solution)/shard_map/ppermute | solution.py:22
  46.2 1.3 %collective-permute-done.9.refs_3_ = bf16[3,2,2,128,128]{4,3,2,1,0:T(8,128)(2,1)S(1)} collective-permute-done((bf16[3,2,2,128,128]{4,3,2,1,0:T(8,128)(2,1)S(1)}, bf16[3,2,2,128,128]{4,3,2,1,0:T(8,128)(2,1)S(1)}, u32[]{:S(2)}, u32[]{:S(2)}) %collective-permute-start.9) | collective-permute-done | bytes 393248 | tf_op jit(solution)/shard_map/ppermute | solution.py:22
  47.5 0.0 collective-permute-done.11.refs_5_
  47.5 0.0 copy-done.1
  47.5 1.9 %finish.1 = (f32[2,1,2,2,128,128]{5,4,3,2,1,0:T(8,128)}, f32[2,1,2,2,128,128]{5,4,3,2,1,0:T(8,128)}) custom-call(s32[25]{0:T(128)S(1)} %dynamic-slice_bitcast_fusion.line, s32[2,2]{1,0:T(2,128)S(1)} %bitcast.8, f32[2,2,2,128,128]{4,3,2,1,0:T(8,128)S(1)} %own_terms.1.own, f32[2,1,2,2,128,128]{5,4,3,2,1,0:T(8,128)S(1)} %copy-done.1, ...), custom_call_target="tpu_custom_call" | custom-call | tf_op jit(solution)/shard_map/finish/pallas_call | solution.py:279
  (1 shorter events, 0.0 us)
Async XLA Ops:
  0.6 1.0 %copy-start = (f32[2,1,2,2,128,128]{5,4,3,2,1,0:T(8,128)S(1)}, f32[2,1,2,2,128,128]{5,4,3,2,1,0:T(8,128)}, u32[]{:S(2)}) copy-start(f32[2,1,2,2,128,128]{5,4,3,2,1,0:T(8,128)} %density.1) | copy-start | bytes 1572868
  1.7 0.9 %copy-start.2 = (bf16[2,1,2,2,128,128]{5,4,3,2,1,0:T(8,128)(2,1)S(1)}, bf16[2,1,2,2,128,128]{5,4,3,2,1,0:T(8,128)(2,1)}, u32[]{:S(2)}) copy-start(bf16[2,1,2,2,128,128]{5,4,3,2,1,0:T(8,128)(2,1)} %energy.1) | copy-start | bytes 786436
  2.7 1.9 %collective-permute-start.1 = (bf16[2,512,128]{2,1,0:T(8,128)(2,1)S(1)}, bf16[2,512,128]{2,1,0:T(8,128)(2,1)S(1)}, u32[]{:S(2)}, u32[]{:S(2)}) collective-permute-start(bf16[2,512,128]{2,1,0:T(8,128)(2,1)S(1)} %get-tuple-element.10.refs_0_.refs_4_.refs_2_), channel_id=1, source_target_pairs={{0,1},{1,0},{2,3},{3,2},{4,5},{5,4},{6,7},{7,6},{8,9},{9,8},{10,11... | collective-permute-start | bytes 786440 | tf_op jit(solution)/shard_map/ppermute | solution.py:22
  3.4 7.9 %collective-permute-start.3 = (bf16[2,512,128]{2,1,0:T(8,128)(2,1)S(1)}, bf16[2,512,128]{2,1,0:T(8,128)(2,1)S(1)}, u32[]{:S(2)}, u32[]{:S(2)}) collective-permute-start(bf16[2,512,128]{2,1,0:T(8,128)(2,1)S(1)} %get-tuple-element.12), channel_id=1, source_target_pairs={{0,2},{1,3},{2,0},{3,1},{4,6},{5,7},{6,4},{7,5},{8,10},{9,11},{10,... | collective-permute-start | bytes 786440 | tf_op jit(solution)/shard_map/ppermute | solution.py:22
  3.7 7.6 %collective-permute-start.2 = (bf16[2,512,128]{2,1,0:T(8,128)(2,1)S(1)}, bf16[2,512,128]{2,1,0:T(8,128)(2,1)S(1)}, u32[]{:S(2)}, u32[]{:S(2)}) collective-permute-start(bf16[2,512,128]{2,1,0:T(8,128)(2,1)S(1)} %get-tuple-element.11.refs_1_.refs_4_), channel_id=1, source_target_pairs={{0,1},{1,0},{2,3},{3,2},{4,5},{5,4},{6,7},{7,6},{8,9},{9,8},{10,11... | collective-permute-start | bytes 786440 | tf_op jit(solution)/shard_map/ppermute | solution.py:22
  4.6 0.7 %copy-start.3 = (s32[2,1,2]{2,1,0:T(1,128)S(1)}, s32[2,1,2]{2,1,0:T(1,128)}, u32[]{:S(2)}) copy-start(s32[2,1,2]{2,1,0:T(1,128)} %param.6) | copy-start | bytes 52
  4.6 12.3 %collective-permute-start.5 = (bf16[2,512,128]{2,1,0:T(8,128)(2,1)S(1)}, bf16[2,512,128]{2,1,0:T(8,128)(2,1)S(1)}, u32[]{:S(2)}, u32[]{:S(2)}) collective-permute-start(bf16[2,512,128]{2,1,0:T(8,128)(2,1)S(1)} %broadcast_select_fusion), channel_id=1, source_target_pairs={{0,2},{1,3},{2,0},{3,1},{4,6},{5,7},{6,4},{7,5},{8,10},{9,11},{10,... | collective-permute-start | bytes 786440 | tf_op jit(solution)/shard_map/ppermute | solution.py:22
  5.4 1.3 %collective-permute-start = (s32[2,2]{1,0:T(2,128)S(1)}, s32[2,2]{1,0:T(2,128)S(1)}, u32[]{:S(2)}, u32[]{:S(2)}) collective-permute-start(s32[2,2]{1,0:T(2,128)S(1)} %bitcast.3), channel_id=1, source_target_pairs={{0,1},{1,0},{2,3},{3,2},{4,5},{5,4},{6,7},{7,6},{8,9},{9,8},{10,11... | collective-permute-start | bytes 56 | tf_op jit(solution)/shard_map/ppermute | solution.py:22
  12.6 11.9 %collective-permute-start.4 = (bf16[3,2,2,128,128]{4,3,2,1,0:T(8,128)(2,1)S(1)}, bf16[3,2,2,128,128]{4,3,2,1,0:T(8,128)(2,1)S(1)}, u32[]{:S(2)}, u32[]{:S(2)}) collective-permute-start(bf16[3,2,2,128,128]{4,3,2,1,0:T(8,128)(2,1)S(1)} %terms_0.1), channel_id=1, source_target_pairs={{0,9},{1,12},{2,11},{3,14},{4,8},{5,13},{6,10},{7,15},{8,17},{9,20... | collective-permute-start | bytes 1179656 | tf_op jit(solution)/shard_map/ppermute | solution.py:245
  18.3 4.7 %collective-permute-start.6 = (bf16[2,512,128]{2,1,0:T(8,128)(2,1)S(1)}, bf16[2,512,128]{2,1,0:T(8,128)(2,1)S(1)}, u32[]{:S(2)}, u32[]{:S(2)}) collective-permute-start(bf16[2,512,128]{2,1,0:T(8,128)(2,1)S(1)} %collective-permute-done.5.refs_7_.refs_5_), channel_id=1, source_target_pairs={{0,1},{1,0},{2,3},{3,2},{4,5},{5,4},{6,7},{7,6},{8,9},{9,8},{10,11... | collective-permute-start | bytes 786440 | tf_op jit(solution)/shard_map/ppermute | solution.py:22
  19.2 23.8 %collective-permute-start.10 = (bf16[4,2,2,128,128]{4,3,2,1,0:T(8,128)(2,1)S(1)}, bf16[4,2,2,128,128]{4,3,2,1,0:T(8,128)(2,1)S(1)}, u32[]{:S(2)}, u32[]{:S(2)}) collective-permute-start(bf16[4,2,2,128,128]{4,3,2,1,0:T(8,128)(2,1)S(1)} %terms_2.1), channel_id=1, source_target_pairs={{1,20},{0,5},{3,22},{2,7},{4,0},{5,17},{6,2},{7,19},{9,28},{8,13},... | collective-permute-start | bytes 1572872 | tf_op jit(solution)/shard_map/ppermute | solution.py:245
  22.8 24.8 %copy-start.1 = (f32[2,1,2,2,128,128]{5,4,3,2,1,0:T(8,128)S(1)}, f32[2,1,2,2,128,128]{5,4,3,2,1,0:T(8,128)}, u32[]{:S(2)}) copy-start(f32[2,1,2,2,128,128]{5,4,3,2,1,0:T(8,128)} %density.1) | copy-start | bytes 1572868
  22.8 21.5 %collective-permute-start.7 = (bf16[3,2,2,128,128]{4,3,2,1,0:T(8,128)(2,1)S(1)}, bf16[3,2,2,128,128]{4,3,2,1,0:T(8,128)(2,1)S(1)}, u32[]{:S(2)}, u32[]{:S(2)}) collective-permute-start(bf16[3,2,2,128,128]{4,3,2,1,0:T(8,128)(2,1)S(1)} %terms_1.1), channel_id=1, source_target_pairs={{0,25},{1,28},{2,27},{3,30},{4,24},{5,29},{6,26},{7,31},{8,1},{9,4... | collective-permute-start | bytes 1179656 | tf_op jit(solution)/shard_map/ppermute | solution.py:245
  24.5 19.8 %collective-permute-start.8 = (bf16[3,2,2,128,128]{4,3,2,1,0:T(8,128)(2,1)S(1)}, bf16[3,2,2,128,128]{4,3,2,1,0:T(8,128)(2,1)S(1)}, u32[]{:S(2)}, u32[]{:S(2)}) collective-permute-start(bf16[3,2,2,128,128]{4,3,2,1,0:T(8,128)(2,1)S(1)} %collective-permute-done.4.refs_0_), channel_id=1, source_target_pairs={{0,1},{1,0},{2,3},{3,2},{4,5},{5,4},{6,7},{7,6},{8,9},{9,8},{10,11... | collective-permute-start | bytes 1179656 | tf_op jit(solution)/shard_map/ppermute | solution.py:22
  43.0 4.5 %collective-permute-start.11 = (bf16[4,2,2,128,128]{4,3,2,1,0:T(8,128)(2,1)S(1)}, bf16[4,2,2,128,128]{4,3,2,1,0:T(8,128)(2,1)S(1)}, u32[]{:S(2)}, u32[]{:S(2)}) collective-permute-start(bf16[4,2,2,128,128]{4,3,2,1,0:T(8,128)(2,1)S(1)} %collective-permute-done.10.refs_4_), channel_id=1, source_target_pairs={{0,1},{1,0},{2,3},{3,2},{4,5},{5,4},{6,7},{7,6},{8,9},{9,8},{10,11... | collective-permute-start | bytes 1572872 | tf_op jit(solution)/shard_map/ppermute | solution.py:22
  44.3 3.2 %collective-permute-start.9 = (bf16[3,2,2,128,128]{4,3,2,1,0:T(8,128)(2,1)S(1)}, bf16[3,2,2,128,128]{4,3,2,1,0:T(8,128)(2,1)S(1)}, u32[]{:S(2)}, u32[]{:S(2)}) collective-permute-start(bf16[3,2,2,128,128]{4,3,2,1,0:T(8,128)(2,1)S(1)} %collective-permute-done.7.refs_2_), channel_id=1, source_target_pairs={{0,1},{1,0},{2,3},{3,2},{4,5},{5,4},{6,7},{7,6},{8,9},{9,8},{10,11... | collective-permute-start | bytes 1179656 | tf_op jit(solution)/shard_map/ppermute | solution.py:22

commit v5 on v4

--- a/solution.py
+++ b/solution.py
@@ -10,11 +10,6 @@
 
 
 SLOTS = 2
-OWN = 0
-CHAIN = [(0, 1)]
-ORDER = (0, 1, 2)
-B1 = ()
-B2 = ()
 PAIR = 2
 
 
@@ -25,7 +20,8 @@
 class Plan:
     def __init__(self, row_count, group_count):
         assert group_count == 4
-        self.turns = [0, 1, 2]
+        self.turns = [0, 1, 2, 3]
+        self.direct = [3]
         self.pairs = {turn: [] for turn in self.turns}
         self.width = {turn: 0 for turn in self.turns}
         sends = {}
@@ -36,22 +32,20 @@
                     if offset == 0:
                         continue
                     target = (row + offset) % row_count
-                    turn, sender, side = self.way(row, first, offset, target, group_count)
-                    taker = first + side
                     blocks = self.blocks(row, first, target, row_count, group_count)
-                    codes = []
-                    for column, slot, have in blocks:
-                        place = (target, column, slot, turn, taker ^ column)
-                        assert place not in finds
-                        finds[place] = len(codes)
-                        codes.append((column ^ sender) * SLOTS + have)
-                    held = ((target % group_count) ^ sender) * SLOTS + (0 if offset > 0 else 1)
-                    assert (row, sender, turn) not in sends
-                    sends[row, sender, turn] = (held, codes)
-                    self.pairs[turn].append(
-                        (row * group_count + sender, target * group_count + taker)
-                    )
-                    self.width[turn] = max(self.width[turn], len(codes))
+                    for turn, sender, taker, columns in self.ways(row, first, offset, target, group_count):
+                        codes = []
+                        for column, slot, have in blocks:
+                            if column in columns:
+                                finds[target, column, slot, turn, taker ^ column] = len(codes)
+                                codes.append((column ^ sender) * SLOTS + have)
+                        held = ((target % group_count) ^ sender) * SLOTS + (0 if offset > 0 else 1)
+                        assert (row, sender, turn) not in sends
+                        sends[row, sender, turn] = (held, codes)
+                        self.pairs[turn].append(
+                            (row * group_count + sender, target * group_count + taker)
+                        )
+                        self.width[turn] = max(self.width[turn], len(codes))
         lines = []
         for row in range(row_count):
             for col in range(group_count):
@@ -69,10 +63,16 @@
                 lines.append(line)
         self.table = np.asarray(lines, np.int32)
 
-    def way(self, row, first, offset, target, group_count):
-        if (target % group_count) // PAIR == (row % group_count) // PAIR:
-            return 2, first + (target + (offset > 0)) % PAIR, int(offset > 0)
-        return int(offset < 0), first + target % PAIR, int(abs(offset) == 2)
+    def ways(self, row, first, offset, target, group_count):
+        both = (first, first + 1)
+        if (target % group_count) // PAIR != (row % group_count) // PAIR:
+            side = int(abs(offset) == 2)
+            return [(int(offset < 0), first + target % PAIR, first + side, both)]
+        behind = int(offset < 0)
+        sender = first + (target + 1 - behind) % PAIR
+        if (target % group_count) // PAIR == first // PAIR:
+            return [(2, sender, first + behind, both)]
+        return [(2 + (side ^ behind), sender, first + side, (first + side,)) for side in range(PAIR)]
 
     def blocks(self, row, first, target, row_count, group_count):
         found = []
@@ -133,27 +133,27 @@
     )
 
 
-def terms_kernel(plan, turn, held_codes, rows, size, line, own_cols, near_cols, *refs):
+def terms_kernel(plan, turns, held_codes, rows, size, line, own_cols, near_cols, *refs):
     columns = refs[:PAIR * SLOTS]
     targets = refs[PAIR * SLOTS:PAIR * SLOTS + len(held_codes)]
-    out, right = refs[PAIR * SLOTS + len(held_codes)], refs[-1]
+    outs, right = refs[-len(turns) - 1:-1], refs[-1]
     for row in range(rows):
         for code in range(PAIR * SLOTS):
             fill_right(right, row, code, columns[code][row], size)
-    base = plan.send_at[turn]
-    held = line[base]
-    for row in range(rows):
+    for row in range(rows):
+        held = line[plan.send_at[turns[0]]]
         left = targets[0][row]
         for code, ref in zip(held_codes[1:], targets[1:]):
             left = jnp.where(held == code, ref[row], left)
-        for place in range(plan.width[turn]):
-            code = jnp.maximum(line[base + 1 + place], 0)
-            pair = code // SLOTS
-            slot = code % SLOTS
-            full = times(left, right[row, code]).astype(jnp.bfloat16)
-            there = jnp.where(pair == 0, own_cols[row, slot], near_cols[row, slot]) % rows
-            out[place, there, 0] = full[:, :size]
-            out[place, there, 1] = full[:, size:]
+        for turn, out in zip(turns, outs):
+            for place in range(plan.width[turn]):
+                code = jnp.maximum(line[plan.send_at[turn] + 1 + place], 0)
+                pair = code // SLOTS
+                slot = code % SLOTS
+                full = times(left, right[row, code]).astype(jnp.bfloat16)
+                there = jnp.where(pair == 0, own_cols[row, slot], near_cols[row, slot]) % rows
+                out[place, there, 0] = full[:, :size]
+                out[place, there, 1] = full[:, size:]
 
 
 def own_kernel(group_count, rows, size, own_cols, *refs):
@@ -228,25 +228,26 @@
 
     arrived = {}
 
-    def send(turn, held, after=()):
+    def send(turns, held):
         sent = pl.pallas_call(
-            functools.partial(terms_kernel, plan, turn, list(held), rows, size),
-            out_shape=jax.ShapeDtypeStruct(
-                (plan.width[turn], rows, parts, size, size), jnp.bfloat16
-            ),
+            functools.partial(terms_kernel, plan, turns, list(held), rows, size),
+            out_shape=[
+                jax.ShapeDtypeStruct((plan.width[turn], rows, parts, size, size), jnp.bfloat16)
+                for turn in turns
+            ],
             in_specs=[smem, smem, smem] + [vmem] * (len(columns) + len(held)),
-            out_specs=vmem,
+            out_specs=[vmem] * len(turns),
             scratch_shapes=[pltpu.VMEM((rows, PAIR * SLOTS, 4 * size, 2 * size), jnp.bfloat16)],
             compiler_params=params,
-            name="terms_%d" % turn,
+            name="terms_%d" % turns[0],
         )(line, own_cols, near_cols, *columns, *held.values())
-        for other in after:
-            sent, arrived[other] = lax.optimization_barrier((sent, arrived[other]))
-        return sent, lax.ppermute(sent, ("row", "col"), plan.pairs[turn])
-
-    _, arrived[0] = send(0, {0: own_0, 4: first_in})
-    _, arrived[1] = send(1, {1: own_1, 5: second_in}, B1)
-    sent, arrived[2] = send(2, {1: own_1, 2: near_0, 5: first_in, 6: second_in}, B2)
+        for turn, one in zip(turns, sent):
+            arrived[turn] = lax.ppermute(one, ("row", "col"), plan.pairs[turn])
+        return sent
+
+    send([0], {0: own_0, 4: first_in})
+    send([1], {1: own_1, 5: second_in})
+    sent = send([2, 3], {1: own_1, 2: near_0, 5: first_in, 6: second_in})[0]
     late, _ = lax.optimization_barrier((second_in, sent))
     late = xor_col(late, group_count, 1)
 
@@ -260,21 +261,15 @@
         name="own_terms",
     )(own_cols, own_0, own_1, own_0, near_0, late, second_in)
 
-    terms = []
-    places = []
-    swapped = {}
-    for turn in ORDER:
-        one = arrived[turn]
-        for before, after in CHAIN:
-            if after == turn:
-                one, swapped[before] = lax.optimization_barrier((one, swapped[before]))
-        if turn == OWN:
-            one, own = lax.optimization_barrier((one, own))
-        arrived[turn] = one
-        swapped[turn] = xor_col(one, group_count, 1)
-    for turn in plan.turns:
-        terms += [arrived[turn], swapped[turn]]
-        places += [plan.find_at[turn, 0], plan.find_at[turn, 1]]
+    arrived[0], own = lax.optimization_barrier((arrived[0], own))
+    arrived[2], arrived[3] = lax.optimization_barrier((arrived[2], arrived[3]))
+    swapped = {
+        turn: xor_col(arrived[turn], group_count, 1)
+        for turn in plan.turns if turn not in plan.direct
+    }
+    terms = [arrived[turn] for turn in plan.turns] + [swapped[turn] for turn in swapped]
+    places = [plan.find_at[turn, 0] for turn in plan.turns]
+    places += [plan.find_at[turn, 1] for turn in swapped]
 
     commutator, section = pl.pallas_call(
         functools.partial(finish_kernel, places),

time: 49.6 us -> 48.3 us (0.974)
  the two profiles are of different devices: /device:TPU:15 before, /device:TPU:0 now
where the time goes in v5:
time: 48.3 us; the launch traced here: 48.1 us
  waiting for transfers between devices  25.2 us (52%)
  starting transfers between devices  12.1 us (25%)
  Pallas kernels  7.34 us (15%)
  local copies, waits for them, and re-layouts  2.69 us (6%)
  between operations  0.71 us (1%)
    ppermute x4, waiting for transfers between devices, send(): arrived[turn] = lax.ppermute(one, ('row', 'col'), plan.pairs[turn])  15.5 us
    ppermute x9, waiting for transfers between devices, xor_col(): return lax.ppermute(value, 'col', [(i, i ^ by) for i in range(group_count)])  9.64 us
    ppermute x9, starting transfers between devices, xor_col(): return lax.ppermute(value, 'col', [(i, i ^ by) for i in range(group_count)])  6.78 us
    ppermute x4, starting transfers between devices, send(): arrived[turn] = lax.ppermute(one, ('row', 'col'), plan.pairs[turn])  5.37 us
    pallas_call x3, Pallas kernels, send(): pl.pallas_call(functools.partial(terms_kernel, plan, turns, list(held), r...  3.88 us
    unnamed x8, local copies, waits for them, and re-layouts  2 us
    pallas_call x1, Pallas kernels, body(): pl.pallas_call(functools.partial(finish_kernel, places), out_shape=[jax.S...  1.95 us
    pallas_call x1, Pallas kernels, body(): pl.pallas_call(functools.partial(own_kernel, group_count, rows, size), ou...  1.45 us
  transfers between devices with their start and end apart: 13, of which 7 were waited for; matrix products, arithmetic and copies ran while one was open for 1% of the time, Pallas kernels for 11%

profile of v5, /device:TPU:0, one launch (start us, length us, event | category | flops | bytes accessed | tf_op | source)
XLA Modules:
  0.0 48.1 jit_solution(13712313171644485205)
XLA Ops:
  0.6 0.0 copy-start
  0.6 1.0 %copy-done = f32[2,1,2,2,128,128]{5,4,3,2,1,0:T(8,128)S(1)} copy-done((f32[2,1,2,2,128,128]{5,4,3,2,1,0:T(8,128)S(1)}, f32[2,1,2,2,128,128]{5,4,3,2,1,0:T(8,128)}, u32[]{:S(2)}) %copy-start) | copy-done | bytes 524312
  1.7 0.0 copy-start.2
  1.7 0.9 %copy-done.2 = bf16[2,1,2,2,128,128]{5,4,3,2,1,0:T(8,128)(2,1)S(1)} copy-done((bf16[2,1,2,2,128,128]{5,4,3,2,1,0:T(8,128)(2,1)S(1)}, bf16[2,1,2,2,128,128]{5,4,3,2,1,0:T(8,128)(2,1)}, u32[]{:S(2)}) %copy-start.2) | copy-done | bytes 262168
  2.6 0.1 pack.1
  2.7 0.5 %collective-permute-start.1 = (bf16[2,512,128]{2,1,0:T(8,128)(2,1)S(1)}, bf16[2,512,128]{2,1,0:T(8,128)(2,1)S(1)}, u32[]{:S(2)}, u32[]{:S(2)}) collective-permute-start(bf16[2,512,128]{2,1,0:T(8,128)(2,1)S(1)} %get-tuple-element.12.refs_0_.refs_4_.refs_2_), channel_id=1, source_target_pairs={{0,1},{1,0},{2,3},{3,2},{4,5},{5,4},{6,7},{7,6},{8,9},{9,8},{10,11... | collective-permute-start | bytes 786440 | tf_op jit(solution)/shard_map/ppermute | solution.py:17
  3.2 2.6 %collective-permute-start.3 = (bf16[2,512,128]{2,1,0:T(8,128)(2,1)S(1)}, bf16[2,512,128]{2,1,0:T(8,128)(2,1)S(1)}, u32[]{:S(2)}, u32[]{:S(2)}) collective-permute-start(bf16[2,512,128]{2,1,0:T(8,128)(2,1)S(1)} %get-tuple-element.14), channel_id=1, source_target_pairs={{0,2},{1,3},{2,0},{3,1},{4,6},{5,7},{6,4},{7,5},{8,10},{9,11},{10,... | collective-permute-start | bytes 786440 | tf_op jit(solution)/shard_map/ppermute | solution.py:17
  5.8 0.2 collective-permute-start.2
  6.0 0.0 collective-permute-done.1.refs_2_.refs_5_.refs_3_
  6.0 0.0 copy-start.3
  6.0 1.4 %collective-permute-start.5 = (bf16[2,512,128]{2,1,0:T(8,128)(2,1)S(1)}, bf16[2,512,128]{2,1,0:T(8,128)(2,1)S(1)}, u32[]{:S(2)}, u32[]{:S(2)}) collective-permute-start(bf16[2,512,128]{2,1,0:T(8,128)(2,1)S(1)} %broadcast_select_fusion), channel_id=1, source_target_pairs={{0,2},{1,3},{2,0},{3,1},{4,6},{5,7},{6,4},{7,5},{8,10},{9,11},{10,... | collective-permute-start | bytes 786440 | tf_op jit(solution)/shard_map/ppermute | solution.py:17
  7.4 0.0 copy-done.3
  7.4 0.0 collective-permute-start
  7.4 0.7 %dynamic-slice_bitcast_fusion.line = s32[30]{0:T(128)S(1)} fusion(s32[32,30]{1,0:T(8,128)} %constant.50.clone, s32[]{:T(128)S(6)} %select_n.26), kind=kLoop, calls=%fused_computation.1 | loop fusion | bytes 244 | tf_op jit(solution)/shard_map/jit(dynamic_index_in_dim)/squeeze | solution.py:211
  8.1 0.4 collective-permute-done.near_cols
  8.5 4.4 %collective-permute-done.3.refs_5_.refs_6_ = bf16[2,512,128]{2,1,0:T(8,128)(2,1)S(1)} collective-permute-done((bf16[2,512,128]{2,1,0:T(8,128)(2,1)S(1)}, bf16[2,512,128]{2,1,0:T(8,128)(2,1)S(1)}, u32[]{:S(2)}, u32[]{:S(2)}) %collective-permute-start.3) | collective-permute-done | bytes 262176 | tf_op jit(solution)/shard_map/ppermute | solution.py:17
  13.0 0.0 collective-permute-done.2.refs_3_
  13.0 1.3 %terms_0.1 = bf16[3,2,2,128,128]{4,3,2,1,0:T(8,128)(2,1)S(1)} custom-call(s32[30]{0:T(128)S(1)} %dynamic-slice_bitcast_fusion.line, s32[2,2]{1,0:T(2,128)S(1)} %bitcast.4, s32[2,2]{1,0:T(2,128)S(1)} %collective-permute-done.near_cols, bf16[2,512,128]{2,1,0:T(8,128)(2,1)S(1)} %get-tuple-element.12.refs_0_.refs_4_.refs_2_, ...), custom_call_target="tpu_custom_call" | custom-call | tf_op jit(solution)/shard_map/terms_0/pallas_call | solution.py:232
  14.2 0.9 %collective-permute-start.4 = (bf16[3,2,2,128,128]{4,3,2,1,0:T(8,128)(2,1)S(1)}, bf16[3,2,2,128,128]{4,3,2,1,0:T(8,128)(2,1)S(1)}, u32[]{:S(2)}, u32[]{:S(2)}) collective-permute-start(bf16[3,2,2,128,128]{4,3,2,1,0:T(8,128)(2,1)S(1)} %terms_0.1), channel_id=1, source_target_pairs={{0,9},{1,12},{2,11},{3,14},{4,8},{5,13},{6,10},{7,15},{8,17},{9,20... | collective-permute-start | bytes 1179656 | tf_op jit(solution)/shard_map/ppermute | solution.py:245
  15.1 3.2 %collective-permute-done.5.refs_7_.refs_5_ = bf16[2,512,128]{2,1,0:T(8,128)(2,1)S(1)} collective-permute-done((bf16[2,512,128]{2,1,0:T(8,128)(2,1)S(1)}, bf16[2,512,128]{2,1,0:T(8,128)(2,1)S(1)}, u32[]{:S(2)}, u32[]{:S(2)}) %collective-permute-start.5) | collective-permute-done | bytes 262176 | tf_op jit(solution)/shard_map/ppermute | solution.py:17
  18.3 1.3 %terms_1.1 = bf16[3,2,2,128,128]{4,3,2,1,0:T(8,128)(2,1)S(1)} custom-call(s32[30]{0:T(128)S(1)} %dynamic-slice_bitcast_fusion.line, s32[2,2]{1,0:T(2,128)S(1)} %bitcast.5, s32[2,2]{1,0:T(2,128)S(1)} %collective-permute-done.near_cols, bf16[2,512,128]{2,1,0:T(8,128)(2,1)S(1)} %get-tuple-element.12.refs_0_.refs_4_.refs_2_, ...), custom_call_target="tpu_custom_call" | custom-call | tf_op jit(solution)/shard_map/terms_1/pallas_call | solution.py:232
  19.6 3.2 %collective-permute-start.7 = (bf16[3,2,2,128,128]{4,3,2,1,0:T(8,128)(2,1)S(1)}, bf16[3,2,2,128,128]{4,3,2,1,0:T(8,128)(2,1)S(1)}, u32[]{:S(2)}, u32[]{:S(2)}) collective-permute-start(bf16[3,2,2,128,128]{4,3,2,1,0:T(8,128)(2,1)S(1)} %terms_1.1), channel_id=1, source_target_pairs={{0,25},{1,28},{2,27},{3,30},{4,24},{5,29},{6,26},{7,31},{8,1},{9,4... | collective-permute-start | bytes 1179656 | tf_op jit(solution)/shard_map/ppermute | solution.py:245
  22.8 1.3 %terms_2.1 = (bf16[2,2,2,128,128]{4,3,2,1,0:T(8,128)(2,1)S(1)}, bf16[2,2,2,128,128]{4,3,2,1,0:T(8,128)(2,1)S(1)}) custom-call(s32[30]{0:T(128)S(1)} %dynamic-slice_bitcast_fusion.line, s32[2,2]{1,0:T(2,128)S(1)} %bitcast.6, s32[2,2]{1,0:T(2,128)S(1)} %collective-permute-done.near_cols, bf16[2,512,128]{2,1,0:T(8,128)(2,1)S(1)} %get-tuple-element.12.refs_0_.refs_4_.refs_2_, ...), custom_call_target="tpu_custom_call" | custom-call | tf_op jit(solution)/shard_map/terms_2/pallas_call | solution.py:232
  24.1 1.8 %collective-permute-start.6 = (bf16[2,512,128]{2,1,0:T(8,128)(2,1)S(1)}, bf16[2,512,128]{2,1,0:T(8,128)(2,1)S(1)}, u32[]{:S(2)}, u32[]{:S(2)}) collective-permute-start(bf16[2,512,128]{2,1,0:T(8,128)(2,1)S(1)} %collective-permute-done.5.refs_7_.refs_5_), channel_id=1, source_target_pairs={{0,1},{1,0},{2,3},{3,2},{4,5},{5,4},{6,7},{7,6},{8,9},{9,8},{10,11... | collective-permute-start | bytes 786440 | tf_op jit(solution)/shard_map/ppermute | solution.py:17
  26.0 0.0 copy-start.1
  26.0 0.8 %collective-permute-start.9 = (bf16[2,2,2,128,128]{4,3,2,1,0:T(8,128)(2,1)S(1)}, bf16[2,2,2,128,128]{4,3,2,1,0:T(8,128)(2,1)S(1)}, u32[]{:S(2)}, u32[]{:S(2)}) collective-permute-start(bf16[2,2,2,128,128]{4,3,2,1,0:T(8,128)(2,1)S(1)} %get-tuple-element.19), channel_id=1, source_target_pairs={{3,22},{2,7},{6,2},{7,19},{9,28},{8,13},{12,8},{13,25},{19,6},{18,... | collective-permute-start | bytes 786440 | tf_op jit(solution)/shard_map/ppermute | solution.py:245
  26.8 0.5 %collective-permute-start.8 = (bf16[2,2,2,128,128]{4,3,2,1,0:T(8,128)(2,1)S(1)}, bf16[2,2,2,128,128]{4,3,2,1,0:T(8,128)(2,1)S(1)}, u32[]{:S(2)}, u32[]{:S(2)}) collective-permute-start(bf16[2,2,2,128,128]{4,3,2,1,0:T(8,128)(2,1)S(1)} %get-tuple-element.15), channel_id=1, source_target_pairs={{1,21},{0,4},{3,23},{2,6},{4,1},{5,16},{6,3},{7,18},{9,29},{8,12},... | collective-permute-start | bytes 786440 | tf_op jit(solution)/shard_map/ppermute | solution.py:245
  27.3 0.0 collective-permute-done.6.refs_4_
  27.3 1.4 %own_terms.1.own = f32[2,2,2,128,128]{4,3,2,1,0:T(8,128)S(1)} custom-call(s32[2,2]{1,0:T(2,128)S(1)} %bitcast.7, bf16[2,512,128]{2,1,0:T(8,128)(2,1)S(1)} %get-tuple-element.12.refs_0_.refs_4_.refs_2_, bf16[2,512,128]{2,1,0:T(8,128)(2,1)S(1)} %get-tuple-element.13.refs_1_.refs_4_, bf16[2,512,128]{2,1,0:T(8,128)(2,1)S(1)} %get-tuple-element.12.refs_0_.refs_4_.refs_2_, ...), custom_call_target="tpu_custom_call" | custom-call | tf_op jit(solution)/shard_map/own_terms/pallas_call | solution.py:254
  28.8 0.6 %collective-permute-done.4.refs_0_ = bf16[3,2,2,128,128]{4,3,2,1,0:T(8,128)(2,1)S(1)} collective-permute-done((bf16[3,2,2,128,128]{4,3,2,1,0:T(8,128)(2,1)S(1)}, bf16[3,2,2,128,128]{4,3,2,1,0:T(8,128)(2,1)S(1)}, u32[]{:S(2)}, u32[]{:S(2)}) %collective-permute-start.4) | collective-permute-done | bytes 393248 | tf_op jit(solution)/shard_map/ppermute | solution.py:245
  29.3 0.0 collective-permute-start.10
  29.3 6.8 %collective-permute-done.7.refs_1_ = bf16[3,2,2,128,128]{4,3,2,1,0:T(8,128)(2,1)S(1)} collective-permute-done((bf16[3,2,2,128,128]{4,3,2,1,0:T(8,128)(2,1)S(1)}, bf16[3,2,2,128,128]{4,3,2,1,0:T(8,128)(2,1)S(1)}, u32[]{:S(2)}, u32[]{:S(2)}) %collective-permute-start.7) | collective-permute-done | bytes 393248 | tf_op jit(solution)/shard_map/ppermute | solution.py:245
  36.2 0.3 collective-permute-start.11
  36.5 0.0 collective-permute-done.9.refs_3_
  36.5 8.1 %collective-permute-done.8.refs_2_ = bf16[2,2,2,128,128]{4,3,2,1,0:T(8,128)(2,1)S(1)} collective-permute-done((bf16[2,2,2,128,128]{4,3,2,1,0:T(8,128)(2,1)S(1)}, bf16[2,2,2,128,128]{4,3,2,1,0:T(8,128)(2,1)S(1)}, u32[]{:S(2)}, u32[]{:S(2)}) %collective-permute-start.8) | collective-permute-done | bytes 262176 | tf_op jit(solution)/shard_map/ppermute | solution.py:245
  44.6 0.0 collective-permute-start.12
  44.6 1.5 %collective-permute-done.12.refs_6_ = bf16[2,2,2,128,128]{4,3,2,1,0:T(8,128)(2,1)S(1)} collective-permute-done((bf16[2,2,2,128,128]{4,3,2,1,0:T(8,128)(2,1)S(1)}, bf16[2,2,2,128,128]{4,3,2,1,0:T(8,128)(2,1)S(1)}, u32[]{:S(2)}, u32[]{:S(2)}) %collective-permute-start.12) | collective-permute-done | bytes 262176 | tf_op jit(solution)/shard_map/ppermute | solution.py:17
  46.1 0.0 collective-permute-done.10.refs_4_
  46.1 0.0 collective-permute-done.11.refs_5_
  46.1 0.0 copy-done.1
  46.1 1.9 %finish.1 = (f32[2,1,2,2,128,128]{5,4,3,2,1,0:T(8,128)}, f32[2,1,2,2,128,128]{5,4,3,2,1,0:T(8,128)}) custom-call(s32[30]{0:T(128)S(1)} %dynamic-slice_bitcast_fusion.line, s32[2,2]{1,0:T(2,128)S(1)} %bitcast.8, f32[2,2,2,128,128]{4,3,2,1,0:T(8,128)S(1)} %own_terms.1.own, f32[2,1,2,2,128,128]{5,4,3,2,1,0:T(8,128)S(1)} %copy-done.1, ...), custom_call_target="tpu_custom_call" | custom-call | tf_op jit(solution)/shard_map/finish/pallas_call | solution.py:274
  (1 shorter events, 0.0 us)
Async XLA Ops:
  0.6 1.0 %copy-start = (f32[2,1,2,2,128,128]{5,4,3,2,1,0:T(8,128)S(1)}, f32[2,1,2,2,128,128]{5,4,3,2,1,0:T(8,128)}, u32[]{:S(2)}) copy-start(f32[2,1,2,2,128,128]{5,4,3,2,1,0:T(8,128)} %density.1) | copy-start | bytes 1572868
  1.7 0.9 %copy-start.2 = (bf16[2,1,2,2,128,128]{5,4,3,2,1,0:T(8,128)(2,1)S(1)}, bf16[2,1,2,2,128,128]{5,4,3,2,1,0:T(8,128)(2,1)}, u32[]{:S(2)}) copy-start(bf16[2,1,2,2,128,128]{5,4,3,2,1,0:T(8,128)(2,1)} %energy.1) | copy-start | bytes 786436
  2.7 3.3 %collective-permute-start.1 = (bf16[2,512,128]{2,1,0:T(8,128)(2,1)S(1)}, bf16[2,512,128]{2,1,0:T(8,128)(2,1)S(1)}, u32[]{:S(2)}, u32[]{:S(2)}) collective-permute-start(bf16[2,512,128]{2,1,0:T(8,128)(2,1)S(1)} %get-tuple-element.12.refs_0_.refs_4_.refs_2_), channel_id=1, source_target_pairs={{0,1},{1,0},{2,3},{3,2},{4,5},{5,4},{6,7},{7,6},{8,9},{9,8},{10,11... | collective-permute-start | bytes 786440 | tf_op jit(solution)/shard_map/ppermute | solution.py:17
  3.2 9.8 %collective-permute-start.3 = (bf16[2,512,128]{2,1,0:T(8,128)(2,1)S(1)}, bf16[2,512,128]{2,1,0:T(8,128)(2,1)S(1)}, u32[]{:S(2)}, u32[]{:S(2)}) collective-permute-start(bf16[2,512,128]{2,1,0:T(8,128)(2,1)S(1)} %get-tuple-element.14), channel_id=1, source_target_pairs={{0,2},{1,3},{2,0},{3,1},{4,6},{5,7},{6,4},{7,5},{8,10},{9,11},{10,... | collective-permute-start | bytes 786440 | tf_op jit(solution)/shard_map/ppermute | solution.py:17
  5.8 7.2 %collective-permute-start.2 = (bf16[2,512,128]{2,1,0:T(8,128)(2,1)S(1)}, bf16[2,512,128]{2,1,0:T(8,128)(2,1)S(1)}, u32[]{:S(2)}, u32[]{:S(2)}) collective-permute-start(bf16[2,512,128]{2,1,0:T(8,128)(2,1)S(1)} %get-tuple-element.13.refs_1_.refs_4_), channel_id=1, source_target_pairs={{0,1},{1,0},{2,3},{3,2},{4,5},{5,4},{6,7},{7,6},{8,9},{9,8},{10,11... | collective-permute-start | bytes 786440 | tf_op jit(solution)/shard_map/ppermute | solution.py:17
  6.0 1.4 %copy-start.3 = (s32[2,1,2]{2,1,0:T(1,128)S(1)}, s32[2,1,2]{2,1,0:T(1,128)}, u32[]{:S(2)}) copy-start(s32[2,1,2]{2,1,0:T(1,128)} %param.6) | copy-start | bytes 52
  6.0 12.3 %collective-permute-start.5 = (bf16[2,512,128]{2,1,0:T(8,128)(2,1)S(1)}, bf16[2,512,128]{2,1,0:T(8,128)(2,1)S(1)}, u32[]{:S(2)}, u32[]{:S(2)}) collective-permute-start(bf16[2,512,128]{2,1,0:T(8,128)(2,1)S(1)} %broadcast_select_fusion), channel_id=1, source_target_pairs={{0,2},{1,3},{2,0},{3,1},{4,6},{5,7},{6,4},{7,5},{8,10},{9,11},{10,... | collective-permute-start | bytes 786440 | tf_op jit(solution)/shard_map/ppermute | solution.py:17
  7.4 1.1 %collective-permute-start = (s32[2,2]{1,0:T(2,128)S(1)}, s32[2,2]{1,0:T(2,128)S(1)}, u32[]{:S(2)}, u32[]{:S(2)}) collective-permute-start(s32[2,2]{1,0:T(2,128)S(1)} %bitcast.3), channel_id=1, source_target_pairs={{0,1},{1,0},{2,3},{3,2},{4,5},{5,4},{6,7},{7,6},{8,9},{9,8},{10,11... | collective-permute-start | bytes 56 | tf_op jit(solution)/shard_map/ppermute | solution.py:17
  14.2 15.1 %collective-permute-start.4 = (bf16[3,2,2,128,128]{4,3,2,1,0:T(8,128)(2,1)S(1)}, bf16[3,2,2,128,128]{4,3,2,1,0:T(8,128)(2,1)S(1)}, u32[]{:S(2)}, u32[]{:S(2)}) collective-permute-start(bf16[3,2,2,128,128]{4,3,2,1,0:T(8,128)(2,1)S(1)} %terms_0.1), channel_id=1, source_target_pairs={{0,9},{1,12},{2,11},{3,14},{4,8},{5,13},{6,10},{7,15},{8,17},{9,20... | collective-permute-start | bytes 1179656 | tf_op jit(solution)/shard_map/ppermute | solution.py:245
  19.6 16.6 %collective-permute-start.7 = (bf16[3,2,2,128,128]{4,3,2,1,0:T(8,128)(2,1)S(1)}, bf16[3,2,2,128,128]{4,3,2,1,0:T(8,128)(2,1)S(1)}, u32[]{:S(2)}, u32[]{:S(2)}) collective-permute-start(bf16[3,2,2,128,128]{4,3,2,1,0:T(8,128)(2,1)S(1)} %terms_1.1), channel_id=1, source_target_pairs={{0,25},{1,28},{2,27},{3,30},{4,24},{5,29},{6,26},{7,31},{8,1},{9,4... | collective-permute-start | bytes 1179656 | tf_op jit(solution)/shard_map/ppermute | solution.py:245
  24.1 3.2 %collective-permute-start.6 = (bf16[2,512,128]{2,1,0:T(8,128)(2,1)S(1)}, bf16[2,512,128]{2,1,0:T(8,128)(2,1)S(1)}, u32[]{:S(2)}, u32[]{:S(2)}) collective-permute-start(bf16[2,512,128]{2,1,0:T(8,128)(2,1)S(1)} %collective-permute-done.5.refs_7_.refs_5_), channel_id=1, source_target_pairs={{0,1},{1,0},{2,3},{3,2},{4,5},{5,4},{6,7},{7,6},{8,9},{9,8},{10,11... | collective-permute-start | bytes 786440 | tf_op jit(solution)/shard_map/ppermute | solution.py:17
  26.0 20.2 %copy-start.1 = (f32[2,1,2,2,128,128]{5,4,3,2,1,0:T(8,128)S(1)}, f32[2,1,2,2,128,128]{5,4,3,2,1,0:T(8,128)}, u32[]{:S(2)}) copy-start(f32[2,1,2,2,128,128]{5,4,3,2,1,0:T(8,128)} %density.1) | copy-start | bytes 1572868
  26.0 10.5 %collective-permute-start.9 = (bf16[2,2,2,128,128]{4,3,2,1,0:T(8,128)(2,1)S(1)}, bf16[2,2,2,128,128]{4,3,2,1,0:T(8,128)(2,1)S(1)}, u32[]{:S(2)}, u32[]{:S(2)}) collective-permute-start(bf16[2,2,2,128,128]{4,3,2,1,0:T(8,128)(2,1)S(1)} %get-tuple-element.19), channel_id=1, source_target_pairs={{3,22},{2,7},{6,2},{7,19},{9,28},{8,13},{12,8},{13,25},{19,6},{18,... | collective-permute-start | bytes 786440 | tf_op jit(solution)/shard_map/ppermute | solution.py:245
  26.8 17.8 %collective-permute-start.8 = (bf16[2,2,2,128,128]{4,3,2,1,0:T(8,128)(2,1)S(1)}, bf16[2,2,2,128,128]{4,3,2,1,0:T(8,128)(2,1)S(1)}, u32[]{:S(2)}, u32[]{:S(2)}) collective-permute-start(bf16[2,2,2,128,128]{4,3,2,1,0:T(8,128)(2,1)S(1)} %get-tuple-element.15), channel_id=1, source_target_pairs={{1,21},{0,4},{3,23},{2,6},{4,1},{5,16},{6,3},{7,18},{9,29},{8,12},... | collective-permute-start | bytes 786440 | tf_op jit(solution)/shard_map/ppermute | solution.py:245
  29.3 16.8 %collective-permute-start.10 = (bf16[3,2,2,128,128]{4,3,2,1,0:T(8,128)(2,1)S(1)}, bf16[3,2,2,128,128]{4,3,2,1,0:T(8,128)(2,1)S(1)}, u32[]{:S(2)}, u32[]{:S(2)}) collective-permute-start(bf16[3,2,2,128,128]{4,3,2,1,0:T(8,128)(2,1)S(1)} %collective-permute-done.4.refs_0_), channel_id=1, source_target_pairs={{0,1},{1,0},{2,3},{3,2},{4,5},{5,4},{6,7},{7,6},{8,9},{9,8},{10,11... | collective-permute-start | bytes 1179656 | tf_op jit(solution)/shard_map/ppermute | solution.py:17
  36.2 10.0 %collective-permute-start.11 = (bf16[3,2,2,128,128]{4,3,2,1,0:T(8,128)(2,1)S(1)}, bf16[3,2,2,128,128]{4,3,2,1,0:T(8,128)(2,1)S(1)}, u32[]{:S(2)}, u32[]{:S(2)}) collective-permute-start(bf16[3,2,2,128,128]{4,3,2,1,0:T(8,128)(2,1)S(1)} %collective-permute-done.7.refs_1_), channel_id=1, source_target_pairs={{0,1},{1,0},{2,3},{3,2},{4,5},{5,4},{6,7},{7,6},{8,9},{9,8},{10,11... | collective-permute-start | bytes 1179656 | tf_op jit(solution)/shard_map/ppermute | solution.py:17
  44.6 1.5 %collective-permute-start.12 = (bf16[2,2,2,128,128]{4,3,2,1,0:T(8,128)(2,1)S(1)}, bf16[2,2,2,128,128]{4,3,2,1,0:T(8,128)(2,1)S(1)}, u32[]{:S(2)}, u32[]{:S(2)}) collective-permute-start(bf16[2,2,2,128,128]{4,3,2,1,0:T(8,128)(2,1)S(1)} %collective-permute-done.8.refs_2_), channel_id=1, source_target_pairs={{0,1},{1,0},{2,3},{3,2},{4,5},{5,4},{6,7},{7,6},{8,9},{9,8},{10,11... | collective-permute-start | bytes 786440 | tf_op jit(solution)/shard_map/ppermute | solution.py:17

commit v6 on v5

--- a/solution.py
+++ b/solution.py
@@ -156,8 +156,9 @@
                 out[place, there, 1] = full[:, size:]
 
 
-def own_kernel(group_count, rows, size, own_cols, *refs):
+def own_kernel(group_count, rows, size, places, line, own_cols, *refs):
     firsts = refs[SLOTS:SLOTS + group_count]
+    early = refs[SLOTS + group_count:-2]
     out, right = refs[-2:]
     me = lax.axis_index("row")
     col = lax.axis_index("col")
@@ -183,6 +184,18 @@
                 out[row, slot, 0] += full[:, :size]
                 out[row, slot, 1] += full[:, size:]
 
+    for row in range(rows):
+        for slot in range(SLOTS):
+            out[row, slot] = add_terms(out[row, slot], row, slot, places, line, own_cols, early)
+
+
+def add_terms(total, row, slot, places, line, cols, terms):
+    for place, ref in zip(places, terms):
+        found = line[place + slot]
+        block = ref[jnp.maximum(found, 0), cols[row, slot] % cols.shape[0]]
+        total += jnp.where(found >= 0, block, 0.0).astype(jnp.float32)
+    return total
+
 
 def finish_kernel(places, line, cols, own, density, *refs):
     terms = refs[:len(places)]
@@ -190,11 +203,7 @@
     rows, slots = own.shape[:2]
     for row in range(rows):
         for slot in range(slots):
-            total = own[row, slot]
-            for place, ref in zip(places, terms):
-                found = line[place + slot]
-                block = ref[jnp.maximum(found, 0), cols[row, slot] % rows]
-                total += jnp.where(found >= 0, block, 0.0).astype(jnp.float32)
+            total = add_terms(own[row, slot], row, slot, places, line, cols, terms)
             commutator[row, 0, slot] = total
             section[row, 0, slot, 0] = density[row, 0, slot, 0] + 0.05 * total[1]
             section[row, 0, slot, 1] = density[row, 0, slot, 1] - 0.05 * total[0]
@@ -251,25 +260,24 @@
     late, _ = lax.optimization_barrier((second_in, sent))
     late = xor_col(late, group_count, 1)
 
+    swapped = {0: xor_col(arrived[0], group_count, 1)}
+    early = [arrived[0], swapped[0]]
+    places = [plan.find_at[0, 0], plan.find_at[0, 1]]
     own = pl.pallas_call(
-        functools.partial(own_kernel, group_count, rows, size),
+        functools.partial(own_kernel, group_count, rows, size, places),
         out_shape=jax.ShapeDtypeStruct((rows, slots, parts, size, size), jnp.float32),
-        in_specs=[smem] + [vmem] * (SLOTS + group_count),
+        in_specs=[smem, smem] + [vmem] * (SLOTS + group_count + len(early)),
         out_specs=vmem,
         scratch_shapes=[pltpu.VMEM((rows, SLOTS, 4 * size, 2 * size), jnp.bfloat16)],
         compiler_params=params,
         name="own_terms",
-    )(own_cols, own_0, own_1, own_0, near_0, late, second_in)
-
-    arrived[0], own = lax.optimization_barrier((arrived[0], own))
-    arrived[2], arrived[3] = lax.optimization_barrier((arrived[2], arrived[3]))
-    swapped = {
-        turn: xor_col(arrived[turn], group_count, 1)
-        for turn in plan.turns if turn not in plan.direct
-    }
-    terms = [arrived[turn] for turn in plan.turns] + [swapped[turn] for turn in swapped]
-    places = [plan.find_at[turn, 0] for turn in plan.turns]
-    places += [plan.find_at[turn, 1] for turn in swapped]
+    )(line, own_cols, own_0, own_1, own_0, near_0, late, second_in, *early)
+
+    arrived[1], arrived[3] = lax.optimization_barrier((arrived[1], arrived[3]))
+    swapped[1] = xor_col(arrived[1], group_count, 1)
+    swapped[2] = xor_col(arrived[2], group_count, 1)
+    terms = [arrived[1], arrived[2], arrived[3], swapped[1], swapped[2]]
+    places = [plan.find_at[turn, 0] for turn in (1, 2, 3)] + [plan.find_at[turn, 1] for turn in (1, 2)]
 
     commutator, section = pl.pallas_call(
         functools.partial(finish_kernel, places),

time: 48.3 us -> 47.9 us (level)
  the two profiles are of different devices: /device:TPU:0 before, /device:TPU:3 now
where the time goes in v6:
time: 47.9 us; the launch traced here: 47.6 us
  waiting for transfers between devices  19.4 us (41%)
  starting transfers between devices  17.4 us (36%)
  Pallas kernels  7.36 us (15%)
  local copies, waits for them, and re-layouts  2.69 us (6%)
  between operations  0.74 us (2%)
    ppermute x4, waiting for transfers between devices, send(): arrived[turn] = lax.ppermute(one, ('row', 'col'), plan.pairs[turn])  12.7 us
    ppermute x9, starting transfers between devices, xor_col(): return lax.ppermute(value, 'col', [(i, i ^ by) for i in range(group_count)])  11.8 us
    ppermute x9, waiting for transfers between devices, xor_col(): return lax.ppermute(value, 'col', [(i, i ^ by) for i in range(group_count)])  6.66 us
    ppermute x4, starting transfers between devices, send(): arrived[turn] = lax.ppermute(one, ('row', 'col'), plan.pairs[turn])  5.61 us
    pallas_call x3, Pallas kernels, send(): pl.pallas_call(functools.partial(terms_kernel, plan, turns, list(held), r...  3.89 us
    unnamed x8, local copies, waits for them, and re-layouts  2 us
    pallas_call x1, Pallas kernels, body(): pl.pallas_call(functools.partial(finish_kernel, places), out_shape=[jax.S...  1.84 us
    pallas_call x1, Pallas kernels, body(): pl.pallas_call(functools.partial(own_kernel, group_count, rows, size, pla...  1.57 us
  transfers between devices with their start and end apart: 13, of which 5 were waited for; matrix products, arithmetic and copies ran while one was open for 2% of the time, Pallas kernels for 11%

profile of v6, /device:TPU:3, one launch (start us, length us, event | category | flops | bytes accessed | tf_op | source)
XLA Modules:
  0.0 47.6 jit_solution(997052592034936076)
XLA Ops:
  0.6 0.0 copy-start
  0.6 1.0 %copy-done = f32[2,1,2,2,128,128]{5,4,3,2,1,0:T(8,128)S(1)} copy-done((f32[2,1,2,2,128,128]{5,4,3,2,1,0:T(8,128)S(1)}, f32[2,1,2,2,128,128]{5,4,3,2,1,0:T(8,128)}, u32[]{:S(2)}) %copy-start) | copy-done | bytes 524312
  1.7 0.0 copy-start.2
  1.7 0.9 %copy-done.2 = bf16[2,1,2,2,128,128]{5,4,3,2,1,0:T(8,128)(2,1)S(1)} copy-done((bf16[2,1,2,2,128,128]{5,4,3,2,1,0:T(8,128)(2,1)S(1)}, bf16[2,1,2,2,128,128]{5,4,3,2,1,0:T(8,128)(2,1)}, u32[]{:S(2)}) %copy-start.2) | copy-done | bytes 262168
  2.6 0.1 pack.1
  2.7 0.7 %collective-permute-start = (bf16[2,512,128]{2,1,0:T(8,128)(2,1)S(1)}, bf16[2,512,128]{2,1,0:T(8,128)(2,1)S(1)}, u32[]{:S(2)}, u32[]{:S(2)}) collective-permute-start(bf16[2,512,128]{2,1,0:T(8,128)(2,1)S(1)} %get-tuple-element.10.refs_0_.refs_4_.refs_2_), channel_id=1, source_target_pairs={{0,1},{1,0},{2,3},{3,2},{4,5},{5,4},{6,7},{7,6},{8,9},{9,8},{10,11... | collective-permute-start | bytes 786440 | tf_op jit(solution)/shard_map/ppermute | solution.py:17
  3.4 0.1 collective-permute-start.3
  3.5 1.2 %collective-permute-start.4 = (bf16[2,512,128]{2,1,0:T(8,128)(2,1)S(1)}, bf16[2,512,128]{2,1,0:T(8,128)(2,1)S(1)}, u32[]{:S(2)}, u32[]{:S(2)}) collective-permute-start(bf16[2,512,128]{2,1,0:T(8,128)(2,1)S(1)} %get-tuple-element.12), channel_id=1, source_target_pairs={{0,2},{1,3},{2,0},{3,1},{4,6},{5,7},{6,4},{7,5},{8,10},{9,11},{10,... | collective-permute-start | bytes 786440 | tf_op jit(solution)/shard_map/ppermute | solution.py:17
  4.8 0.0 collective-permute-done.refs_2_.refs_5_.refs_3_
  4.8 0.0 copy-start.3
  4.8 1.1 %collective-permute-start.1 = (bf16[2,512,128]{2,1,0:T(8,128)(2,1)S(1)}, bf16[2,512,128]{2,1,0:T(8,128)(2,1)S(1)}, u32[]{:S(2)}, u32[]{:S(2)}) collective-permute-start(bf16[2,512,128]{2,1,0:T(8,128)(2,1)S(1)} %broadcast_select_fusion), channel_id=1, source_target_pairs={{0,2},{1,3},{2,0},{3,1},{4,6},{5,7},{6,4},{7,5},{8,10},{9,11},{10,... | collective-permute-start | bytes 786440 | tf_op jit(solution)/shard_map/ppermute | solution.py:17
  5.9 0.0 copy-done.3
  5.9 0.7 %collective-permute-start.2 = (s32[2,2]{1,0:T(2,128)S(1)}, s32[2,2]{1,0:T(2,128)S(1)}, u32[]{:S(2)}, u32[]{:S(2)}) collective-permute-start(s32[2,2]{1,0:T(2,128)S(1)} %bitcast.3), channel_id=1, source_target_pairs={{0,1},{1,0},{2,3},{3,2},{4,5},{5,4},{6,7},{7,6},{8,9},{9,8},{10,11... | collective-permute-start | bytes 56 | tf_op jit(solution)/shard_map/ppermute | solution.py:17
  6.6 0.7 %dynamic-slice_bitcast_fusion.line = s32[30]{0:T(128)S(1)} fusion(s32[32,30]{1,0:T(8,128)} %constant.50.clone, s32[]{:T(128)S(6)} %select_n.26), kind=kLoop, calls=%fused_computation.1 | loop fusion | bytes 244 | tf_op jit(solution)/shard_map/jit(dynamic_index_in_dim)/squeeze | solution.py:220
  7.3 0.1 collective-permute-done.2.near_cols
  7.4 0.0 collective-permute-done.3.refs_3_
  7.4 3.5 %collective-permute-done.4.refs_6_.refs_5_ = bf16[2,512,128]{2,1,0:T(8,128)(2,1)S(1)} collective-permute-done((bf16[2,512,128]{2,1,0:T(8,128)(2,1)S(1)}, bf16[2,512,128]{2,1,0:T(8,128)(2,1)S(1)}, u32[]{:S(2)}, u32[]{:S(2)}) %collective-permute-start.4) | collective-permute-done | bytes 262176 | tf_op jit(solution)/shard_map/ppermute | solution.py:17
  11.0 1.3 %terms_0.1 = bf16[3,2,2,128,128]{4,3,2,1,0:T(8,128)(2,1)S(1)} custom-call(s32[30]{0:T(128)S(1)} %dynamic-slice_bitcast_fusion.line, s32[2,2]{1,0:T(2,128)S(1)} %bitcast.4, s32[2,2]{1,0:T(2,128)S(1)} %collective-permute-done.2.near_cols, bf16[2,512,128]{2,1,0:T(8,128)(2,1)S(1)} %get-tuple-element.10.refs_0_.refs_4_.refs_2_, ...), custom_call_target="tpu_custom_call" | custom-call | tf_op jit(solution)/shard_map/terms_0/pallas_call | solution.py:241
  12.2 1.4 %collective-permute-start.6 = (bf16[3,2,2,128,128]{4,3,2,1,0:T(8,128)(2,1)S(1)}, bf16[3,2,2,128,128]{4,3,2,1,0:T(8,128)(2,1)S(1)}, u32[]{:S(2)}, u32[]{:S(2)}) collective-permute-start(bf16[3,2,2,128,128]{4,3,2,1,0:T(8,128)(2,1)S(1)} %terms_0.1), channel_id=1, source_target_pairs={{0,9},{1,12},{2,11},{3,14},{4,8},{5,13},{6,10},{7,15},{8,17},{9,20... | collective-permute-start | bytes 1179656 | tf_op jit(solution)/shard_map/ppermute | solution.py:254
  13.6 3.0 %collective-permute-done.1.refs_7_.refs_5_ = bf16[2,512,128]{2,1,0:T(8,128)(2,1)S(1)} collective-permute-done((bf16[2,512,128]{2,1,0:T(8,128)(2,1)S(1)}, bf16[2,512,128]{2,1,0:T(8,128)(2,1)S(1)}, u32[]{:S(2)}, u32[]{:S(2)}) %collective-permute-start.1) | collective-permute-done | bytes 262176 | tf_op jit(solution)/shard_map/ppermute | solution.py:17
  16.6 1.3 %terms_1.1 = bf16[3,2,2,128,128]{4,3,2,1,0:T(8,128)(2,1)S(1)} custom-call(s32[30]{0:T(128)S(1)} %dynamic-slice_bitcast_fusion.line, s32[2,2]{1,0:T(2,128)S(1)} %bitcast.5, s32[2,2]{1,0:T(2,128)S(1)} %collective-permute-done.2.near_cols, bf16[2,512,128]{2,1,0:T(8,128)(2,1)S(1)} %get-tuple-element.10.refs_0_.refs_4_.refs_2_, ...), custom_call_target="tpu_custom_call" | custom-call | tf_op jit(solution)/shard_map/terms_1/pallas_call | solution.py:241
  17.9 3.4 %collective-permute-start.8 = (bf16[3,2,2,128,128]{4,3,2,1,0:T(8,128)(2,1)S(1)}, bf16[3,2,2,128,128]{4,3,2,1,0:T(8,128)(2,1)S(1)}, u32[]{:S(2)}, u32[]{:S(2)}) collective-permute-start(bf16[3,2,2,128,128]{4,3,2,1,0:T(8,128)(2,1)S(1)} %terms_1.1), channel_id=1, source_target_pairs={{0,25},{1,28},{2,27},{3,30},{4,24},{5,29},{6,26},{7,31},{8,1},{9,4... | collective-permute-start | bytes 1179656 | tf_op jit(solution)/shard_map/ppermute | solution.py:254
  21.2 1.4 %terms_2.1 = (bf16[2,2,2,128,128]{4,3,2,1,0:T(8,128)(2,1)S(1)}, bf16[2,2,2,128,128]{4,3,2,1,0:T(8,128)(2,1)S(1)}) custom-call(s32[30]{0:T(128)S(1)} %dynamic-slice_bitcast_fusion.line, s32[2,2]{1,0:T(2,128)S(1)} %bitcast.6, s32[2,2]{1,0:T(2,128)S(1)} %collective-permute-done.2.near_cols, bf16[2,512,128]{2,1,0:T(8,128)(2,1)S(1)} %get-tuple-element.10.refs_0_.refs_4_.refs_2_, ...), custom_call_target="tpu_custom_call" | custom-call | tf_op jit(solution)/shard_map/terms_2/pallas_call | solution.py:241
  22.6 0.7 %collective-permute-start.9 = (bf16[2,2,2,128,128]{4,3,2,1,0:T(8,128)(2,1)S(1)}, bf16[2,2,2,128,128]{4,3,2,1,0:T(8,128)(2,1)S(1)}, u32[]{:S(2)}, u32[]{:S(2)}) collective-permute-start(bf16[2,2,2,128,128]{4,3,2,1,0:T(8,128)(2,1)S(1)} %get-tuple-element.15), channel_id=1, source_target_pairs={{3,22},{2,7},{6,2},{7,19},{9,28},{8,13},{12,8},{13,25},{19,6},{18,... | collective-permute-start | bytes 786440 | tf_op jit(solution)/shard_map/ppermute | solution.py:254
  23.3 0.0 copy-start.1
  23.3 0.2 collective-permute-start.10
  23.5 0.0 collective-permute-done.6.refs_6_
  23.5 5.1 %collective-permute-start.7 = (bf16[3,2,2,128,128]{4,3,2,1,0:T(8,128)(2,1)S(1)}, bf16[3,2,2,128,128]{4,3,2,1,0:T(8,128)(2,1)S(1)}, u32[]{:S(2)}, u32[]{:S(2)}) collective-permute-start(bf16[3,2,2,128,128]{4,3,2,1,0:T(8,128)(2,1)S(1)} %collective-permute-done.6.refs_6_), channel_id=1, source_target_pairs={{0,1},{1,0},{2,3},{3,2},{4,5},{5,4},{6,7},{7,6},{8,9},{9,8},{10,11... | collective-permute-start | bytes 1179656 | tf_op jit(solution)/shard_map/ppermute | solution.py:17
  28.6 0.0 collective-permute-done.9.refs_2_
  28.6 5.0 %collective-permute-done.8.refs_0_ = bf16[3,2,2,128,128]{4,3,2,1,0:T(8,128)(2,1)S(1)} collective-permute-done((bf16[3,2,2,128,128]{4,3,2,1,0:T(8,128)(2,1)S(1)}, bf16[3,2,2,128,128]{4,3,2,1,0:T(8,128)(2,1)S(1)}, u32[]{:S(2)}, u32[]{:S(2)}) %collective-permute-start.8) | collective-permute-done | bytes 393248 | tf_op jit(solution)/shard_map/ppermute | solution.py:254
  33.6 2.8 %collective-permute-start.11 = (bf16[3,2,2,128,128]{4,3,2,1,0:T(8,128)(2,1)S(1)}, bf16[3,2,2,128,128]{4,3,2,1,0:T(8,128)(2,1)S(1)}, u32[]{:S(2)}, u32[]{:S(2)}) collective-permute-start(bf16[3,2,2,128,128]{4,3,2,1,0:T(8,128)(2,1)S(1)} %collective-permute-done.8.refs_0_), channel_id=1, source_target_pairs={{0,1},{1,0},{2,3},{3,2},{4,5},{5,4},{6,7},{7,6},{8,9},{9,8},{10,11... | collective-permute-start | bytes 1179656 | tf_op jit(solution)/shard_map/ppermute | solution.py:17
  36.4 0.0 collective-permute-start.5
  36.4 7.7 %collective-permute-done.10.refs_1_ = bf16[2,2,2,128,128]{4,3,2,1,0:T(8,128)(2,1)S(1)} collective-permute-done((bf16[2,2,2,128,128]{4,3,2,1,0:T(8,128)(2,1)S(1)}, bf16[2,2,2,128,128]{4,3,2,1,0:T(8,128)(2,1)S(1)}, u32[]{:S(2)}, u32[]{:S(2)}) %collective-permute-start.10) | collective-permute-done | bytes 262176 | tf_op jit(solution)/shard_map/ppermute | solution.py:254
  44.1 0.0 collective-permute-start.12
  44.2 0.0 collective-permute-done.5.refs_4_
  44.2 0.0 collective-permute-done.7.refs_7_
  44.2 1.6 %own_terms.1.own = f32[2,2,2,128,128]{4,3,2,1,0:T(8,128)S(1)} custom-call(s32[30]{0:T(128)S(1)} %dynamic-slice_bitcast_fusion.line, s32[2,2]{1,0:T(2,128)S(1)} %bitcast.7, bf16[2,512,128]{2,1,0:T(8,128)(2,1)S(1)} %get-tuple-element.10.refs_0_.refs_4_.refs_2_, bf16[2,512,128]{2,1,0:T(8,128)(2,1)S(1)} %get-tuple-element.11.refs_1_.refs_4_, ...), custom_call_target="tpu_custom_call" | custom-call | tf_op jit(solution)/shard_map/own_terms/pallas_call | solution.py:266
  45.7 0.0 collective-permute-done.12.refs_4_
  45.7 0.0 collective-permute-done.11.refs_3_
  45.8 0.0 copy-done.1
  45.8 1.8 %finish.1 = (f32[2,1,2,2,128,128]{5,4,3,2,1,0:T(8,128)}, f32[2,1,2,2,128,128]{5,4,3,2,1,0:T(8,128)}) custom-call(s32[30]{0:T(128)S(1)} %dynamic-slice_bitcast_fusion.line, s32[2,2]{1,0:T(2,128)S(1)} %bitcast.8, f32[2,2,2,128,128]{4,3,2,1,0:T(8,128)S(1)} %own_terms.1.own, f32[2,1,2,2,128,128]{5,4,3,2,1,0:T(8,128)S(1)} %copy-done.1, ...), custom_call_target="tpu_custom_call" | custom-call | tf_op jit(solution)/shard_map/finish/pallas_call | solution.py:282
  (1 shorter events, 0.0 us)
Async XLA Ops:
  0.6 1.0 %copy-start = (f32[2,1,2,2,128,128]{5,4,3,2,1,0:T(8,128)S(1)}, f32[2,1,2,2,128,128]{5,4,3,2,1,0:T(8,128)}, u32[]{:S(2)}) copy-start(f32[2,1,2,2,128,128]{5,4,3,2,1,0:T(8,128)} %density.1) | copy-start | bytes 1572868
  1.7 0.9 %copy-start.2 = (bf16[2,1,2,2,128,128]{5,4,3,2,1,0:T(8,128)(2,1)S(1)}, bf16[2,1,2,2,128,128]{5,4,3,2,1,0:T(8,128)(2,1)}, u32[]{:S(2)}) copy-start(bf16[2,1,2,2,128,128]{5,4,3,2,1,0:T(8,128)(2,1)} %energy.1) | copy-start | bytes 786436
  2.7 2.1 %collective-permute-start = (bf16[2,512,128]{2,1,0:T(8,128)(2,1)S(1)}, bf16[2,512,128]{2,1,0:T(8,128)(2,1)S(1)}, u32[]{:S(2)}, u32[]{:S(2)}) collective-permute-start(bf16[2,512,128]{2,1,0:T(8,128)(2,1)S(1)} %get-tuple-element.10.refs_0_.refs_4_.refs_2_), channel_id=1, source_target_pairs={{0,1},{1,0},{2,3},{3,2},{4,5},{5,4},{6,7},{7,6},{8,9},{9,8},{10,11... | collective-permute-start | bytes 786440 | tf_op jit(solution)/shard_map/ppermute | solution.py:17
  3.4 4.0 %collective-permute-start.3 = (bf16[2,512,128]{2,1,0:T(8,128)(2,1)S(1)}, bf16[2,512,128]{2,1,0:T(8,128)(2,1)S(1)}, u32[]{:S(2)}, u32[]{:S(2)}) collective-permute-start(bf16[2,512,128]{2,1,0:T(8,128)(2,1)S(1)} %get-tuple-element.11.refs_1_.refs_4_), channel_id=1, source_target_pairs={{0,1},{1,0},{2,3},{3,2},{4,5},{5,4},{6,7},{7,6},{8,9},{9,8},{10,11... | collective-permute-start | bytes 786440 | tf_op jit(solution)/shard_map/ppermute | solution.py:17
  3.5 7.4 %collective-permute-start.4 = (bf16[2,512,128]{2,1,0:T(8,128)(2,1)S(1)}, bf16[2,512,128]{2,1,0:T(8,128)(2,1)S(1)}, u32[]{:S(2)}, u32[]{:S(2)}) collective-permute-start(bf16[2,512,128]{2,1,0:T(8,128)(2,1)S(1)} %get-tuple-element.12), channel_id=1, source_target_pairs={{0,2},{1,3},{2,0},{3,1},{4,6},{5,7},{6,4},{7,5},{8,10},{9,11},{10,... | collective-permute-start | bytes 786440 | tf_op jit(solution)/shard_map/ppermute | solution.py:17
  4.8 1.2 %copy-start.3 = (s32[2,1,2]{2,1,0:T(1,128)S(1)}, s32[2,1,2]{2,1,0:T(1,128)}, u32[]{:S(2)}) copy-start(s32[2,1,2]{2,1,0:T(1,128)} %param.6) | copy-start | bytes 52
  4.8 11.8 %collective-permute-start.1 = (bf16[2,512,128]{2,1,0:T(8,128)(2,1)S(1)}, bf16[2,512,128]{2,1,0:T(8,128)(2,1)S(1)}, u32[]{:S(2)}, u32[]{:S(2)}) collective-permute-start(bf16[2,512,128]{2,1,0:T(8,128)(2,1)S(1)} %broadcast_select_fusion), channel_id=1, source_target_pairs={{0,2},{1,3},{2,0},{3,1},{4,6},{5,7},{6,4},{7,5},{8,10},{9,11},{10,... | collective-permute-start | bytes 786440 | tf_op jit(solution)/shard_map/ppermute | solution.py:17
  5.9 1.5 %collective-permute-start.2 = (s32[2,2]{1,0:T(2,128)S(1)}, s32[2,2]{1,0:T(2,128)S(1)}, u32[]{:S(2)}, u32[]{:S(2)}) collective-permute-start(s32[2,2]{1,0:T(2,128)S(1)} %bitcast.3), channel_id=1, source_target_pairs={{0,1},{1,0},{2,3},{3,2},{4,5},{5,4},{6,7},{7,6},{8,9},{9,8},{10,11... | collective-permute-start | bytes 56 | tf_op jit(solution)/shard_map/ppermute | solution.py:17
  12.2 11.3 %collective-permute-start.6 = (bf16[3,2,2,128,128]{4,3,2,1,0:T(8,128)(2,1)S(1)}, bf16[3,2,2,128,128]{4,3,2,1,0:T(8,128)(2,1)S(1)}, u32[]{:S(2)}, u32[]{:S(2)}) collective-permute-start(bf16[3,2,2,128,128]{4,3,2,1,0:T(8,128)(2,1)S(1)} %terms_0.1), channel_id=1, source_target_pairs={{0,9},{1,12},{2,11},{3,14},{4,8},{5,13},{6,10},{7,15},{8,17},{9,20... | collective-permute-start | bytes 1179656 | tf_op jit(solution)/shard_map/ppermute | solution.py:254
  17.9 15.8 %collective-permute-start.8 = (bf16[3,2,2,128,128]{4,3,2,1,0:T(8,128)(2,1)S(1)}, bf16[3,2,2,128,128]{4,3,2,1,0:T(8,128)(2,1)S(1)}, u32[]{:S(2)}, u32[]{:S(2)}) collective-permute-start(bf16[3,2,2,128,128]{4,3,2,1,0:T(8,128)(2,1)S(1)} %terms_1.1), channel_id=1, source_target_pairs={{0,25},{1,28},{2,27},{3,30},{4,24},{5,29},{6,26},{7,31},{8,1},{9,4... | collective-permute-start | bytes 1179656 | tf_op jit(solution)/shard_map/ppermute | solution.py:254
  22.6 6.0 %collective-permute-start.9 = (bf16[2,2,2,128,128]{4,3,2,1,0:T(8,128)(2,1)S(1)}, bf16[2,2,2,128,128]{4,3,2,1,0:T(8,128)(2,1)S(1)}, u32[]{:S(2)}, u32[]{:S(2)}) collective-permute-start(bf16[2,2,2,128,128]{4,3,2,1,0:T(8,128)(2,1)S(1)} %get-tuple-element.15), channel_id=1, source_target_pairs={{3,22},{2,7},{6,2},{7,19},{9,28},{8,13},{12,8},{13,25},{19,6},{18,... | collective-permute-start | bytes 786440 | tf_op jit(solution)/shard_map/ppermute | solution.py:254
  23.3 22.5 %copy-start.1 = (f32[2,1,2,2,128,128]{5,4,3,2,1,0:T(8,128)S(1)}, f32[2,1,2,2,128,128]{5,4,3,2,1,0:T(8,128)}, u32[]{:S(2)}) copy-start(f32[2,1,2,2,128,128]{5,4,3,2,1,0:T(8,128)} %density.1) | copy-start | bytes 1572868
  23.3 20.9 %collective-permute-start.10 = (bf16[2,2,2,128,128]{4,3,2,1,0:T(8,128)(2,1)S(1)}, bf16[2,2,2,128,128]{4,3,2,1,0:T(8,128)(2,1)S(1)}, u32[]{:S(2)}, u32[]{:S(2)}) collective-permute-start(bf16[2,2,2,128,128]{4,3,2,1,0:T(8,128)(2,1)S(1)} %get-tuple-element.13), channel_id=1, source_target_pairs={{1,21},{0,4},{3,23},{2,6},{4,1},{5,16},{6,3},{7,18},{9,29},{8,12},... | collective-permute-start | bytes 786440 | tf_op jit(solution)/shard_map/ppermute | solution.py:254
  23.5 20.7 %collective-permute-start.7 = (bf16[3,2,2,128,128]{4,3,2,1,0:T(8,128)(2,1)S(1)}, bf16[3,2,2,128,128]{4,3,2,1,0:T(8,128)(2,1)S(1)}, u32[]{:S(2)}, u32[]{:S(2)}) collective-permute-start(bf16[3,2,2,128,128]{4,3,2,1,0:T(8,128)(2,1)S(1)} %collective-permute-done.6.refs_6_), channel_id=1, source_target_pairs={{0,1},{1,0},{2,3},{3,2},{4,5},{5,4},{6,7},{7,6},{8,9},{9,8},{10,11... | collective-permute-start | bytes 1179656 | tf_op jit(solution)/shard_map/ppermute | solution.py:17
  33.6 12.1 %collective-permute-start.11 = (bf16[3,2,2,128,128]{4,3,2,1,0:T(8,128)(2,1)S(1)}, bf16[3,2,2,128,128]{4,3,2,1,0:T(8,128)(2,1)S(1)}, u32[]{:S(2)}, u32[]{:S(2)}) collective-permute-start(bf16[3,2,2,128,128]{4,3,2,1,0:T(8,128)(2,1)S(1)} %collective-permute-done.8.refs_0_), channel_id=1, source_target_pairs={{0,1},{1,0},{2,3},{3,2},{4,5},{5,4},{6,7},{7,6},{8,9},{9,8},{10,11... | collective-permute-start | bytes 1179656 | tf_op jit(solution)/shard_map/ppermute | solution.py:17
  36.4 7.7 %collective-permute-start.5 = (bf16[2,512,128]{2,1,0:T(8,128)(2,1)S(1)}, bf16[2,512,128]{2,1,0:T(8,128)(2,1)S(1)}, u32[]{:S(2)}, u32[]{:S(2)}) collective-permute-start(bf16[2,512,128]{2,1,0:T(8,128)(2,1)S(1)} %collective-permute-done.1.refs_7_.refs_5_), channel_id=1, source_target_pairs={{0,1},{1,0},{2,3},{3,2},{4,5},{5,4},{6,7},{7,6},{8,9},{9,8},{10,11... | collective-permute-start | bytes 786440 | tf_op jit(solution)/shard_map/ppermute | solution.py:17
  44.1 1.6 %collective-permute-start.12 = (bf16[2,2,2,128,128]{4,3,2,1,0:T(8,128)(2,1)S(1)}, bf16[2,2,2,128,128]{4,3,2,1,0:T(8,128)(2,1)S(1)}, u32[]{:S(2)}, u32[]{:S(2)}) collective-permute-start(bf16[2,2,2,128,128]{4,3,2,1,0:T(8,128)(2,1)S(1)} %collective-permute-done.10.refs_1_), channel_id=1, source_target_pairs={{0,1},{1,0},{2,3},{3,2},{4,5},{5,4},{6,7},{7,6},{8,9},{9,8},{10,11... | collective-permute-start | bytes 786440 | tf_op jit(solution)/shard_map/ppermute | solution.py:17

commit v7 on v6

--- a/solution.py
+++ b/solution.py
@@ -248,6 +248,7 @@
             out_specs=[vmem] * len(turns),
             scratch_shapes=[pltpu.VMEM((rows, PAIR * SLOTS, 4 * size, 2 * size), jnp.bfloat16)],
             compiler_params=params,
+            cost_estimate=pl.CostEstimate(flops=20000000, bytes_accessed=60000, transcendentals=0),
             name="terms_%d" % turns[0],
         )(line, own_cols, near_cols, *columns, *held.values())
         for turn, one in zip(turns, sent):
@@ -270,7 +271,8 @@
         out_specs=vmem,
         scratch_shapes=[pltpu.VMEM((rows, SLOTS, 4 * size, 2 * size), jnp.bfloat16)],
         compiler_params=params,
-        name="own_terms",
+        cost_estimate=pl.CostEstimate(flops=20000000, bytes_accessed=60000, transcendentals=0),
+            name="own_terms",
     )(line, own_cols, own_0, own_1, own_0, near_0, late, second_in, *early)
 
     arrived[1], arrived[3] = lax.optimization_barrier((arrived[1], arrived[3]))

time: 47.9 us -> 47.9 us (level)
  no operation moved by 1% of the time
where the time goes in v7:
time: 47.9 us; the launch traced here: 47.6 us
  waiting for transfers between devices  19.4 us (41%)
  starting transfers between devices  17.4 us (36%)
  Pallas kernels  7.36 us (15%)
  local copies, waits for them, and re-layouts  2.69 us (6%)
  between operations  0.74 us (2%)
    ppermute x4, waiting for transfers between devices, send(): arrived[turn] = lax.ppermute(one, ('row', 'col'), plan.pairs[turn])  12.7 us
    ppermute x9, starting transfers between devices, xor_col(): return lax.ppermute(value, 'col', [(i, i ^ by) for i in range(group_count)])  11.8 us
    ppermute x9, waiting for transfers between devices, xor_col(): return lax.ppermute(value, 'col', [(i, i ^ by) for i in range(group_count)])  6.66 us
    ppermute x4, starting transfers between devices, send(): arrived[turn] = lax.ppermute(one, ('row', 'col'), plan.pairs[turn])  5.61 us
    pallas_call x3, Pallas kernels, send(): pl.pallas_call(functools.partial(terms_kernel, plan, turns, list(held), r...  3.89 us
    unnamed x8, local copies, waits for them, and re-layouts  2 us
    pallas_call x1, Pallas kernels, body(): pl.pallas_call(functools.partial(finish_kernel, places), out_shape=[jax.S...  1.84 us
    pallas_call x1, Pallas kernels, body(): pl.pallas_call(functools.partial(own_kernel, group_count, rows, size, pla...  1.57 us
  transfers between devices with their start and end apart: 13, of which 5 were waited for; matrix products, arithmetic and copies ran while one was open for 2% of the time, Pallas kernels for 11%

profile of v7, /device:TPU:3, one launch (start us, length us, event | category | flops | bytes accessed | tf_op | source)
XLA Modules:
  0.0 47.6 jit_solution(997052592034936076)
XLA Ops:
  0.6 0.0 copy-start
  0.6 1.0 %copy-done = f32[2,1,2,2,128,128]{5,4,3,2,1,0:T(8,128)S(1)} copy-done((f32[2,1,2,2,128,128]{5,4,3,2,1,0:T(8,128)S(1)}, f32[2,1,2,2,128,128]{5,4,3,2,1,0:T(8,128)}, u32[]{:S(2)}) %copy-start) | copy-done | bytes 524312
  1.7 0.0 copy-start.2
  1.7 0.9 %copy-done.2 = bf16[2,1,2,2,128,128]{5,4,3,2,1,0:T(8,128)(2,1)S(1)} copy-done((bf16[2,1,2,2,128,128]{5,4,3,2,1,0:T(8,128)(2,1)S(1)}, bf16[2,1,2,2,128,128]{5,4,3,2,1,0:T(8,128)(2,1)}, u32[]{:S(2)}) %copy-start.2) | copy-done | bytes 262168
  2.6 0.1 pack.1
  2.7 0.7 %collective-permute-start = (bf16[2,512,128]{2,1,0:T(8,128)(2,1)S(1)}, bf16[2,512,128]{2,1,0:T(8,128)(2,1)S(1)}, u32[]{:S(2)}, u32[]{:S(2)}) collective-permute-start(bf16[2,512,128]{2,1,0:T(8,128)(2,1)S(1)} %get-tuple-element.10.refs_0_.refs_4_.refs_2_), channel_id=1, source_target_pairs={{0,1},{1,0},{2,3},{3,2},{4,5},{5,4},{6,7},{7,6},{8,9},{9,8},{10,11... | collective-permute-start | bytes 786440 | tf_op jit(solution)/shard_map/ppermute | solution.py:17
  3.4 0.1 collective-permute-start.3
  3.5 1.2 %collective-permute-start.4 = (bf16[2,512,128]{2,1,0:T(8,128)(2,1)S(1)}, bf16[2,512,128]{2,1,0:T(8,128)(2,1)S(1)}, u32[]{:S(2)}, u32[]{:S(2)}) collective-permute-start(bf16[2,512,128]{2,1,0:T(8,128)(2,1)S(1)} %get-tuple-element.12), channel_id=1, source_target_pairs={{0,2},{1,3},{2,0},{3,1},{4,6},{5,7},{6,4},{7,5},{8,10},{9,11},{10,... | collective-permute-start | bytes 786440 | tf_op jit(solution)/shard_map/ppermute | solution.py:17
  4.8 0.0 collective-permute-done.refs_2_.refs_5_.refs_3_
  4.8 0.0 copy-start.3
  4.8 1.1 %collective-permute-start.1 = (bf16[2,512,128]{2,1,0:T(8,128)(2,1)S(1)}, bf16[2,512,128]{2,1,0:T(8,128)(2,1)S(1)}, u32[]{:S(2)}, u32[]{:S(2)}) collective-permute-start(bf16[2,512,128]{2,1,0:T(8,128)(2,1)S(1)} %broadcast_select_fusion), channel_id=1, source_target_pairs={{0,2},{1,3},{2,0},{3,1},{4,6},{5,7},{6,4},{7,5},{8,10},{9,11},{10,... | collective-permute-start | bytes 786440 | tf_op jit(solution)/shard_map/ppermute | solution.py:17
  5.9 0.0 copy-done.3
  5.9 0.7 %collective-permute-start.2 = (s32[2,2]{1,0:T(2,128)S(1)}, s32[2,2]{1,0:T(2,128)S(1)}, u32[]{:S(2)}, u32[]{:S(2)}) collective-permute-start(s32[2,2]{1,0:T(2,128)S(1)} %bitcast.3), channel_id=1, source_target_pairs={{0,1},{1,0},{2,3},{3,2},{4,5},{5,4},{6,7},{7,6},{8,9},{9,8},{10,11... | collective-permute-start | bytes 56 | tf_op jit(solution)/shard_map/ppermute | solution.py:17
  6.6 0.7 %dynamic-slice_bitcast_fusion.line = s32[30]{0:T(128)S(1)} fusion(s32[32,30]{1,0:T(8,128)} %constant.50.clone, s32[]{:T(128)S(6)} %select_n.26), kind=kLoop, calls=%fused_computation.1 | loop fusion | bytes 244 | tf_op jit(solution)/shard_map/jit(dynamic_index_in_dim)/squeeze | solution.py:220
  7.3 0.1 collective-permute-done.2.near_cols
  7.4 0.0 collective-permute-done.3.refs_3_
  7.4 3.5 %collective-permute-done.4.refs_6_.refs_5_ = bf16[2,512,128]{2,1,0:T(8,128)(2,1)S(1)} collective-permute-done((bf16[2,512,128]{2,1,0:T(8,128)(2,1)S(1)}, bf16[2,512,128]{2,1,0:T(8,128)(2,1)S(1)}, u32[]{:S(2)}, u32[]{:S(2)}) %collective-permute-start.4) | collective-permute-done | bytes 262176 | tf_op jit(solution)/shard_map/ppermute | solution.py:17
  11.0 1.3 %terms_0.1 = bf16[3,2,2,128,128]{4,3,2,1,0:T(8,128)(2,1)S(1)} custom-call(s32[30]{0:T(128)S(1)} %dynamic-slice_bitcast_fusion.line, s32[2,2]{1,0:T(2,128)S(1)} %bitcast.4, s32[2,2]{1,0:T(2,128)S(1)} %collective-permute-done.2.near_cols, bf16[2,512,128]{2,1,0:T(8,128)(2,1)S(1)} %get-tuple-element.10.refs_0_.refs_4_.refs_2_, ...), custom_call_target="tpu_custom_call" | custom-call | flops 20000000 | bytes 60000 | tf_op jit(solution)/shard_map/terms_0/pallas_call | solution.py:241
  12.2 1.4 %collective-permute-start.6 = (bf16[3,2,2,128,128]{4,3,2,1,0:T(8,128)(2,1)S(1)}, bf16[3,2,2,128,128]{4,3,2,1,0:T(8,128)(2,1)S(1)}, u32[]{:S(2)}, u32[]{:S(2)}) collective-permute-start(bf16[3,2,2,128,128]{4,3,2,1,0:T(8,128)(2,1)S(1)} %terms_0.1), channel_id=1, source_target_pairs={{0,9},{1,12},{2,11},{3,14},{4,8},{5,13},{6,10},{7,15},{8,17},{9,20... | collective-permute-start | bytes 1179656 | tf_op jit(solution)/shard_map/ppermute | solution.py:255
  13.6 3.0 %collective-permute-done.1.refs_7_.refs_5_ = bf16[2,512,128]{2,1,0:T(8,128)(2,1)S(1)} collective-permute-done((bf16[2,512,128]{2,1,0:T(8,128)(2,1)S(1)}, bf16[2,512,128]{2,1,0:T(8,128)(2,1)S(1)}, u32[]{:S(2)}, u32[]{:S(2)}) %collective-permute-start.1) | collective-permute-done | bytes 262176 | tf_op jit(solution)/shard_map/ppermute | solution.py:17
  16.6 1.3 %terms_1.1 = bf16[3,2,2,128,128]{4,3,2,1,0:T(8,128)(2,1)S(1)} custom-call(s32[30]{0:T(128)S(1)} %dynamic-slice_bitcast_fusion.line, s32[2,2]{1,0:T(2,128)S(1)} %bitcast.5, s32[2,2]{1,0:T(2,128)S(1)} %collective-permute-done.2.near_cols, bf16[2,512,128]{2,1,0:T(8,128)(2,1)S(1)} %get-tuple-element.10.refs_0_.refs_4_.refs_2_, ...), custom_call_target="tpu_custom_call" | custom-call | flops 20000000 | bytes 60000 | tf_op jit(solution)/shard_map/terms_1/pallas_call | solution.py:241
  17.9 3.4 %collective-permute-start.8 = (bf16[3,2,2,128,128]{4,3,2,1,0:T(8,128)(2,1)S(1)}, bf16[3,2,2,128,128]{4,3,2,1,0:T(8,128)(2,1)S(1)}, u32[]{:S(2)}, u32[]{:S(2)}) collective-permute-start(bf16[3,2,2,128,128]{4,3,2,1,0:T(8,128)(2,1)S(1)} %terms_1.1), channel_id=1, source_target_pairs={{0,25},{1,28},{2,27},{3,30},{4,24},{5,29},{6,26},{7,31},{8,1},{9,4... | collective-permute-start | bytes 1179656 | tf_op jit(solution)/shard_map/ppermute | solution.py:255
  21.2 1.4 %terms_2.1 = (bf16[2,2,2,128,128]{4,3,2,1,0:T(8,128)(2,1)S(1)}, bf16[2,2,2,128,128]{4,3,2,1,0:T(8,128)(2,1)S(1)}) custom-call(s32[30]{0:T(128)S(1)} %dynamic-slice_bitcast_fusion.line, s32[2,2]{1,0:T(2,128)S(1)} %bitcast.6, s32[2,2]{1,0:T(2,128)S(1)} %collective-permute-done.2.near_cols, bf16[2,512,128]{2,1,0:T(8,128)(2,1)S(1)} %get-tuple-element.10.refs_0_.refs_4_.refs_2_, ...), custom_call_target="tpu_custom_call" | custom-call | flops 20000000 | bytes 60000 | tf_op jit(solution)/shard_map/terms_2/pallas_call | solution.py:241
  22.6 0.7 %collective-permute-start.9 = (bf16[2,2,2,128,128]{4,3,2,1,0:T(8,128)(2,1)S(1)}, bf16[2,2,2,128,128]{4,3,2,1,0:T(8,128)(2,1)S(1)}, u32[]{:S(2)}, u32[]{:S(2)}) collective-permute-start(bf16[2,2,2,128,128]{4,3,2,1,0:T(8,128)(2,1)S(1)} %get-tuple-element.15), channel_id=1, source_target_pairs={{3,22},{2,7},{6,2},{7,19},{9,28},{8,13},{12,8},{13,25},{19,6},{18,... | collective-permute-start | bytes 786440 | tf_op jit(solution)/shard_map/ppermute | solution.py:255
  23.3 0.0 copy-start.1
  23.3 0.2 collective-permute-start.10
  23.5 0.0 collective-permute-done.6.refs_6_
  23.5 5.1 %collective-permute-start.7 = (bf16[3,2,2,128,128]{4,3,2,1,0:T(8,128)(2,1)S(1)}, bf16[3,2,2,128,128]{4,3,2,1,0:T(8,128)(2,1)S(1)}, u32[]{:S(2)}, u32[]{:S(2)}) collective-permute-start(bf16[3,2,2,128,128]{4,3,2,1,0:T(8,128)(2,1)S(1)} %collective-permute-done.6.refs_6_), channel_id=1, source_target_pairs={{0,1},{1,0},{2,3},{3,2},{4,5},{5,4},{6,7},{7,6},{8,9},{9,8},{10,11... | collective-permute-start | bytes 1179656 | tf_op jit(solution)/shard_map/ppermute | solution.py:17
  28.6 0.0 collective-permute-done.9.refs_2_
  28.6 5.0 %collective-permute-done.8.refs_0_ = bf16[3,2,2,128,128]{4,3,2,1,0:T(8,128)(2,1)S(1)} collective-permute-done((bf16[3,2,2,128,128]{4,3,2,1,0:T(8,128)(2,1)S(1)}, bf16[3,2,2,128,128]{4,3,2,1,0:T(8,128)(2,1)S(1)}, u32[]{:S(2)}, u32[]{:S(2)}) %collective-permute-start.8) | collective-permute-done | bytes 393248 | tf_op jit(solution)/shard_map/ppermute | solution.py:255
  33.6 2.8 %collective-permute-start.11 = (bf16[3,2,2,128,128]{4,3,2,1,0:T(8,128)(2,1)S(1)}, bf16[3,2,2,128,128]{4,3,2,1,0:T(8,128)(2,1)S(1)}, u32[]{:S(2)}, u32[]{:S(2)}) collective-permute-start(bf16[3,2,2,128,128]{4,3,2,1,0:T(8,128)(2,1)S(1)} %collective-permute-done.8.refs_0_), channel_id=1, source_target_pairs={{0,1},{1,0},{2,3},{3,2},{4,5},{5,4},{6,7},{7,6},{8,9},{9,8},{10,11... | collective-permute-start | bytes 1179656 | tf_op jit(solution)/shard_map/ppermute | solution.py:17
  36.4 0.0 collective-permute-start.5
  36.4 7.7 %collective-permute-done.10.refs_1_ = bf16[2,2,2,128,128]{4,3,2,1,0:T(8,128)(2,1)S(1)} collective-permute-done((bf16[2,2,2,128,128]{4,3,2,1,0:T(8,128)(2,1)S(1)}, bf16[2,2,2,128,128]{4,3,2,1,0:T(8,128)(2,1)S(1)}, u32[]{:S(2)}, u32[]{:S(2)}) %collective-permute-start.10) | collective-permute-done | bytes 262176 | tf_op jit(solution)/shard_map/ppermute | solution.py:255
  44.1 0.0 collective-permute-start.12
  44.2 0.0 collective-permute-done.5.refs_4_
  44.2 0.0 collective-permute-done.7.refs_7_
  44.2 1.6 %own_terms.1.own = f32[2,2,2,128,128]{4,3,2,1,0:T(8,128)S(1)} custom-call(s32[30]{0:T(128)S(1)} %dynamic-slice_bitcast_fusion.line, s32[2,2]{1,0:T(2,128)S(1)} %bitcast.7, bf16[2,512,128]{2,1,0:T(8,128)(2,1)S(1)} %get-tuple-element.10.refs_0_.refs_4_.refs_2_, bf16[2,512,128]{2,1,0:T(8,128)(2,1)S(1)} %get-tuple-element.11.refs_1_.refs_4_, ...), custom_call_target="tpu_custom_call" | custom-call | flops 20000000 | bytes 60000 | tf_op jit(solution)/shard_map/own_terms/pallas_call | solution.py:267
  45.7 0.0 collective-permute-done.12.refs_4_
  45.7 0.0 collective-permute-done.11.refs_3_
  45.8 0.0 copy-done.1
  45.8 1.8 %finish.1 = (f32[2,1,2,2,128,128]{5,4,3,2,1,0:T(8,128)}, f32[2,1,2,2,128,128]{5,4,3,2,1,0:T(8,128)}) custom-call(s32[30]{0:T(128)S(1)} %dynamic-slice_bitcast_fusion.line, s32[2,2]{1,0:T(2,128)S(1)} %bitcast.8, f32[2,2,2,128,128]{4,3,2,1,0:T(8,128)S(1)} %own_terms.1.own, f32[2,1,2,2,128,128]{5,4,3,2,1,0:T(8,128)S(1)} %copy-done.1, ...), custom_call_target="tpu_custom_call" | custom-call | tf_op jit(solution)/shard_map/finish/pallas_call | solution.py:284
  (1 shorter events, 0.0 us)
Async XLA Ops:
  0.6 1.0 %copy-start = (f32[2,1,2,2,128,128]{5,4,3,2,1,0:T(8,128)S(1)}, f32[2,1,2,2,128,128]{5,4,3,2,1,0:T(8,128)}, u32[]{:S(2)}) copy-start(f32[2,1,2,2,128,128]{5,4,3,2,1,0:T(8,128)} %density.1) | copy-start | bytes 1572868
  1.7 0.9 %copy-start.2 = (bf16[2,1,2,2,128,128]{5,4,3,2,1,0:T(8,128)(2,1)S(1)}, bf16[2,1,2,2,128,128]{5,4,3,2,1,0:T(8,128)(2,1)}, u32[]{:S(2)}) copy-start(bf16[2,1,2,2,128,128]{5,4,3,2,1,0:T(8,128)(2,1)} %energy.1) | copy-start | bytes 786436
  2.7 2.1 %collective-permute-start = (bf16[2,512,128]{2,1,0:T(8,128)(2,1)S(1)}, bf16[2,512,128]{2,1,0:T(8,128)(2,1)S(1)}, u32[]{:S(2)}, u32[]{:S(2)}) collective-permute-start(bf16[2,512,128]{2,1,0:T(8,128)(2,1)S(1)} %get-tuple-element.10.refs_0_.refs_4_.refs_2_), channel_id=1, source_target_pairs={{0,1},{1,0},{2,3},{3,2},{4,5},{5,4},{6,7},{7,6},{8,9},{9,8},{10,11... | collective-permute-start | bytes 786440 | tf_op jit(solution)/shard_map/ppermute | solution.py:17
  3.4 4.0 %collective-permute-start.3 = (bf16[2,512,128]{2,1,0:T(8,128)(2,1)S(1)}, bf16[2,512,128]{2,1,0:T(8,128)(2,1)S(1)}, u32[]{:S(2)}, u32[]{:S(2)}) collective-permute-start(bf16[2,512,128]{2,1,0:T(8,128)(2,1)S(1)} %get-tuple-element.11.refs_1_.refs_4_), channel_id=1, source_target_pairs={{0,1},{1,0},{2,3},{3,2},{4,5},{5,4},{6,7},{7,6},{8,9},{9,8},{10,11... | collective-permute-start | bytes 786440 | tf_op jit(solution)/shard_map/ppermute | solution.py:17
  3.5 7.4 %collective-permute-start.4 = (bf16[2,512,128]{2,1,0:T(8,128)(2,1)S(1)}, bf16[2,512,128]{2,1,0:T(8,128)(2,1)S(1)}, u32[]{:S(2)}, u32[]{:S(2)}) collective-permute-start(bf16[2,512,128]{2,1,0:T(8,128)(2,1)S(1)} %get-tuple-element.12), channel_id=1, source_target_pairs={{0,2},{1,3},{2,0},{3,1},{4,6},{5,7},{6,4},{7,5},{8,10},{9,11},{10,... | collective-permute-start | bytes 786440 | tf_op jit(solution)/shard_map/ppermute | solution.py:17
  4.8 1.2 %copy-start.3 = (s32[2,1,2]{2,1,0:T(1,128)S(1)}, s32[2,1,2]{2,1,0:T(1,128)}, u32[]{:S(2)}) copy-start(s32[2,1,2]{2,1,0:T(1,128)} %param.6) | copy-start | bytes 52
  4.8 11.8 %collective-permute-start.1 = (bf16[2,512,128]{2,1,0:T(8,128)(2,1)S(1)}, bf16[2,512,128]{2,1,0:T(8,128)(2,1)S(1)}, u32[]{:S(2)}, u32[]{:S(2)}) collective-permute-start(bf16[2,512,128]{2,1,0:T(8,128)(2,1)S(1)} %broadcast_select_fusion), channel_id=1, source_target_pairs={{0,2},{1,3},{2,0},{3,1},{4,6},{5,7},{6,4},{7,5},{8,10},{9,11},{10,... | collective-permute-start | bytes 786440 | tf_op jit(solution)/shard_map/ppermute | solution.py:17
  5.9 1.5 %collective-permute-start.2 = (s32[2,2]{1,0:T(2,128)S(1)}, s32[2,2]{1,0:T(2,128)S(1)}, u32[]{:S(2)}, u32[]{:S(2)}) collective-permute-start(s32[2,2]{1,0:T(2,128)S(1)} %bitcast.3), channel_id=1, source_target_pairs={{0,1},{1,0},{2,3},{3,2},{4,5},{5,4},{6,7},{7,6},{8,9},{9,8},{10,11... | collective-permute-start | bytes 56 | tf_op jit(solution)/shard_map/ppermute | solution.py:17
  12.2 11.3 %collective-permute-start.6 = (bf16[3,2,2,128,128]{4,3,2,1,0:T(8,128)(2,1)S(1)}, bf16[3,2,2,128,128]{4,3,2,1,0:T(8,128)(2,1)S(1)}, u32[]{:S(2)}, u32[]{:S(2)}) collective-permute-start(bf16[3,2,2,128,128]{4,3,2,1,0:T(8,128)(2,1)S(1)} %terms_0.1), channel_id=1, source_target_pairs={{0,9},{1,12},{2,11},{3,14},{4,8},{5,13},{6,10},{7,15},{8,17},{9,20... | collective-permute-start | bytes 1179656 | tf_op jit(solution)/shard_map/ppermute | solution.py:255
  17.9 15.8 %collective-permute-start.8 = (bf16[3,2,2,128,128]{4,3,2,1,0:T(8,128)(2,1)S(1)}, bf16[3,2,2,128,128]{4,3,2,1,0:T(8,128)(2,1)S(1)}, u32[]{:S(2)}, u32[]{:S(2)}) collective-permute-start(bf16[3,2,2,128,128]{4,3,2,1,0:T(8,128)(2,1)S(1)} %terms_1.1), channel_id=1, source_target_pairs={{0,25},{1,28},{2,27},{3,30},{4,24},{5,29},{6,26},{7,31},{8,1},{9,4... | collective-permute-start | bytes 1179656 | tf_op jit(solution)/shard_map/ppermute | solution.py:255
  22.6 6.0 %collective-permute-start.9 = (bf16[2,2,2,128,128]{4,3,2,1,0:T(8,128)(2,1)S(1)}, bf16[2,2,2,128,128]{4,3,2,1,0:T(8,128)(2,1)S(1)}, u32[]{:S(2)}, u32[]{:S(2)}) collective-permute-start(bf16[2,2,2,128,128]{4,3,2,1,0:T(8,128)(2,1)S(1)} %get-tuple-element.15), channel_id=1, source_target_pairs={{3,22},{2,7},{6,2},{7,19},{9,28},{8,13},{12,8},{13,25},{19,6},{18,... | collective-permute-start | bytes 786440 | tf_op jit(solution)/shard_map/ppermute | solution.py:255
  23.3 22.5 %copy-start.1 = (f32[2,1,2,2,128,128]{5,4,3,2,1,0:T(8,128)S(1)}, f32[2,1,2,2,128,128]{5,4,3,2,1,0:T(8,128)}, u32[]{:S(2)}) copy-start(f32[2,1,2,2,128,128]{5,4,3,2,1,0:T(8,128)} %density.1) | copy-start | bytes 1572868
  23.3 20.9 %collective-permute-start.10 = (bf16[2,2,2,128,128]{4,3,2,1,0:T(8,128)(2,1)S(1)}, bf16[2,2,2,128,128]{4,3,2,1,0:T(8,128)(2,1)S(1)}, u32[]{:S(2)}, u32[]{:S(2)}) collective-permute-start(bf16[2,2,2,128,128]{4,3,2,1,0:T(8,128)(2,1)S(1)} %get-tuple-element.13), channel_id=1, source_target_pairs={{1,21},{0,4},{3,23},{2,6},{4,1},{5,16},{6,3},{7,18},{9,29},{8,12},... | collective-permute-start | bytes 786440 | tf_op jit(solution)/shard_map/ppermute | solution.py:255
  23.5 20.7 %collective-permute-start.7 = (bf16[3,2,2,128,128]{4,3,2,1,0:T(8,128)(2,1)S(1)}, bf16[3,2,2,128,128]{4,3,2,1,0:T(8,128)(2,1)S(1)}, u32[]{:S(2)}, u32[]{:S(2)}) collective-permute-start(bf16[3,2,2,128,128]{4,3,2,1,0:T(8,128)(2,1)S(1)} %collective-permute-done.6.refs_6_), channel_id=1, source_target_pairs={{0,1},{1,0},{2,3},{3,2},{4,5},{5,4},{6,7},{7,6},{8,9},{9,8},{10,11... | collective-permute-start | bytes 1179656 | tf_op jit(solution)/shard_map/ppermute | solution.py:17
  33.6 12.1 %collective-permute-start.11 = (bf16[3,2,2,128,128]{4,3,2,1,0:T(8,128)(2,1)S(1)}, bf16[3,2,2,128,128]{4,3,2,1,0:T(8,128)(2,1)S(1)}, u32[]{:S(2)}, u32[]{:S(2)}) collective-permute-start(bf16[3,2,2,128,128]{4,3,2,1,0:T(8,128)(2,1)S(1)} %collective-permute-done.8.refs_0_), channel_id=1, source_target_pairs={{0,1},{1,0},{2,3},{3,2},{4,5},{5,4},{6,7},{7,6},{8,9},{9,8},{10,11... | collective-permute-start | bytes 1179656 | tf_op jit(solution)/shard_map/ppermute | solution.py:17
  36.4 7.7 %collective-permute-start.5 = (bf16[2,512,128]{2,1,0:T(8,128)(2,1)S(1)}, bf16[2,512,128]{2,1,0:T(8,128)(2,1)S(1)}, u32[]{:S(2)}, u32[]{:S(2)}) collective-permute-start(bf16[2,512,128]{2,1,0:T(8,128)(2,1)S(1)} %collective-permute-done.1.refs_7_.refs_5_), channel_id=1, source_target_pairs={{0,1},{1,0},{2,3},{3,2},{4,5},{5,4},{6,7},{7,6},{8,9},{9,8},{10,11... | collective-permute-start | bytes 786440 | tf_op jit(solution)/shard_map/ppermute | solution.py:17
  44.1 1.6 %collective-permute-start.12 = (bf16[2,2,2,128,128]{4,3,2,1,0:T(8,128)(2,1)S(1)}, bf16[2,2,2,128,128]{4,3,2,1,0:T(8,128)(2,1)S(1)}, u32[]{:S(2)}, u32[]{:S(2)}) collective-permute-start(bf16[2,2,2,128,128]{4,3,2,1,0:T(8,128)(2,1)S(1)} %collective-permute-done.10.refs_1_), channel_id=1, source_target_pairs={{0,1},{1,0},{2,3},{3,2},{4,5},{5,4},{6,7},{7,6},{8,9},{9,8},{10,11... | collective-permute-start | bytes 786440 | tf_op jit(solution)/shard_map/ppermute | solution.py:17
